TPU v7x, 256 devices: a whole 4x4x8 slice. The times are simulated.
256 devices in a mesh: outer: 16 (over x, y), inner: 16 (over z, core).
Axes of the slice: x: 4, y: 4, z: 8, core: 2. Of those that a mesh axis runs over, the one named last changes fastest.
Arguments:
- queries: bfloat16 [1, 32768, 512], P(None, ('outer', 'inner')), may hold values from -70 to 70
- keys_values: bfloat16 [1, 32768, 1024], P(None, ('outer', 'inner')), may hold values from -4 to 4
- cotangent: bfloat16 [1, 32768, 512], P(None, ('outer', 'inner')), may hold values from -6 to 6
Outputs:
- attended: bfloat16 [1, 32768, 512], P(None, ('outer', 'inner'))
- query_grad: bfloat16 [1, 32768, 512], P(None, ('outer', 'inner'))
- kv_grad: bfloat16 [1, 32768, 1024], P(None, ('outer', 'inner'))
All inputs are finite; a program needn't handle non-finite values.
Results may differ from a plain program's by a relative error of at most 0.012.
The roundings to bfloat16 on the way count: a program that leaves them out, or rounds other values in their place, can miss the bound.
Values may be sent and summed in bfloat16 or wider, within the bound.
No kernel may reach another device: no remote copies, remote signals or barrier semaphores. Data moves between devices by JAX's collectives and lax.ppermute only.
A program may use at most 128 MiB of HBM per device.

v0:
```python
import functools
import math

import jax
import jax.numpy as jnp
from jax import lax
from jax.experimental import pallas as pl
from jax.experimental.pallas import tpu as pltpu
from jax.sharding import PartitionSpec as P

LEAF = 128
D = 512
TEAM = 4
COLS = 128
HEAD_DIM = 64
HALF_ROOT = 1.0 / math.sqrt(2.0)
SCALE = 1.0 / math.sqrt(HEAD_DIM)
BF16 = jnp.bfloat16
F32 = jnp.float32
VMEM = pl.BlockSpec(memory_space=pltpu.VMEM)


def call(body, name, outs, scratch=(), flops=0):
    def run(*operands):
        shapes = [jax.ShapeDtypeStruct(shape, dtype) for shape, dtype in outs]
        moved = sum(math.prod(s.shape) * s.dtype.itemsize for s in (*operands, *shapes))
        return pl.pallas_call(
            body,
            out_shape=shapes,
            in_specs=[VMEM] * len(operands),
            out_specs=[VMEM] * len(shapes),
            scratch_shapes=list(scratch),
            name=name,
            cost_estimate=pl.CostEstimate(flops=flops, bytes_accessed=moved, transcendentals=0),
            compiler_params=pltpu.CompilerParams(vmem_limit_bytes=24 * 1024 * 1024),
        )(*operands)

    return run


def exchange(array, bits):
    return lax.ppermute(array, "inner", [(i, i ^ bits) for i in range(16)])


def trade_slots(slots):
    groups = [[16 * o + 4 * team + m for o in range(16) for m in range(TEAM)] for team in range(4)]
    return lax.all_to_all(slots, ("outer", "inner"), 0, 0, axis_index_groups=groups, tiled=True)


def member():
    return lax.axis_index("inner") & 3


def columns(start, group):
    return pl.ds(pl.multiple_of(start + COLS * group, COLS), COLS)


def class_of(k):
    return k.bit_length() - 1


def row_index():
    return lax.broadcasted_iota(jnp.int32, (8, 2 * D), 0)


def read_rows(ref, count, first=0, step=1):
    return jnp.concatenate([ref[c, pl.ds(first, count, stride=step), :] for c in range(ref.shape[0])], axis=1)


def write_rows(ref, rows, first=0, step=1):
    for c in range(ref.shape[0]):
        ref[c, pl.ds(first, rows.shape[0], stride=step), :] = rows[:, 128 * c : 128 * c + 128]


def pool_rows(ref, count):
    pooled = ((read_rows(ref, count // 2, 0, 2) + read_rows(ref, count // 2, 1, 2)) * HALF_ROOT).astype(BF16)
    write_rows(ref, pooled.astype(F32))
    return pooled


def halve(rows, apart):
    pooled = (rows + pltpu.roll(rows, 8 - apart, 0)) * HALF_ROOT
    return pooled.astype(BF16).astype(F32)


def spread(rows, apart):
    row = row_index()
    return rows + jnp.where(row & apart == 0, pltpu.roll(rows, 8 - apart, 0), pltpu.roll(rows, apart, 0))


def pool_kernel(kv_ref, slots_ref, own_ref, out1_ref, out2_ref, out3_ref, rows_ref):
    write_rows(rows_ref, kv_ref[...].astype(F32))
    for count in (128, 64, 32, 16):
        four = pool_rows(rows_ref, count)
    four = four.astype(F32)
    outer = lax.axis_index("outer")
    row = row_index()
    five = halve(four, 1)
    six = halve(five, 2)
    seven = halve(six, 4)
    five = jnp.where(row & 1 == 0, five, pltpu.roll(five, 1, 0))
    six = spread(spread(jnp.where(row & 3 == 0, six, 0.0), 1), 2)
    seven = jnp.broadcast_to(seven[:1], seven.shape)
    table = [
        four,
        jnp.where(row & 1 == outer & 1, five, 0.0),
        jnp.where(row & 3 == outer & 3, six, 0.0),
        jnp.where(row == outer & 7, seven, 0.0),
    ]
    for m in range(TEAM):
        keys, values = slice(COLS * m, COLS * m + COLS), slice(D + COLS * m, D + COLS * m + COLS)
        blocks = [jnp.concatenate([rows[:, keys], rows[:, values]], axis=0).astype(BF16) for rows in table]
        slots_ref[outer * TEAM + m] = jnp.zeros_like(blocks[0])
        for k in range(1, 16):
            slots_ref[(outer ^ k) * TEAM + m] = blocks[class_of(k)]
    pack(kv_ref, 0, kv_ref, D, (own_ref, out1_ref, out2_ref, out3_ref))


def pack(left_ref, left, right_ref, right, out_refs):
    for k, ref in enumerate(out_refs):
        ref[:, :COLS] = left_ref[:, columns(left, member() ^ k)]
        ref[:, COLS:] = right_ref[:, columns(right, member() ^ k)]


def pack_kernel(q_ref, cot_ref, *out_refs):
    pack(q_ref, 0, cot_ref, 0, out_refs)


def class_sums(slots_ref):
    outer = lax.axis_index("outer")

    def total(c, m):
        return functools.reduce(jnp.add, [slots_ref[(outer ^ k) * TEAM + m].astype(F32) for k in range(1 << c, 2 << c)])

    return [[total(c, m) for m in range(TEAM)] for c in range(4)]


def side_by_side(block):
    return jnp.concatenate([block[:8], block[8:]], axis=1)


def collect_kernel(slots_ref, own_ref, got1_ref, got2_ref, got3_ref, _, tokens_ref, one_ref, near_ref, far_ref, rows_ref):
    for k, ref in enumerate((own_ref, got1_ref, got2_ref, got3_ref)):
        tokens_ref[LEAF * k : LEAF * k + LEAF, :] = ref[...]
    write_rows(rows_ref, tokens_ref[...].astype(F32))
    one_ref[...] = pool_rows(rows_ref, 512)
    near_ref[128:256, :] = pool_rows(rows_ref, 256)
    far_ref[128:192, :] = pool_rows(rows_ref, 128)
    block = jnp.concatenate([side_by_side(b) for blocks in class_sums(slots_ref) for b in blocks], axis=0).astype(BF16)
    near_ref[0:128, :] = block
    far_ref[0:128, :] = block


def across(a, b):
    return lax.dot_general(a, b, (((1,), (1,)), ((), ())), preferred_element_type=F32)


def along(a, b):
    return lax.dot_general(a, b, (((0,), (0,)), ((), ())), preferred_element_type=F32)


def two_heads(block):
    low_half = lax.broadcasted_iota(jnp.int32, block.shape, 1) < HEAD_DIM
    return jnp.concatenate([jnp.where(low_half, block, 0.0), jnp.where(low_half, 0.0, block)], axis=0).astype(BF16)


def first_kernel(
    own_ref, got1_ref, got2_ref, got3_ref, tokens_ref, one_ref, far_ref, keys_ref, q2_ref, cot2_ref, exps_ref, dweights_ref, max_ref, sum_ref, dot_ref
):
    for s, refs in enumerate(((own_ref, got1_ref), (got2_ref, got3_ref))):
        keys_ref[s, 0:256, :] = tokens_ref[256 * s : 256 * s + 256, :]
        keys_ref[s, 256:384, :] = one_ref[128 - 128 * s : 256 - 128 * s, :]
        keys_ref[s, 384:512, :] = far_ref[0:128, :]
        tokens = jnp.concatenate([ref[...] for ref in refs], axis=0).astype(F32)
        queries = two_heads(tokens[:, :COLS] * SCALE)
        grads = two_heads(tokens[:, COLS:])
        q2_ref[s] = queries
        cot2_ref[s] = grads
        scores = across(keys_ref[s, :, 0:128], queries)
        top = jnp.max(scores, axis=0, keepdims=True)
        exps = jnp.exp(scores - top)
        dweights = across(keys_ref[s, :, 128:256], grads)
        exps_ref[s] = exps
        dweights_ref[s] = dweights
        max_ref[s] = top
        sum_ref[s] = jnp.sum(exps, axis=0, keepdims=True)
        dot_ref[s] = jnp.sum(exps * dweights, axis=0, keepdims=True)


def second_kernel(
    got2_ref, got4_ref, got6_ref, q2_ref, cot2_ref, max_ref, sum_ref, dot_ref,
    send2_ref, send4_ref, send6_ref, keys_ref, factor_ref, centre_ref, rounded_ref, dscores_ref,
):
    keys_ref[0:256, :] = got2_ref[...]
    keys_ref[256:448, :] = got4_ref[...]
    keys_ref[448:640, :] = got6_ref[...]
    dkeys, dvals = [], []
    for s in range(2):
        queries, grads = q2_ref[s], cot2_ref[s]
        scores = across(keys_ref[:, 0:128], queries)
        dweights = across(keys_ref[:, 128:256], grads)
        top = jnp.maximum(max_ref[s], jnp.max(scores, axis=0, keepdims=True))
        exps = jnp.exp(scores - top)
        before = jnp.exp(max_ref[s] - top)
        inverse = 1.0 / (sum_ref[s] * before + jnp.sum(exps, axis=0, keepdims=True))
        centre = (dot_ref[s] * before + jnp.sum(exps * dweights, axis=0, keepdims=True)) * inverse
        weights = exps * inverse
        rounded = weights.astype(BF16)
        dscores = (weights * (dweights - centre)).astype(BF16)
        factor_ref[s] = before * inverse
        centre_ref[s] = centre
        rounded_ref[s] = rounded
        dscores_ref[s] = dscores
        dkeys.append(jnp.dot(dscores, queries, preferred_element_type=F32))
        dvals.append(jnp.dot(rounded, grads, preferred_element_type=F32))
    for cols, parts in ((slice(0, 128), dkeys), (slice(128, 256), dvals)):
        total = (parts[0] + parts[1]).astype(BF16)
        send2_ref[:, cols] = total[0:256]
        send4_ref[:, cols] = total[256:448]
        send6_ref[:, cols] = total[448:640]


def rest_kernel(
    keys_ref, later_ref, q2_ref, cot2_ref, exps_ref, dweights_ref, factor_ref, centre_ref, rounded_ref, dscores_ref,
    block_ref, one_ref, zero_ref, *results_refs,
):
    totals = []
    for s in range(2):
        weights = exps_ref[s] * factor_ref[s]
        rounded = weights.astype(BF16)
        dscores = (weights * (dweights_ref[s] - centre_ref[s])).astype(BF16)
        dkeys = jnp.dot(dscores, q2_ref[s], preferred_element_type=F32)
        dvals = jnp.dot(rounded, cot2_ref[s], preferred_element_type=F32)
        total = jnp.concatenate([dkeys, dvals], axis=1)
        zero_ref[256 * s : 256 * s + 256, :] = total[0:256]
        one_ref[128 - 128 * s : 256 - 128 * s, :] = total[256:384]
        totals.append(total[384:512])
        attended = along(keys_ref[s, :, 128:256], rounded) + along(later_ref[:, 128:256], rounded_ref[s])
        query_grad = along(keys_ref[s, :, 0:128], dscores) + along(later_ref[:, 0:128], dscores_ref[s])
        for i in range(2):
            low, high = slice(LEAF * i, LEAF * i + LEAF), slice(256 + LEAF * i, 256 + LEAF * i + LEAF)
            for cols, pair, scale in ((slice(0, 128), attended, 1.0), (slice(128, 256), query_grad, SCALE)):
                mine = jnp.concatenate([pair[:HEAD_DIM, low], pair[HEAD_DIM:, high]], axis=0).T
                results_refs[2 * s + i][:, cols] = (mine * scale).astype(BF16)
    block_ref[...] = totals[0] + totals[1]


def add(*parts):
    return functools.reduce(jnp.add, [p.astype(F32) for p in parts])


def scatter_kernel(
    block_ref, back2_ref, back4_ref, back6_ref, one_ref, zero_ref,
    slots_ref, own_ref, out1_ref, out2_ref, out3_ref, rows_ref,
):
    outer = lax.axis_index("outer")
    total = add(block_ref[...], back2_ref[0:128, :], back4_ref[0:128, :], back6_ref[0:128, :]).astype(BF16)
    for m in range(TEAM):
        slots_ref[outer * TEAM + m] = jnp.zeros((16, COLS), BF16)
        for c in range(4):
            rows = total[32 * c + 8 * m : 32 * c + 8 * m + 8]
            block = jnp.concatenate([rows[:, :COLS], rows[:, COLS:]], axis=0)
            for k in range(1 << c, 2 << c):
                slots_ref[(outer ^ k) * TEAM + m] = block
    total = add(back4_ref[128:192, :], back6_ref[128:192, :])
    count = 64
    for level in (back2_ref[128:256, :], one_ref[...], zero_ref[...]):
        write_rows(rows_ref, total, 0, 2)
        write_rows(rows_ref, total, 1, 2)
        count *= 2
        total = level.astype(F32) + HALF_ROOT * read_rows(rows_ref, count)
    own_ref[...] = total[0:LEAF]
    for k, ref in enumerate((out1_ref, out2_ref, out3_ref)):
        ref[...] = total[LEAF * (k + 1) : LEAF * (k + 2)].astype(BF16)


def outputs_kernel(own_ref, got1_ref, got2_ref, got3_ref, att_ref, dq_ref):
    for k, ref in enumerate((own_ref, got1_ref, got2_ref, got3_ref)):
        cols = columns(0, member() ^ k)
        att_ref[:, cols] = ref[:, :COLS]
        dq_ref[:, cols] = ref[:, COLS:]


def finish_kernel(slots_ref, own_ref, got1_ref, got2_ref, got3_ref, out_ref, sum_ref):
    outer = lax.axis_index("outer")
    row = row_index()
    four, five, six, seven = [
        jnp.concatenate([b[:8] for b in blocks] + [b[8:] for b in blocks], axis=1) for blocks in class_sums(slots_ref)
    ]
    five = spread(jnp.where(row & 1 == outer & 1, five, 0.0), 1)
    six = spread(spread(jnp.where(row & 3 == outer & 3, six, 0.0), 1), 2)
    seven = jnp.sum(jnp.where(row == outer & 7, seven, 0.0), axis=0, keepdims=True)
    total = four + HALF_ROOT * (five + HALF_ROOT * (six + HALF_ROOT * seven))
    total = total * 0.25
    for k, ref in enumerate((own_ref, got1_ref, got2_ref, got3_ref)):
        for start, cols in ((0, slice(0, COLS)), (D, slice(COLS, 2 * COLS))):
            sum_ref[:, columns(start, member() ^ k)] = ref[:, cols].astype(F32)
    for r in range(8):
        rows = slice(16 * r, 16 * r + 16)
        out_ref[rows, :] = (sum_ref[rows, :] + total[r : r + 1]).astype(BF16)


def shards(queries, keys_values, cotangent):
    queries, keys_values, cotangent = queries[0], keys_values[0], cotangent[0]
    slots = ((16 * TEAM, 16, COLS), BF16)
    whole = ((LEAF, D), BF16)
    piece = ((LEAF, 2 * COLS), BF16)
    own_rows = pltpu.VMEM((8, LEAF, 128), F32)
    team_rows = pltpu.VMEM((2, TEAM * LEAF, 128), F32)

    sent, own, out1, out2, out3 = call(pool_kernel, "pool", [slots, *[piece] * 4], [own_rows])(keys_values)
    taken = trade_slots(sent)
    got2, got3, got1 = exchange(out2, 2), exchange(out3, 3), exchange(out1, 1)
    own_q, out1, out2, out3 = call(pack_kernel, "pack", [piece] * 4)(queries, cotangent)
    tokens, one, near, far = call(
        collect_kernel, "collect", [((512, 256), BF16), ((256, 256), BF16), ((256, 256), BF16), ((192, 256), BF16)], [team_rows]
    )(taken, own, got1, got2, got3, own_q)
    got4 = exchange(far, 8)
    got6 = exchange(far, 12)
    near = exchange(near, 4)
    got2, got3, got1 = exchange(out2, 2), exchange(out3, 3), exchange(out1, 1)

    stacks = ((2, 512, 128), BF16)
    stat = ((2, 1, 512), F32)
    squares = ((2, 512, 512), F32)
    keys, q2, cot2, exps, dweights, top, sums, dots = call(
        first_kernel,
        "first",
        [((2, 512, 256), BF16), stacks, stacks, squares, squares, stat, stat, stat],
        flops=4 * 512 * 1024 * 128,
    )(own_q, got1, got2, got3, tokens, one, far)
    later = ((2, 640, 512), BF16)
    send2, send4, send6, later_keys, factor, centre, rounded, dscores = call(
        second_kernel,
        "second",
        [((256, 256), BF16), ((192, 256), BF16), ((192, 256), BF16), ((640, 256), BF16), stat, stat, later, later],
        flops=8 * 640 * 1024 * 128,
    )(near, got4, got6, q2, cot2, top, sums, dots)
    back4 = exchange(send4, 8)
    back6 = exchange(send6, 12)
    back2 = exchange(send2, 4)
    block, one, zero, own_results, out1, out2, out3 = call(
        rest_kernel,
        "rest",
        [((128, 256), F32), ((256, 256), F32), ((512, 256), F32), *[piece] * 4],
        flops=8 * 1152 * 1024 * 128,
    )(keys, later_keys, q2, cot2, exps, dweights, factor, centre, rounded, dscores)
    got2, got3, got1 = exchange(out2, 2), exchange(out3, 3), exchange(out1, 1)
    attended, query_grad = call(outputs_kernel, "outputs", [whole, whole])(own_results, got1, got2, got3)

    sent, own, out1, out2, out3 = call(
        scatter_kernel, "scatter", [slots, ((LEAF, 256), F32), *[piece] * 3], [team_rows]
    )(block, back2, back4, back6, one, zero)
    taken = trade_slots(sent)
    got2, got3, got1 = exchange(out2, 2), exchange(out3, 3), exchange(out1, 1)
    (kv_grad,) = call(finish_kernel, "finish", [((LEAF, 2 * D), BF16)], [pltpu.VMEM((LEAF, 2 * D), F32)])(
        taken, own, got1, got2, got3
    )
    return attended[None], query_grad[None], kv_grad[None]


def solution(mesh):
    spec = P(None, ("outer", "inner"), None)
    return jax.shard_map(shards, mesh=mesh, in_specs=(spec,) * 3, out_specs=(spec,) * 3, check_vma=False)
```

profile of v0, /device:TPU:1, one launch (start us, length us, event | category | flops | bytes accessed | tf_op | source)
XLA Modules:
  0.0 79.3 jit_solution(11669426596657140895)
XLA Ops:
  0.6 0.9 %copy-done = bf16[1,128,1024]{2,1,0:T(8,128)(2,1)S(1)} copy-done((bf16[1,128,1024]{2,1,0:T(8,128)(2,1)S(1)}, bf16[1,128,1024]{2,1,0:T(8,128)(2,1)}, u32[]{:S(2)}) %copy-start) | copy-done | bytes 262168
  1.6 0.9 %pool.1 = (bf16[64,16,128]{2,1,0:T(8,128)(2,1)}, bf16[128,256]{1,0:T(8,128)(2,1)S(1)}, bf16[128,256]{1,0:T(8,128)(2,1)S(1)}, bf16[128,256]{1,0:T(8,128)(2,1)S(1)}, bf16[128,256]{1,0:T(8,128)(2,1)S(1)}) custom-call(bf16[128,1024]{1,0:T(8,128)(2,1)S(1)} %bitcast.6), custom_call_target="tpu_custom_call" | custom-call | bytes 786432 | tf_op jit(solution)/shard_map/pool/pallas_call | solution.py:27
  2.5 10.3 %all-to-all-start = ((bf16[64,16,128]{2,1,0:T(8,128)(2,1)}), bf16[64,16,128]{2,1,0:T(8,128)(2,1)S(1)}, u32[]{:S(2)}, u32[]{:S(2)}) async-start(bf16[64,16,128]{2,1,0:T(8,128)(2,1)} %get-tuple-element.50), calls=%async_computation | async-start | bytes 524288 | tf_op jit(solution)/shard_map/all_to_all | solution.py:47
  12.9 0.5 collective-permute-start.3
  13.4 1.3 %collective-permute-start.4 = (bf16[128,256]{1,0:T(8,128)(2,1)S(1)}, bf16[128,256]{1,0:T(8,128)(2,1)S(1)}, u32[]{:S(2)}, u32[]{:S(2)}) collective-permute-start(bf16[128,256]{1,0:T(8,128)(2,1)S(1)} %get-tuple-element.53), channel_id=1, source_target_pairs={{0,2},{1,3},{2,0},{3,1},{4,6},{5,7},{6,4},{7,5},{8,10},{9,11},{10,... | collective-permute-start | bytes 196616 | tf_op jit(solution)/shard_map/ppermute | solution.py:42
  14.7 0.4 collective-permute-start.5
  15.2 0.9 %copy-done.1 = bf16[1,128,512]{2,1,0:T(8,128)(2,1)S(1)} copy-done((bf16[1,128,512]{2,1,0:T(8,128)(2,1)S(1)}, bf16[1,128,512]{2,1,0:T(8,128)(2,1)}, u32[]{:S(2)}) %copy-start.1) | copy-done | bytes 131096
  16.1 0.9 %copy-done.2 = bf16[1,128,512]{2,1,0:T(8,128)(2,1)S(1)} copy-done((bf16[1,128,512]{2,1,0:T(8,128)(2,1)S(1)}, bf16[1,128,512]{2,1,0:T(8,128)(2,1)}, u32[]{:S(2)}) %copy-start.2) | copy-done | bytes 131096
  17.0 0.2 collective-permute-start
  17.3 0.0 collective-permute-done.3.got1_ref
  17.3 1.8 %collective-permute-done.4.got2_ref = bf16[128,256]{1,0:T(8,128)(2,1)S(1)} collective-permute-done((bf16[128,256]{1,0:T(8,128)(2,1)S(1)}, bf16[128,256]{1,0:T(8,128)(2,1)S(1)}, u32[]{:S(2)}, u32[]{:S(2)}) %collective-permute-start.4) | collective-permute-done | bytes 65568 | tf_op jit(solution)/shard_map/ppermute | solution.py:42
  19.1 1.9 %collective-permute-done.5.got3_ref = bf16[128,256]{1,0:T(8,128)(2,1)S(1)} collective-permute-done((bf16[128,256]{1,0:T(8,128)(2,1)S(1)}, bf16[128,256]{1,0:T(8,128)(2,1)S(1)}, u32[]{:S(2)}, u32[]{:S(2)}) %collective-permute-start.5) | collective-permute-done | bytes 65568 | tf_op jit(solution)/shard_map/ppermute | solution.py:42
  21.0 2.4 %all-to-all-done.slots_ref = bf16[64,16,128]{2,1,0:T(8,128)(2,1)S(1)} async-done(((bf16[64,16,128]{2,1,0:T(8,128)(2,1)}), bf16[64,16,128]{2,1,0:T(8,128)(2,1)S(1)}, u32[]{:S(2)}, u32[]{:S(2)}) %all-to-all-start) | async-done | bytes 262176 | tf_op jit(solution)/shard_map/all_to_all | solution.py:47
  23.3 0.2 collect.1
  23.5 3.1 %collective-permute-start.6 = (bf16[256,256]{1,0:T(8,128)(2,1)S(1)}, bf16[256,256]{1,0:T(8,128)(2,1)S(1)}, u32[]{:S(2)}, u32[]{:S(2)}) collective-permute-start(bf16[256,256]{1,0:T(8,128)(2,1)S(1)} %get-tuple-element.59), channel_id=1, source_target_pairs={{0,4},{1,5},{2,6},{3,7},{4,0},{5,1},{6,2},{7,3},{8,12},{9,13},{10,... | collective-permute-start | bytes 393224 | tf_op jit(solution)/shard_map/ppermute | solution.py:42
  26.6 3.3 %collective-permute-start.8 = (bf16[192,256]{1,0:T(8,128)(2,1)S(1)}, bf16[192,256]{1,0:T(8,128)(2,1)S(1)}, u32[]{:S(2)}, u32[]{:S(2)}) collective-permute-start(bf16[192,256]{1,0:T(8,128)(2,1)S(1)} %get-tuple-element.57.far_ref), channel_id=1, source_target_pairs={{0,12},{1,13},{2,14},{3,15},{4,8},{5,9},{6,10},{7,11},{8,4},{9,5},... | collective-permute-start | bytes 294920 | tf_op jit(solution)/shard_map/ppermute | solution.py:42
  29.9 0.9 %collective-permute-start.7 = (bf16[192,256]{1,0:T(8,128)(2,1)S(1)}, bf16[192,256]{1,0:T(8,128)(2,1)S(1)}, u32[]{:S(2)}, u32[]{:S(2)}) collective-permute-start(bf16[192,256]{1,0:T(8,128)(2,1)S(1)} %get-tuple-element.57.far_ref), channel_id=1, source_target_pairs={{0,8},{1,9},{2,10},{3,11},{4,12},{5,13},{6,14},{7,15},{8,0},{9,1},... | collective-permute-start | bytes 294920 | tf_op jit(solution)/shard_map/ppermute | solution.py:42
  30.8 0.0 collective-permute-start.1
  30.8 2.6 %collective-permute-start.2 = (bf16[128,256]{1,0:T(8,128)(2,1)S(1)}, bf16[128,256]{1,0:T(8,128)(2,1)S(1)}, u32[]{:S(2)}, u32[]{:S(2)}) collective-permute-start(bf16[128,256]{1,0:T(8,128)(2,1)S(1)} %get-tuple-element.49), channel_id=1, source_target_pairs={{0,3},{1,2},{2,1},{3,0},{4,7},{5,6},{6,5},{7,4},{8,11},{9,10},{10,... | collective-permute-start | bytes 196616 | tf_op jit(solution)/shard_map/ppermute | solution.py:42
  33.4 6.8 %collective-permute-done.1.got2_ref = bf16[128,256]{1,0:T(8,128)(2,1)S(1)} collective-permute-done((bf16[128,256]{1,0:T(8,128)(2,1)S(1)}, bf16[128,256]{1,0:T(8,128)(2,1)S(1)}, u32[]{:S(2)}, u32[]{:S(2)}) %collective-permute-start.1) | collective-permute-done | bytes 65568 | tf_op jit(solution)/shard_map/ppermute | solution.py:42
  40.2 1.4 %collective-permute-done.2.got3_ref = bf16[128,256]{1,0:T(8,128)(2,1)S(1)} collective-permute-done((bf16[128,256]{1,0:T(8,128)(2,1)S(1)}, bf16[128,256]{1,0:T(8,128)(2,1)S(1)}, u32[]{:S(2)}, u32[]{:S(2)}) %collective-permute-start.2) | collective-permute-done | bytes 65568 | tf_op jit(solution)/shard_map/ppermute | solution.py:42
  41.6 0.9 %first.1 = (bf16[2,512,256]{2,1,0:T(8,128)(2,1)S(1)}, bf16[2,512,128]{2,1,0:T(8,128)(2,1)S(1)}, bf16[2,512,128]{2,1,0:T(8,128)(2,1)S(1)}, f32[2,512,512]{2,1,0:T...) custom-call(bf16[128,256]{1,0:T(8,128)(2,1)S(1)} %get-tuple-element., ...), custom_call_target="tpu_custom_call" | custom-call | flops 268435456 | bytes 6008832 | tf_op jit(solution)/shard_map/first/pallas_call | solution.py:27
  42.5 0.0 collective-permute-done.7.got4_ref
  42.5 0.0 collective-permute-done.6.got2_ref
  42.5 2.6 %second.1 = (bf16[256,256]{1,0:T(8,128)(2,1)S(1)}, bf16[192,256]{1,0:T(8,128)(2,1)S(1)}, bf16[192,256]{1,0:T(8,128)(2,1)S(1)}, bf16[640,256]{1,0:T(8,128)(2,1)S(...) custom-call(bf16[256,256]{1,0:T(8,128)(2,1)S(1)} %collective-permute, ...), custom_call_target="tpu_custom_call" | custom-call | flops 671088640 | bytes 4149248 | tf_op jit(solution)/shard_map/second/pallas_call | solution.py:27
  45.1 0.1 collective-permute-start.12
  45.2 4.1 %collective-permute-start.13 = (bf16[192,256]{1,0:T(8,128)(2,1)S(1)}, bf16[192,256]{1,0:T(8,128)(2,1)S(1)}, u32[]{:S(2)}, u32[]{:S(2)}) collective-permute-start(bf16[192,256]{1,0:T(8,128)(2,1)S(1)} %get-tuple-element.80), channel_id=1, source_target_pairs={{0,8},{1,9},{2,10},{3,11},{4,12},{5,13},{6,14},{7,15},{8,0},{9,1},... | collective-permute-start | bytes 294920 | tf_op jit(solution)/shard_map/ppermute | solution.py:42
  49.4 1.5 %collective-permute-start.14 = (bf16[192,256]{1,0:T(8,128)(2,1)S(1)}, bf16[192,256]{1,0:T(8,128)(2,1)S(1)}, u32[]{:S(2)}, u32[]{:S(2)}) collective-permute-start(bf16[192,256]{1,0:T(8,128)(2,1)S(1)} %get-tuple-element.81), channel_id=1, source_target_pairs={{0,12},{1,13},{2,14},{3,15},{4,8},{5,9},{6,10},{7,11},{8,4},{9,5},... | collective-permute-start | bytes 294920 | tf_op jit(solution)/shard_map/ppermute | solution.py:42
  50.9 1.5 %rest.1 = (f32[128,256]{1,0:T(8,128)S(1)}, f32[256,256]{1,0:T(8,128)S(1)}, f32[512,256]{1,0:T(8,128)S(1)}, bf16[128,256]{1,0:T(8,128)(2,1)S(1)}, bf16[128,256]{1...) custom-call(bf16[2,512,256]{2,1,0:T(8,128)(2,1)S(1)} %get-tuple-element.58.keys_ref, ...), custom_call_target="tpu_custom_call" | custom-call | flops 1207959552 | bytes 9379840 | tf_op jit(solution)/shard_map/rest/pallas_call | solution.py:27
  52.4 2.8 %collective-permute-done.13.back4_ref = bf16[192,256]{1,0:T(8,128)(2,1)S(1)} collective-permute-done((bf16[192,256]{1,0:T(8,128)(2,1)S(1)}, bf16[192,256]{1,0:T(8,128)(2,1)S(1)}, u32[]{:S(2)}, u32[]{:S(2)}) %collective-permute-start.13) | collective-permute-done | bytes 98336 | tf_op jit(solution)/shard_map/ppermute | solution.py:42
  55.2 4.3 %collective-permute-done.14.back6_ref = bf16[192,256]{1,0:T(8,128)(2,1)S(1)} collective-permute-done((bf16[192,256]{1,0:T(8,128)(2,1)S(1)}, bf16[192,256]{1,0:T(8,128)(2,1)S(1)}, u32[]{:S(2)}, u32[]{:S(2)}) %collective-permute-start.14) | collective-permute-done | bytes 98336 | tf_op jit(solution)/shard_map/ppermute | solution.py:42
  59.5 0.0 collective-permute-done.12.back2_ref
  59.6 0.8 %scatter.1 = (bf16[64,16,128]{2,1,0:T(8,128)(2,1)}, f32[128,256]{1,0:T(8,128)S(1)}, bf16[128,256]{1,0:T(8,128)(2,1)S(1)}, bf16[128,256]{1,0:T(8,128)(2,1)S(1)}, bf16[128,256]{1,0:T(8,128)(2,1)S(1)}) custom-call(f32[128,256]{1,0:T(8,128)S(1)} %get-tuple-element.78.block_ref, bf16[256,256]{1,0:T(8,128)(2,1)S(1)} %collective-permute-done.12.back2_ref, ...), custom_call_target="tpu_custom_call" | custom-call | bytes 1835008 | tf_op jit(solution)/shard_map/scatter/pallas_call | solution.py:27
  60.4 7.4 %all-to-all-start.1 = ((bf16[64,16,128]{2,1,0:T(8,128)(2,1)}), bf16[64,16,128]{2,1,0:T(8,128)(2,1)S(1)}, u32[]{:S(2)}, u32[]{:S(2)}) async-start(bf16[64,16,128]{2,1,0:T(8,128)(2,1)} %get-tuple-element.84), calls=%async_computation.1 | async-start | bytes 524288 | tf_op jit(solution)/shard_map/all_to_all | solution.py:47
  67.8 0.5 collective-permute-start.9
  68.4 1.3 %collective-permute-start.10 = (bf16[128,256]{1,0:T(8,128)(2,1)S(1)}, bf16[128,256]{1,0:T(8,128)(2,1)S(1)}, u32[]{:S(2)}, u32[]{:S(2)}) collective-permute-start(bf16[128,256]{1,0:T(8,128)(2,1)S(1)} %get-tuple-element.74), channel_id=1, source_target_pairs={{0,2},{1,3},{2,0},{3,1},{4,6},{5,7},{6,4},{7,5},{8,10},{9,11},{10,... | collective-permute-start | bytes 196616 | tf_op jit(solution)/shard_map/ppermute | solution.py:42
  69.7 0.4 collective-permute-start.11
  70.1 0.1 collective-permute-start.15
  70.3 1.3 %collective-permute-start.16 = (bf16[128,256]{1,0:T(8,128)(2,1)S(1)}, bf16[128,256]{1,0:T(8,128)(2,1)S(1)}, u32[]{:S(2)}, u32[]{:S(2)}) collective-permute-start(bf16[128,256]{1,0:T(8,128)(2,1)S(1)} %get-tuple-element.87), channel_id=1, source_target_pairs={{0,2},{1,3},{2,0},{3,1},{4,6},{5,7},{6,4},{7,5},{8,10},{9,11},{10,... | collective-permute-start | bytes 196616 | tf_op jit(solution)/shard_map/ppermute | solution.py:42
  71.5 0.7 collective-permute-start.17
  72.3 1.8 %collective-permute-done.10.got2_ref = bf16[128,256]{1,0:T(8,128)(2,1)S(1)} collective-permute-done((bf16[128,256]{1,0:T(8,128)(2,1)S(1)}, bf16[128,256]{1,0:T(8,128)(2,1)S(1)}, u32[]{:S(2)}, u32[]{:S(2)}) %collective-permute-start.10) | collective-permute-done | bytes 65568 | tf_op jit(solution)/shard_map/ppermute | solution.py:42
  74.0 2.4 %collective-permute-done.11.got3_ref = bf16[128,256]{1,0:T(8,128)(2,1)S(1)} collective-permute-done((bf16[128,256]{1,0:T(8,128)(2,1)S(1)}, bf16[128,256]{1,0:T(8,128)(2,1)S(1)}, u32[]{:S(2)}, u32[]{:S(2)}) %collective-permute-start.11) | collective-permute-done | bytes 65568 | tf_op jit(solution)/shard_map/ppermute | solution.py:42
  76.4 0.7 outputs.1
  77.1 0.0 collective-permute-done.15.got1_ref
  77.1 0.0 collective-permute-done.16.got2_ref
  77.2 1.3 %collective-permute-done.17.got3_ref = bf16[128,256]{1,0:T(8,128)(2,1)S(1)} collective-permute-done((bf16[128,256]{1,0:T(8,128)(2,1)S(1)}, bf16[128,256]{1,0:T(8,128)(2,1)S(1)}, u32[]{:S(2)}, u32[]{:S(2)}) %collective-permute-start.17) | collective-permute-done | bytes 65568 | tf_op jit(solution)/shard_map/ppermute | solution.py:42
  78.4 0.0 all-to-all-done.1.slots_ref
  78.4 0.9 %finish.1 = bf16[128,1024]{1,0:T(8,128)(2,1)} custom-call(bf16[64,16,128]{2,1,0:T(8,128)(2,1)S(1)} %all-to-all-done.1.slots_ref, f32[128,256]{1,0:T(8,128)S(1)} %get-tuple-element.85.own_ref, bf16[128,256]{1,0:T(8,128)(2,1)S(1)} %collective-permute-done.15.got1_ref, bf16[128,256]{1,0:T(8,128)(2,1)S(1)} %collective-permute-done.16.got2_ref, ...), custom_call_target="tpu_custom_call" | custom-call | bytes 851968 | tf_op jit(solution)/shard_map/finish/pallas_call | solution.py:27
  (7 shorter events, 0.1 us)
Async XLA Ops:
  0.6 1.0 %copy-start = (bf16[1,128,1024]{2,1,0:T(8,128)(2,1)S(1)}, bf16[1,128,1024]{2,1,0:T(8,128)(2,1)}, u32[]{:S(2)}) copy-start(bf16[1,128,1024]{2,1,0:T(8,128)(2,1)} %param.4) | copy-start | bytes 786436
  2.5 20.8 %all-to-all-start = ((bf16[64,16,128]{2,1,0:T(8,128)(2,1)}), bf16[64,16,128]{2,1,0:T(8,128)(2,1)S(1)}, u32[]{:S(2)}, u32[]{:S(2)}) async-start(bf16[64,16,128]{2,1,0:T(8,128)(2,1)} %get-tuple-element.50), calls=%async_computation | async-start | bytes 524288 | tf_op jit(solution)/shard_map/all_to_all | solution.py:47
  12.9 4.4 %collective-permute-start.3 = (bf16[128,256]{1,0:T(8,128)(2,1)S(1)}, bf16[128,256]{1,0:T(8,128)(2,1)S(1)}, u32[]{:S(2)}, u32[]{:S(2)}) collective-permute-start(bf16[128,256]{1,0:T(8,128)(2,1)S(1)} %get-tuple-element.52), channel_id=1, source_target_pairs={{0,1},{1,0},{2,3},{3,2},{4,5},{5,4},{6,7},{7,6},{8,9},{9,8},{10,11... | collective-permute-start | bytes 196616 | tf_op jit(solution)/shard_map/ppermute | solution.py:42
  13.4 5.7 %collective-permute-start.4 = (bf16[128,256]{1,0:T(8,128)(2,1)S(1)}, bf16[128,256]{1,0:T(8,128)(2,1)S(1)}, u32[]{:S(2)}, u32[]{:S(2)}) collective-permute-start(bf16[128,256]{1,0:T(8,128)(2,1)S(1)} %get-tuple-element.53), channel_id=1, source_target_pairs={{0,2},{1,3},{2,0},{3,1},{4,6},{5,7},{6,4},{7,5},{8,10},{9,11},{10,... | collective-permute-start | bytes 196616 | tf_op jit(solution)/shard_map/ppermute | solution.py:42
  14.7 6.3 %collective-permute-start.5 = (bf16[128,256]{1,0:T(8,128)(2,1)S(1)}, bf16[128,256]{1,0:T(8,128)(2,1)S(1)}, u32[]{:S(2)}, u32[]{:S(2)}) collective-permute-start(bf16[128,256]{1,0:T(8,128)(2,1)S(1)} %get-tuple-element.54), channel_id=1, source_target_pairs={{0,3},{1,2},{2,1},{3,0},{4,7},{5,6},{6,5},{7,4},{8,11},{9,10},{10,... | collective-permute-start | bytes 196616 | tf_op jit(solution)/shard_map/ppermute | solution.py:42
  15.2 0.9 %copy-start.1 = (bf16[1,128,512]{2,1,0:T(8,128)(2,1)S(1)}, bf16[1,128,512]{2,1,0:T(8,128)(2,1)}, u32[]{:S(2)}) copy-start(bf16[1,128,512]{2,1,0:T(8,128)(2,1)} %param.3) | copy-start | bytes 393220
  16.1 0.9 %copy-start.2 = (bf16[1,128,512]{2,1,0:T(8,128)(2,1)S(1)}, bf16[1,128,512]{2,1,0:T(8,128)(2,1)}, u32[]{:S(2)}) copy-start(bf16[1,128,512]{2,1,0:T(8,128)(2,1)} %param.5) | copy-start | bytes 393220
  17.0 13.8 %collective-permute-start = (bf16[128,256]{1,0:T(8,128)(2,1)S(1)}, bf16[128,256]{1,0:T(8,128)(2,1)S(1)}, u32[]{:S(2)}, u32[]{:S(2)}) collective-permute-start(bf16[128,256]{1,0:T(8,128)(2,1)S(1)} %get-tuple-element.47), channel_id=1, source_target_pairs={{0,1},{1,0},{2,3},{3,2},{4,5},{5,4},{6,7},{7,6},{8,9},{9,8},{10,11... | collective-permute-start | bytes 196616 | tf_op jit(solution)/shard_map/ppermute | solution.py:42
  23.5 19.0 %collective-permute-start.6 = (bf16[256,256]{1,0:T(8,128)(2,1)S(1)}, bf16[256,256]{1,0:T(8,128)(2,1)S(1)}, u32[]{:S(2)}, u32[]{:S(2)}) collective-permute-start(bf16[256,256]{1,0:T(8,128)(2,1)S(1)} %get-tuple-element.59), channel_id=1, source_target_pairs={{0,4},{1,5},{2,6},{3,7},{4,0},{5,1},{6,2},{7,3},{8,12},{9,13},{10,... | collective-permute-start | bytes 393224 | tf_op jit(solution)/shard_map/ppermute | solution.py:42
  26.6 15.9 %collective-permute-start.8 = (bf16[192,256]{1,0:T(8,128)(2,1)S(1)}, bf16[192,256]{1,0:T(8,128)(2,1)S(1)}, u32[]{:S(2)}, u32[]{:S(2)}) collective-permute-start(bf16[192,256]{1,0:T(8,128)(2,1)S(1)} %get-tuple-element.57.far_ref), channel_id=1, source_target_pairs={{0,12},{1,13},{2,14},{3,15},{4,8},{5,9},{6,10},{7,11},{8,4},{9,5},... | collective-permute-start | bytes 294920 | tf_op jit(solution)/shard_map/ppermute | solution.py:42
  29.9 12.6 %collective-permute-start.7 = (bf16[192,256]{1,0:T(8,128)(2,1)S(1)}, bf16[192,256]{1,0:T(8,128)(2,1)S(1)}, u32[]{:S(2)}, u32[]{:S(2)}) collective-permute-start(bf16[192,256]{1,0:T(8,128)(2,1)S(1)} %get-tuple-element.57.far_ref), channel_id=1, source_target_pairs={{0,8},{1,9},{2,10},{3,11},{4,12},{5,13},{6,14},{7,15},{8,0},{9,1},... | collective-permute-start | bytes 294920 | tf_op jit(solution)/shard_map/ppermute | solution.py:42
  30.8 9.4 %collective-permute-start.1 = (bf16[128,256]{1,0:T(8,128)(2,1)S(1)}, bf16[128,256]{1,0:T(8,128)(2,1)S(1)}, u32[]{:S(2)}, u32[]{:S(2)}) collective-permute-start(bf16[128,256]{1,0:T(8,128)(2,1)S(1)} %get-tuple-element.48), channel_id=1, source_target_pairs={{0,2},{1,3},{2,0},{3,1},{4,6},{5,7},{6,4},{7,5},{8,10},{9,11},{10,... | collective-permute-start | bytes 196616 | tf_op jit(solution)/shard_map/ppermute | solution.py:42
  30.8 10.7 %collective-permute-start.2 = (bf16[128,256]{1,0:T(8,128)(2,1)S(1)}, bf16[128,256]{1,0:T(8,128)(2,1)S(1)}, u32[]{:S(2)}, u32[]{:S(2)}) collective-permute-start(bf16[128,256]{1,0:T(8,128)(2,1)S(1)} %get-tuple-element.49), channel_id=1, source_target_pairs={{0,3},{1,2},{2,1},{3,0},{4,7},{5,6},{6,5},{7,4},{8,11},{9,10},{10,... | collective-permute-start | bytes 196616 | tf_op jit(solution)/shard_map/ppermute | solution.py:42
  45.1 14.4 %collective-permute-start.12 = (bf16[256,256]{1,0:T(8,128)(2,1)S(1)}, bf16[256,256]{1,0:T(8,128)(2,1)S(1)}, u32[]{:S(2)}, u32[]{:S(2)}) collective-permute-start(bf16[256,256]{1,0:T(8,128)(2,1)S(1)} %get-tuple-element.79), channel_id=1, source_target_pairs={{0,4},{1,5},{2,6},{3,7},{4,0},{5,1},{6,2},{7,3},{8,12},{9,13},{10,... | collective-permute-start | bytes 393224 | tf_op jit(solution)/shard_map/ppermute | solution.py:42
  45.2 10.0 %collective-permute-start.13 = (bf16[192,256]{1,0:T(8,128)(2,1)S(1)}, bf16[192,256]{1,0:T(8,128)(2,1)S(1)}, u32[]{:S(2)}, u32[]{:S(2)}) collective-permute-start(bf16[192,256]{1,0:T(8,128)(2,1)S(1)} %get-tuple-element.80), channel_id=1, source_target_pairs={{0,8},{1,9},{2,10},{3,11},{4,12},{5,13},{6,14},{7,15},{8,0},{9,1},... | collective-permute-start | bytes 294920 | tf_op jit(solution)/shard_map/ppermute | solution.py:42
  49.4 10.2 %collective-permute-start.14 = (bf16[192,256]{1,0:T(8,128)(2,1)S(1)}, bf16[192,256]{1,0:T(8,128)(2,1)S(1)}, u32[]{:S(2)}, u32[]{:S(2)}) collective-permute-start(bf16[192,256]{1,0:T(8,128)(2,1)S(1)} %get-tuple-element.81), channel_id=1, source_target_pairs={{0,12},{1,13},{2,14},{3,15},{4,8},{5,9},{6,10},{7,11},{8,4},{9,5},... | collective-permute-start | bytes 294920 | tf_op jit(solution)/shard_map/ppermute | solution.py:42
  60.4 18.1 %all-to-all-start.1 = ((bf16[64,16,128]{2,1,0:T(8,128)(2,1)}), bf16[64,16,128]{2,1,0:T(8,128)(2,1)S(1)}, u32[]{:S(2)}, u32[]{:S(2)}) async-start(bf16[64,16,128]{2,1,0:T(8,128)(2,1)} %get-tuple-element.84), calls=%async_computation.1 | async-start | bytes 524288 | tf_op jit(solution)/shard_map/all_to_all | solution.py:47
  67.8 3.7 %collective-permute-start.9 = (bf16[128,256]{1,0:T(8,128)(2,1)S(1)}, bf16[128,256]{1,0:T(8,128)(2,1)S(1)}, u32[]{:S(2)}, u32[]{:S(2)}) collective-permute-start(bf16[128,256]{1,0:T(8,128)(2,1)S(1)} %get-tuple-element.73), channel_id=1, source_target_pairs={{0,1},{1,0},{2,3},{3,2},{4,5},{5,4},{6,7},{7,6},{8,9},{9,8},{10,11... | collective-permute-start | bytes 196616 | tf_op jit(solution)/shard_map/ppermute | solution.py:42
  68.4 5.7 %collective-permute-start.10 = (bf16[128,256]{1,0:T(8,128)(2,1)S(1)}, bf16[128,256]{1,0:T(8,128)(2,1)S(1)}, u32[]{:S(2)}, u32[]{:S(2)}) collective-permute-start(bf16[128,256]{1,0:T(8,128)(2,1)S(1)} %get-tuple-element.74), channel_id=1, source_target_pairs={{0,2},{1,3},{2,0},{3,1},{4,6},{5,7},{6,4},{7,5},{8,10},{9,11},{10,... | collective-permute-start | bytes 196616 | tf_op jit(solution)/shard_map/ppermute | solution.py:42
  69.7 6.7 %collective-permute-start.11 = (bf16[128,256]{1,0:T(8,128)(2,1)S(1)}, bf16[128,256]{1,0:T(8,128)(2,1)S(1)}, u32[]{:S(2)}, u32[]{:S(2)}) collective-permute-start(bf16[128,256]{1,0:T(8,128)(2,1)S(1)} %get-tuple-element.75), channel_id=1, source_target_pairs={{0,3},{1,2},{2,1},{3,0},{4,7},{5,6},{6,5},{7,4},{8,11},{9,10},{10,... | collective-permute-start | bytes 196616 | tf_op jit(solution)/shard_map/ppermute | solution.py:42
  70.1 7.0 %collective-permute-start.15 = (bf16[128,256]{1,0:T(8,128)(2,1)S(1)}, bf16[128,256]{1,0:T(8,128)(2,1)S(1)}, u32[]{:S(2)}, u32[]{:S(2)}) collective-permute-start(bf16[128,256]{1,0:T(8,128)(2,1)S(1)} %get-tuple-element.86), channel_id=1, source_target_pairs={{0,1},{1,0},{2,3},{3,2},{4,5},{5,4},{6,7},{7,6},{8,9},{9,8},{10,11... | collective-permute-start | bytes 196616 | tf_op jit(solution)/shard_map/ppermute | solution.py:42
  70.3 6.9 %collective-permute-start.16 = (bf16[128,256]{1,0:T(8,128)(2,1)S(1)}, bf16[128,256]{1,0:T(8,128)(2,1)S(1)}, u32[]{:S(2)}, u32[]{:S(2)}) collective-permute-start(bf16[128,256]{1,0:T(8,128)(2,1)S(1)} %get-tuple-element.87), channel_id=1, source_target_pairs={{0,2},{1,3},{2,0},{3,1},{4,6},{5,7},{6,4},{7,5},{8,10},{9,11},{10,... | collective-permute-start | bytes 196616 | tf_op jit(solution)/shard_map/ppermute | solution.py:42
  71.5 6.9 %collective-permute-start.17 = (bf16[128,256]{1,0:T(8,128)(2,1)S(1)}, bf16[128,256]{1,0:T(8,128)(2,1)S(1)}, u32[]{:S(2)}, u32[]{:S(2)}) collective-permute-start(bf16[128,256]{1,0:T(8,128)(2,1)S(1)} %get-tuple-element.88), channel_id=1, source_target_pairs={{0,3},{1,2},{2,1},{3,0},{4,7},{5,6},{6,5},{7,4},{8,11},{9,10},{10,... | collective-permute-start | bytes 196616 | tf_op jit(solution)/shard_map/ppermute | solution.py:42
where the time goes:
time: 79.6 us; the launch traced here: 79.3 us
  starting transfers between devices  40.3 us (51%)
  waiting for transfers between devices  26.9 us (34%)
  Pallas kernels  8.64 us (11%)
  local copies, waits for them, and re-layouts  2.75 us (3%)
    ppermute x18, waiting for transfers between devices, exchange(): return lax.ppermute(array, 'inner', [(i, i ^ bits) for i in range(16)])  24.5 us
    ppermute x18, starting transfers between devices, exchange(): return lax.ppermute(array, 'inner', [(i, i ^ bits) for i in range(16)])  22.5 us
    all_to_all x2, starting transfers between devices, trade_slots(): lax.all_to_all(slots, ('outer', 'inner'), 0, 0, axis_index_groups=groups,...  17.8 us
    pallas_call x9, Pallas kernels, run(): pl.pallas_call(body, out_shape=shapes, in_specs=[VMEM] * len(operands), o...  8.64 us
    unnamed x6, local copies, waits for them, and re-layouts  2.75 us
    all_to_all x2, waiting for transfers between devices, trade_slots(): lax.all_to_all(slots, ('outer', 'inner'), 0, 0, axis_index_groups=groups,...  2.37 us
  transfers between devices with their start and end apart: 20, of which 10 were waited for; matrix products, arithmetic and copies ran while one was open for 0% of the time, Pallas kernels for 4%

commit v1 on v0

v1 whole, which is shorter than its diff:
```python
import functools
import math

import jax
import jax.numpy as jnp
from jax import lax
from jax.experimental import pallas as pl
from jax.experimental.pallas import tpu as pltpu
from jax.sharding import PartitionSpec as P

LEAF = 128
D = 512
TEAM = 4
COLS = 128
HEAD_DIM = 64
LONG = 2 * 10**10
HALF_ROOT = 1.0 / math.sqrt(2.0)
SCALE = 1.0 / math.sqrt(HEAD_DIM)
BF16 = jnp.bfloat16
F32 = jnp.float32
VMEM = pl.BlockSpec(memory_space=pltpu.VMEM)
HBM = pl.BlockSpec(memory_space=pltpu.HBM)
ANYWHERE = pl.BlockSpec(memory_space=pl.ANY)


def call(body, name, outs, scratch=(), flops=0, spec=VMEM, limit=24, after=()):
    def run(*operands):
        count = len(operands)
        operands = (*operands, *after)
        shapes = [jax.ShapeDtypeStruct(shape, dtype) for shape, dtype in outs]
        moved = sum(math.prod(s.shape) * s.dtype.itemsize for s in (*operands, *shapes))
        return pl.pallas_call(
            (lambda *refs: body(*refs[:count], *refs[count + len(after) :])),
            out_shape=shapes,
            in_specs=[spec] * count + [ANYWHERE] * len(after),
            out_specs=[VMEM] * len(shapes),
            scratch_shapes=list(scratch),
            name=name,
            cost_estimate=pl.CostEstimate(flops=flops, bytes_accessed=moved, transcendentals=0),
            compiler_params=pltpu.CompilerParams(vmem_limit_bytes=limit * 1024 * 1024),
        )(*operands)

    return run


def exchange(array, bits):
    return lax.ppermute(array, "inner", [(i, i ^ bits) for i in range(16)])


def trade_slots(slots):
    groups = [[16 * o + 4 * team + m for o in range(16) for m in range(TEAM)] for team in range(4)]
    return lax.all_to_all(slots, ("outer", "inner"), 0, 0, axis_index_groups=groups, tiled=True)


def member():
    return lax.axis_index("inner") & 3


def columns(start, group):
    return pl.ds(pl.multiple_of(start + COLS * group, COLS), COLS)


def class_of(k):
    return k.bit_length() - 1


def row_index():
    return lax.broadcasted_iota(jnp.int32, (8, 2 * D), 0)


def read_rows(ref, count, first=0, step=1):
    return jnp.concatenate([ref[c, pl.ds(first, count, stride=step), :] for c in range(ref.shape[0])], axis=1)


def write_rows(ref, rows, first=0, step=1):
    for c in range(ref.shape[0]):
        ref[c, pl.ds(first, rows.shape[0], stride=step), :] = rows[:, 128 * c : 128 * c + 128]


def pool_rows(ref, count):
    pooled = ((read_rows(ref, count // 2, 0, 2) + read_rows(ref, count // 2, 1, 2)) * HALF_ROOT).astype(BF16)
    write_rows(ref, pooled.astype(F32))
    return pooled


def halve(rows, apart):
    pooled = (rows + pltpu.roll(rows, 8 - apart, 0)) * HALF_ROOT
    return pooled.astype(BF16).astype(F32)


def spread(rows, apart):
    row = row_index()
    return rows + jnp.where(row & apart == 0, pltpu.roll(rows, 8 - apart, 0), pltpu.roll(rows, apart, 0))


def pool_kernel(
    q_hbm, kv_hbm, cot_hbm, slots_ref, own_ref, out1_ref, out2_ref, out3_ref, q_ref, kv_ref, cot_ref, rows_ref, sems
):
    pairs = ((kv_hbm, kv_ref), (q_hbm, q_ref), (cot_hbm, cot_ref))
    copies = [pltpu.make_async_copy(a, b, sems.at[i]) for i, (a, b) in enumerate(pairs)]
    for copy in copies:
        copy.start()
    copies[0].wait()
    write_rows(rows_ref, kv_ref[...].astype(F32))
    for count in (128, 64, 32, 16):
        four = pool_rows(rows_ref, count)
    four = four.astype(F32)
    outer = lax.axis_index("outer")
    row = row_index()
    five = halve(four, 1)
    six = halve(five, 2)
    seven = halve(six, 4)
    five = jnp.where(row & 1 == 0, five, pltpu.roll(five, 1, 0))
    six = spread(spread(jnp.where(row & 3 == 0, six, 0.0), 1), 2)
    seven = jnp.broadcast_to(seven[:1], seven.shape)
    table = [
        four,
        jnp.where(row & 1 == outer & 1, five, 0.0),
        jnp.where(row & 3 == outer & 3, six, 0.0),
        jnp.where(row == outer & 7, seven, 0.0),
    ]
    for m in range(TEAM):
        keys, values = slice(COLS * m, COLS * m + COLS), slice(D + COLS * m, D + COLS * m + COLS)
        blocks = [jnp.concatenate([rows[:, keys], rows[:, values]], axis=0).astype(BF16) for rows in table]
        slots_ref[outer * TEAM + m] = jnp.zeros_like(blocks[0])
        for k in range(1, 16):
            slots_ref[(outer ^ k) * TEAM + m] = blocks[class_of(k)]
    copies[1].wait()
    copies[2].wait()
    for k, ref in enumerate((own_ref, out1_ref, out2_ref, out3_ref)):
        group = member() ^ k
        ref[:, 0:128] = q_ref[:, columns(0, group)]
        ref[:, 128:256] = kv_ref[:, columns(0, group)]
        ref[:, 256:384] = kv_ref[:, columns(D, group)]
        ref[:, 384:512] = cot_ref[:, columns(0, group)]


def class_sums(slots_ref):
    outer = lax.axis_index("outer")

    def total(c, m):
        return functools.reduce(jnp.add, [slots_ref[(outer ^ k) * TEAM + m].astype(F32) for k in range(1 << c, 2 << c)])

    return [[total(c, m) for m in range(TEAM)] for c in range(4)]


def side_by_side(block):
    return jnp.concatenate([block[:8], block[8:]], axis=1)


def team_kernel(own_ref, got1_ref, got2_ref, got3_ref, tokens_ref, one_ref, two_ref, three_ref, rows_ref):
    for k, ref in enumerate((own_ref, got1_ref, got2_ref, got3_ref)):
        tokens_ref[LEAF * k : LEAF * k + LEAF, :] = ref[...]
    write_rows(rows_ref, tokens_ref[:, 128:384].astype(F32))
    one_ref[...] = pool_rows(rows_ref, 512)
    two_ref[...] = pool_rows(rows_ref, 256)
    three_ref[...] = pool_rows(rows_ref, 128)


def collect_kernel(slots_ref, block_ref):
    block_ref[...] = jnp.concatenate(
        [side_by_side(b) for blocks in class_sums(slots_ref) for b in blocks], axis=0
    ).astype(BF16)


def low_kernel(two_ref, six_ref, four_ref, out_ref):
    out_ref[0:128, :] = two_ref[...]
    out_ref[128:192, :] = four_ref[...]
    out_ref[192:256, :] = six_ref[...]


def across(a, b):
    return lax.dot_general(a, b, (((1,), (1,)), ((), ())), preferred_element_type=F32)


def along(a, b):
    return lax.dot_general(a, b, (((0,), (0,)), ((), ())), preferred_element_type=F32)


def two_heads(block):
    low_half = lax.broadcasted_iota(jnp.int32, block.shape, 1) < HEAD_DIM
    return jnp.concatenate([jnp.where(low_half, block, 0.0), jnp.where(low_half, 0.0, block)], axis=0).astype(BF16)


def first_kernel(
    tokens_ref, one_ref, block_ref, low_ref, keys_ref, q2_ref, cot2_ref, exps_ref, dweights_ref, max_ref, sum_ref, dot_ref
):
    for s in range(2):
        tokens = slice(256 * s, 256 * s + 256)
        keys_ref[s, 0:256, :] = tokens_ref[tokens, 128:384]
        keys_ref[s, 256:384, :] = one_ref[128 - 128 * s : 256 - 128 * s, :]
        keys_ref[s, 384:512, :] = block_ref[...]
        keys_ref[s, 512:768, :] = low_ref[...]
        queries = two_heads(tokens_ref[tokens, 0:128].astype(F32) * SCALE)
        grads = two_heads(tokens_ref[tokens, 384:512].astype(F32))
        q2_ref[s] = queries
        cot2_ref[s] = grads
        scores = across(keys_ref[s, :, 0:128], queries)
        top = jnp.max(scores, axis=0, keepdims=True)
        exps = jnp.exp(scores - top)
        dweights = across(keys_ref[s, :, 128:256], grads)
        exps_ref[s] = exps
        dweights_ref[s] = dweights
        max_ref[s] = top
        sum_ref[s] = jnp.sum(exps, axis=0, keepdims=True)
        dot_ref[s] = jnp.sum(exps * dweights, axis=0, keepdims=True)


def second_kernel(
    got2_ref, got6_ref, got4_ref, low_ref, q2_ref, cot2_ref, exps_ref, dweights_ref, max_ref, sum_ref, dot_ref,
    send2_ref, send4_ref, send6_ref, keys_ref, factor_ref, centre_ref, rounded_ref, dscores_ref,
):
    keys_ref[0:128, :] = got2_ref[...]
    keys_ref[128:256, :] = got4_ref[...]
    keys_ref[256:384, :] = got6_ref[...]
    keys_ref[384:640, :] = low_ref[...]
    dkeys, dvals = [], []
    for s in range(2):
        queries, grads = q2_ref[s], cot2_ref[s]
        scores = across(keys_ref[0:384, 0:128], queries)
        dweights = across(keys_ref[0:384, 128:256], grads)
        top = jnp.maximum(max_ref[s], jnp.max(scores, axis=0, keepdims=True))
        exps = jnp.exp(scores - top)
        before = jnp.exp(max_ref[s] - top)
        inverse = 1.0 / (sum_ref[s] * before + jnp.sum(exps, axis=0, keepdims=True))
        centre = (dot_ref[s] * before + jnp.sum(exps * dweights, axis=0, keepdims=True)) * inverse
        factor = before * inverse
        weights = jnp.concatenate([exps * inverse, exps_ref[s, 512:768, :] * factor], axis=0)
        dweights = jnp.concatenate([dweights, dweights_ref[s, 512:768, :]], axis=0)
        rounded = weights.astype(BF16)
        dscores = (weights * (dweights - centre)).astype(BF16)
        factor_ref[s] = factor
        centre_ref[s] = centre
        rounded_ref[s] = rounded
        dscores_ref[s] = dscores
        dkeys.append(jnp.dot(dscores, queries, preferred_element_type=F32))
        dvals.append(jnp.dot(rounded, grads, preferred_element_type=F32))
    for cols, parts in ((slice(0, 128), dkeys), (slice(128, 256), dvals)):
        total = (parts[0] + parts[1]).astype(BF16)
        send2_ref[0:128, cols] = total[0:128]
        send2_ref[128:256, cols] = total[384:512]
        send4_ref[0:128, cols] = total[128:256]
        send4_ref[128:192, cols] = total[512:576]
        send6_ref[0:128, cols] = total[256:384]
        send6_ref[128:192, cols] = total[576:640]


def rest_kernel(
    keys_ref, later_ref, q2_ref, cot2_ref, exps_ref, dweights_ref, factor_ref, centre_ref, rounded_ref, dscores_ref,
    block_ref, one_ref, zero_ref, results_ref,
):
    totals = []
    for s in range(2):
        weights = exps_ref[s, 0:512, :] * factor_ref[s]
        rounded = weights.astype(BF16)
        dscores = (weights * (dweights_ref[s, 0:512, :] - centre_ref[s])).astype(BF16)
        dkeys = jnp.dot(dscores, q2_ref[s], preferred_element_type=F32)
        dvals = jnp.dot(rounded, cot2_ref[s], preferred_element_type=F32)
        total = jnp.concatenate([dkeys, dvals], axis=1)
        zero_ref[256 * s : 256 * s + 256, :] = total[0:256]
        one_ref[128 - 128 * s : 256 - 128 * s, :] = total[256:384]
        totals.append(total[384:512])
        attended = along(keys_ref[s, 0:512, 128:256], rounded) + along(later_ref[:, 128:256], rounded_ref[s])
        query_grad = along(keys_ref[s, 0:512, 0:128], dscores) + along(later_ref[:, 0:128], dscores_ref[s])
        for i in range(2):
            rows = slice(256 * s + LEAF * i, 256 * s + LEAF * i + LEAF)
            low, high = slice(LEAF * i, LEAF * i + LEAF), slice(256 + LEAF * i, 256 + LEAF * i + LEAF)
            for cols, pair, scale in ((slice(0, 128), attended, 1.0), (slice(128, 256), query_grad, SCALE)):
                mine = jnp.concatenate([pair[:HEAD_DIM, low], pair[HEAD_DIM:, high]], axis=0).T
                results_ref[rows, cols] = (mine * scale).astype(BF16)
    block_ref[...] = totals[0] + totals[1]


def add(*parts):
    return functools.reduce(jnp.add, [p.astype(F32) for p in parts])


def scatter_kernel(
    block_ref, back2_ref, back4_ref, back6_ref, one_ref, zero_ref, results_ref,
    slots_ref, own_ref, out1_ref, out2_ref, out3_ref, rows_ref,
):
    outer = lax.axis_index("outer")
    total = add(block_ref[...], back2_ref[0:128, :], back4_ref[0:128, :], back6_ref[0:128, :]).astype(BF16)
    for m in range(TEAM):
        slots_ref[outer * TEAM + m] = jnp.zeros((16, COLS), BF16)
        for c in range(4):
            rows = total[32 * c + 8 * m : 32 * c + 8 * m + 8]
            block = jnp.concatenate([rows[:, :COLS], rows[:, COLS:]], axis=0)
            for k in range(1 << c, 2 << c):
                slots_ref[(outer ^ k) * TEAM + m] = block
    total = add(back4_ref[128:192, :], back6_ref[128:192, :])
    count = 64
    for level in (back2_ref[128:256, :], one_ref[...], zero_ref[...]):
        write_rows(rows_ref, total, 0, 2)
        write_rows(rows_ref, total, 1, 2)
        count *= 2
        total = level.astype(F32) + HALF_ROOT * read_rows(rows_ref, count)
    own_ref[...] = total[0:LEAF]
    for k, ref in enumerate((out1_ref, out2_ref, out3_ref)):
        rows = slice(LEAF * (k + 1), LEAF * (k + 2))
        ref[:, 0:256] = total[rows].astype(BF16)
        ref[:, 256:512] = results_ref[rows, :]


def merge_kernel(results_ref, own_ref, got1_ref, got2_ref, got3_ref, att_ref, dq_ref, sum_ref):
    for k, ref in enumerate((own_ref, got1_ref, got2_ref, got3_ref)):
        group = member() ^ k
        sum_ref[:, columns(0, group)] = ref[:, 0:128].astype(F32)
        sum_ref[:, columns(D, group)] = ref[:, 128:256].astype(F32)
        part = results_ref[0:LEAF, :] if k == 0 else ref[:, 256:512]
        att_ref[:, columns(0, group)] = part[:, :COLS]
        dq_ref[:, columns(0, group)] = part[:, COLS:]


def finish_kernel(slots_ref, sum_ref, out_ref):
    outer = lax.axis_index("outer")
    row = row_index()
    four, five, six, seven = [
        jnp.concatenate([b[:8] for b in blocks] + [b[8:] for b in blocks], axis=1) for blocks in class_sums(slots_ref)
    ]
    five = spread(jnp.where(row & 1 == outer & 1, five, 0.0), 1)
    six = spread(spread(jnp.where(row & 3 == outer & 3, six, 0.0), 1), 2)
    seven = jnp.sum(jnp.where(row == outer & 7, seven, 0.0), axis=0, keepdims=True)
    total = four + HALF_ROOT * (five + HALF_ROOT * (six + HALF_ROOT * seven))
    total = total * 0.25
    for r in range(8):
        rows = slice(16 * r, 16 * r + 16)
        out_ref[rows, :] = (sum_ref[rows, :] + total[r : r + 1]).astype(BF16)


def shards(queries, keys_values, cotangent):
    queries, keys_values, cotangent = queries[0], keys_values[0], cotangent[0]
    slots = ((16 * TEAM, 16, COLS), BF16)
    piece = ((LEAF, D), BF16)
    loaded = [pltpu.VMEM((LEAF, D), BF16), pltpu.VMEM((LEAF, 2 * D), BF16), pltpu.VMEM((LEAF, D), BF16)]
    own_rows = pltpu.VMEM((8, LEAF, 128), F32)
    team_rows = pltpu.VMEM((2, TEAM * LEAF, 128), F32)

    sent, own, out1, out2, out3 = call(
        pool_kernel, "pool", [slots, piece, piece, piece, piece], [*loaded, own_rows, pltpu.SemaphoreType.DMA((3,))], spec=HBM, limit=56
    )(queries, keys_values, cotangent)
    taken = trade_slots(sent)
    got2 = exchange(out2, 2)
    got3 = exchange(out3, 3)
    got1 = exchange(out1, 1)
    tokens, one, two, three = call(
        team_kernel,
        "team",
        [((512, D), BF16), ((256, 256), BF16), ((128, 256), BF16), ((64, 256), BF16)],
        [team_rows],
        flops=LONG,
    )(own, got1, got2, got3)
    low4 = exchange(three, 8)
    low6 = exchange(three, 12)
    low2 = exchange(two, 4)
    (block,) = call(collect_kernel, "collect", [((128, 256), BF16)], flops=LONG)(taken)
    got4 = exchange(block, 8)
    got6 = exchange(block, 12)
    got2 = exchange(block, 4)
    (low,) = call(low_kernel, "low", [((256, 256), BF16)], flops=LONG)(low2, low6, low4)

    stacks = ((2, 512, 128), BF16)
    stat = ((2, 1, 512), F32)
    squares = ((2, 768, 512), F32)
    keys, q2, cot2, exps, dweights, top, sums, dots = call(
        first_kernel,
        "first",
        [((2, 768, 256), BF16), stacks, stacks, squares, squares, stat, stat, stat],
        flops=4 * 768 * 1024 * 128,
    )(tokens, one, block, low)
    later = ((2, 640, 512), BF16)
    send2, send4, send6, later_keys, factor, centre, rounded, dscores = call(
        second_kernel,
        "second",
        [((256, 256), BF16), ((192, 256), BF16), ((192, 256), BF16), ((640, 256), BF16), stat, stat, later, later],
        flops=8 * 640 * 1024 * 128,
    )(got2, got6, got4, low, q2, cot2, exps, dweights, top, sums, dots)
    back4 = exchange(send4, 8)
    back6 = exchange(send6, 12)
    back2 = exchange(send2, 4)
    block, one, zero, results = call(
        rest_kernel,
        "rest",
        [((128, 256), F32), ((256, 256), F32), ((512, 256), F32), ((512, 256), BF16)],
        flops=8 * 1152 * 1024 * 128,
    )(keys, later_keys, q2, cot2, exps, dweights, factor, centre, rounded, dscores)

    sent, own, out1, out2, out3 = call(
        scatter_kernel, "scatter", [slots, ((LEAF, 256), F32), piece, piece, piece], [team_rows]
    )(block, back2, back4, back6, one, zero, results)
    taken = trade_slots(sent)
    got2 = exchange(out2, 2)
    got3 = exchange(out3, 3)
    got1 = exchange(out1, 1)
    attended, query_grad, total = call(
        merge_kernel, "merge", [((LEAF, D), BF16), ((LEAF, D), BF16), ((LEAF, 2 * D), F32)], flops=LONG
    )(results, own, got1, got2, got3)
    (kv_grad,) = call(finish_kernel, "finish", [((LEAF, 2 * D), BF16)])(taken, total)
    return attended[None], query_grad[None], kv_grad[None]


def solution(mesh):
    spec = P(None, ("outer", "inner"), None)
    return jax.shard_map(shards, mesh=mesh, in_specs=(spec,) * 3, out_specs=(spec,) * 3, check_vma=False)
```

time: 79.6 us -> 76.4 us (0.960)
  waiting for transfers between devices: 26.9 us -> 22.6 us
  starting transfers between devices: 40.3 us -> 42.3 us
  local copies, waits for them, and re-layouts: 2.75 us -> 0.9 us
  Pallas kernels: 8.64 us -> 9.58 us
    ppermute x18 -> x15, waiting for transfers between devices: 24.5 us -> 11.9 us  [exchange(): return lax.ppermute(array, 'inner', [(i, i ^ bits) for i in range(16)])]
    all_to_all x2, waiting for transfers between devices: 2.37 us -> 10.7 us  [trade_slots(): lax.all_to_all(slots, ('outer', 'inner'), 0, 0, axis_index_groups=groups,...]
    ppermute x18 -> x15, starting transfers between devices: 22.5 us -> 28 us  [exchange(): return lax.ppermute(array, 'inner', [(i, i ^ bits) for i in range(16)])]
    all_to_all x2, starting transfers between devices: 17.8 us -> 14.2 us  [trade_slots(): lax.all_to_all(slots, ('outer', 'inner'), 0, 0, axis_index_groups=groups,...]
    unnamed x6 -> x2, local copies, waits for them, and re-layouts: 2.75 us -> 0.9 us
    pallas_call x9 -> x10, Pallas kernels: 8.64 us -> 9.58 us  [run(): pl.pallas_call(lambda *refs: body(*refs[:count], *refs[count + len(after)...]
  transfers between devices with their start and end apart: 20 -> 17, of which waited for: 10 -> 6; matrix products, arithmetic and copies ran while one was open for 0% -> 0% of each run, Pallas kernels for 4% -> 5%
where the time goes in v1:
time: 76.4 us; the launch traced here: 76.1 us
  starting transfers between devices  42.3 us (55%)
  waiting for transfers between devices  22.6 us (30%)
  Pallas kernels  9.58 us (13%)
  local copies, waits for them, and re-layouts  0.9 us (1%)
    ppermute x15, starting transfers between devices, exchange(): return lax.ppermute(array, 'inner', [(i, i ^ bits) for i in range(16)])  28 us
    all_to_all x2, starting transfers between devices, trade_slots(): lax.all_to_all(slots, ('outer', 'inner'), 0, 0, axis_index_groups=groups,...  14.2 us
    ppermute x15, waiting for transfers between devices, exchange(): return lax.ppermute(array, 'inner', [(i, i ^ bits) for i in range(16)])  11.9 us
    all_to_all x2, waiting for transfers between devices, trade_slots(): lax.all_to_all(slots, ('outer', 'inner'), 0, 0, axis_index_groups=groups,...  10.7 us
    pallas_call x10, Pallas kernels, run(): pl.pallas_call(lambda *refs: body(*refs[:count], *refs[count + len(after)...  9.58 us
  transfers between devices with their start and end apart: 17, of which 6 were waited for; matrix products, arithmetic and copies ran while one was open for 0% of the time, Pallas kernels for 5%

profile of v1, /device:TPU:1, one launch (start us, length us, event | category | flops | bytes accessed | tf_op | source)
XLA Modules:
  0.0 76.1 jit_solution(9155589507791791124)
XLA Ops:
  0.6 2.2 %pool.1 = (bf16[64,16,128]{2,1,0:T(8,128)(2,1)}, bf16[128,512]{1,0:T(8,128)(2,1)}, bf16[128,512]{1,0:T(8,128)(2,1)}, bf16[128,512]{1,0:T(8,128)(2,1)}, bf16[128,512]{1,0:T(8,128)(2,1)}) custom-call(bf16[128,512]{1,0:T(8,128)(2,1)} %bitcast.8, bf16[128,1024]{1,0:T(8,128)(2,1)} %bitcast.6, bf16[128,512]{1,0:T(8,128)(2,1)} %bitcast.9), custom_call_target="tpu_custom_call" | custom-call | bytes 1310720 | tf_op jit(solution)/shard_map/pool/pallas_call | solution.py:32
  2.8 3.3 %collective-permute-start = (bf16[128,512]{1,0:T(8,128)(2,1)}, bf16[128,512]{1,0:T(8,128)(2,1)S(1)}, u32[]{:S(2)}, u32[]{:S(2)}) collective-permute-start(bf16[128,512]{1,0:T(8,128)(2,1)} %get-tuple-element.41), channel_id=1, source_target_pairs={{0,1},{1,0},{2,3},{3,2},{4,5},{5,4},{6,7},{7,6},{8,9},{9,8},{10,11... | collective-permute-start | bytes 393224 | tf_op jit(solution)/shard_map/ppermute | solution.py:47
  6.1 0.0 collective-permute-start.1
  6.1 1.7 %collective-permute-start.2 = (bf16[128,512]{1,0:T(8,128)(2,1)}, bf16[128,512]{1,0:T(8,128)(2,1)S(1)}, u32[]{:S(2)}, u32[]{:S(2)}) collective-permute-start(bf16[128,512]{1,0:T(8,128)(2,1)} %get-tuple-element.43), channel_id=1, source_target_pairs={{0,3},{1,2},{2,1},{3,0},{4,7},{5,6},{6,5},{7,4},{8,11},{9,10},{10,... | collective-permute-start | bytes 393224 | tf_op jit(solution)/shard_map/ppermute | solution.py:47
  7.9 7.3 %all-to-all-start = ((bf16[64,16,128]{2,1,0:T(8,128)(2,1)}), bf16[64,16,128]{2,1,0:T(8,128)(2,1)S(1)}, u32[]{:S(2)}, u32[]{:S(2)}) async-start(bf16[64,16,128]{2,1,0:T(8,128)(2,1)} %get-tuple-element.46), calls=%async_computation | async-start | bytes 524288 | tf_op jit(solution)/shard_map/all_to_all | solution.py:52
  15.1 0.0 collective-permute-done.refs_1_
  15.2 0.0 collective-permute-done.1.refs_2_
  15.2 0.0 collective-permute-done.2.refs_3_
  15.2 0.0 copy-start
  15.2 0.9 %copy-done = bf16[128,512]{1,0:T(8,128)(2,1)S(1)} copy-done((bf16[128,512]{1,0:T(8,128)(2,1)S(1)}, bf16[128,512]{1,0:T(8,128)(2,1)}, u32[]{:S(2)}) %copy-start) | copy-done | bytes 131096
  16.1 0.2 team.1
  16.3 6.1 %collective-permute-start.5 = (bf16[64,256]{1,0:T(8,128)(2,1)S(1)}, bf16[64,256]{1,0:T(8,128)(2,1)S(1)}, u32[]{:S(2)}, u32[]{:S(2)}) collective-permute-start(bf16[64,256]{1,0:T(8,128)(2,1)S(1)} %get-tuple-element.48), channel_id=1, source_target_pairs={{0,8},{1,9},{2,10},{3,11},{4,12},{5,13},{6,14},{7,15},{8,0},{9,1},... | collective-permute-start | bytes 98312 | tf_op jit(solution)/shard_map/ppermute | solution.py:47
  22.4 0.3 collective-permute-start.4
  22.6 0.9 %collective-permute-start.3 = (bf16[128,256]{1,0:T(8,128)(2,1)S(1)}, bf16[128,256]{1,0:T(8,128)(2,1)S(1)}, u32[]{:S(2)}, u32[]{:S(2)}) collective-permute-start(bf16[128,256]{1,0:T(8,128)(2,1)S(1)} %get-tuple-element.47), channel_id=1, source_target_pairs={{0,4},{1,5},{2,6},{3,7},{4,0},{5,1},{6,2},{7,3},{8,12},{9,13},{10,... | collective-permute-start | bytes 196616 | tf_op jit(solution)/shard_map/ppermute | solution.py:47
  23.6 1.6 %all-to-all-done.refs_0_ = bf16[64,16,128]{2,1,0:T(8,128)(2,1)S(1)} async-done(((bf16[64,16,128]{2,1,0:T(8,128)(2,1)}), bf16[64,16,128]{2,1,0:T(8,128)(2,1)S(1)}, u32[]{:S(2)}, u32[]{:S(2)}) %all-to-all-start) | async-done | bytes 262176 | tf_op jit(solution)/shard_map/all_to_all | solution.py:52
  25.2 6.4 %collective-permute-start.8 = (bf16[128,256]{1,0:T(8,128)(2,1)S(1)}, bf16[128,256]{1,0:T(8,128)(2,1)S(1)}, u32[]{:S(2)}, u32[]{:S(2)}) collective-permute-start(bf16[128,256]{1,0:T(8,128)(2,1)S(1)} %collect.1.refs_2_), channel_id=1, source_target_pairs={{0,8},{1,9},{2,10},{3,11},{4,12},{5,13},{6,14},{7,15},{8,0},{9,1},... | collective-permute-start | bytes 196616 | tf_op jit(solution)/shard_map/ppermute | solution.py:47
  31.6 0.0 collective-permute-start.7
  31.6 0.0 collective-permute-done.5.refs_2_
  31.6 1.1 %collective-permute-start.6 = (bf16[128,256]{1,0:T(8,128)(2,1)S(1)}, bf16[128,256]{1,0:T(8,128)(2,1)S(1)}, u32[]{:S(2)}, u32[]{:S(2)}) collective-permute-start(bf16[128,256]{1,0:T(8,128)(2,1)S(1)} %collect.1.refs_2_), channel_id=1, source_target_pairs={{0,4},{1,5},{2,6},{3,7},{4,0},{5,1},{6,2},{7,3},{8,12},{9,13},{10,... | collective-permute-start | bytes 196616 | tf_op jit(solution)/shard_map/ppermute | solution.py:47
  32.7 0.0 collective-permute-done.4.refs_1_
  32.7 0.0 collective-permute-done.3.refs_0_
  32.7 1.3 %first.1 = (bf16[2,768,256]{2,1,0:T(8,128)(2,1)S(1)}, bf16[2,512,128]{2,1,0:T(8,128)(2,1)S(1)}, bf16[2,512,128]{2,1,0:T(8,128)(2,1)S(1)}, f32[2,768,512]{2,1,0:T...) custom-call(bf16[512,512]{1,0:T(8,128)(2,1)S(1)} %get-tuple-element., ...), custom_call_target="tpu_custom_call" | custom-call | flops 402653184 | bytes 8466432 | tf_op jit(solution)/shard_map/first/pallas_call | solution.py:32
  34.0 0.0 collective-permute-done.8.refs_2_
  34.0 3.1 %collective-permute-done.7.refs_1_ = bf16[128,256]{1,0:T(8,128)(2,1)S(1)} collective-permute-done((bf16[128,256]{1,0:T(8,128)(2,1)S(1)}, bf16[128,256]{1,0:T(8,128)(2,1)S(1)}, u32[]{:S(2)}, u32[]{:S(2)}) %collective-permute-start.7) | collective-permute-done | bytes 65568 | tf_op jit(solution)/shard_map/ppermute | solution.py:47
  37.1 1.0 %collective-permute-done.6.refs_0_ = bf16[128,256]{1,0:T(8,128)(2,1)S(1)} collective-permute-done((bf16[128,256]{1,0:T(8,128)(2,1)S(1)}, bf16[128,256]{1,0:T(8,128)(2,1)S(1)}, u32[]{:S(2)}, u32[]{:S(2)}) %collective-permute-start.6) | collective-permute-done | bytes 65568 | tf_op jit(solution)/shard_map/ppermute | solution.py:47
  38.1 2.0 %second.1 = (bf16[256,256]{1,0:T(8,128)(2,1)S(1)}, bf16[192,256]{1,0:T(8,128)(2,1)S(1)}, bf16[192,256]{1,0:T(8,128)(2,1)S(1)}, bf16[640,256]{1,0:T(8,128)(2,1)S(...) custom-call(bf16[128,256]{1,0:T(8,128)(2,1)S(1)} %collective-permute, ...), custom_call_target="tpu_custom_call" | custom-call | flops 671088640 | bytes 10440704 | tf_op jit(solution)/shard_map/second/pallas_call | solution.py:32
  40.1 2.3 %collective-permute-start.9 = (bf16[256,256]{1,0:T(8,128)(2,1)S(1)}, bf16[256,256]{1,0:T(8,128)(2,1)S(1)}, u32[]{:S(2)}, u32[]{:S(2)}) collective-permute-start(bf16[256,256]{1,0:T(8,128)(2,1)S(1)} %get-tuple-element.64), channel_id=1, source_target_pairs={{0,4},{1,5},{2,6},{3,7},{4,0},{5,1},{6,2},{7,3},{8,12},{9,13},{10,... | collective-permute-start | bytes 393224 | tf_op jit(solution)/shard_map/ppermute | solution.py:47
  42.4 2.9 %collective-permute-start.10 = (bf16[192,256]{1,0:T(8,128)(2,1)S(1)}, bf16[192,256]{1,0:T(8,128)(2,1)S(1)}, u32[]{:S(2)}, u32[]{:S(2)}) collective-permute-start(bf16[192,256]{1,0:T(8,128)(2,1)S(1)} %get-tuple-element.65), channel_id=1, source_target_pairs={{0,8},{1,9},{2,10},{3,11},{4,12},{5,13},{6,14},{7,15},{8,0},{9,1},... | collective-permute-start | bytes 294920 | tf_op jit(solution)/shard_map/ppermute | solution.py:47
  45.3 0.6 collective-permute-start.11
  45.8 1.5 %rest.1 = (f32[128,256]{1,0:T(8,128)S(1)}, f32[256,256]{1,0:T(8,128)S(1)}, f32[512,256]{1,0:T(8,128)S(1)}, bf16[512,256]{1,0:T(8,128)(2,1)S(1)}) custom-call(bf16[2,768,256]{2,1,0:T(8,128)(2,1)S(1)} %get-tuple-element.49.refs_0_, bf16[640,256]{1,0:T(8,128)(2,1)S(1)} %get-tuple-element.57.refs_1_, bf16[2,512,128]{2,1,0:T(8,128)(2,1)S(1)} %get-tuple-element.50.refs_4_.refs_2_, ...), custom_call_target="tpu_custom_call" | custom-call | flops 1207959552 | bytes 11739136 | tf_op jit(solution)/shard_map/rest/pallas_call | solution.py:32
  47.3 5.1 %collective-permute-done.10.refs_2_ = bf16[192,256]{1,0:T(8,128)(2,1)S(1)} collective-permute-done((bf16[192,256]{1,0:T(8,128)(2,1)S(1)}, bf16[192,256]{1,0:T(8,128)(2,1)S(1)}, u32[]{:S(2)}, u32[]{:S(2)}) %collective-permute-start.10) | collective-permute-done | bytes 98336 | tf_op jit(solution)/shard_map/ppermute | solution.py:47
  52.5 2.6 %collective-permute-done.11.refs_3_ = bf16[192,256]{1,0:T(8,128)(2,1)S(1)} collective-permute-done((bf16[192,256]{1,0:T(8,128)(2,1)S(1)}, bf16[192,256]{1,0:T(8,128)(2,1)S(1)}, u32[]{:S(2)}, u32[]{:S(2)}) %collective-permute-start.11) | collective-permute-done | bytes 98336 | tf_op jit(solution)/shard_map/ppermute | solution.py:47
  55.0 0.0 collective-permute-done.9.refs_1_
  55.0 0.8 %scatter.1 = (bf16[64,16,128]{2,1,0:T(8,128)(2,1)}, f32[128,256]{1,0:T(8,128)S(1)}, bf16[128,512]{1,0:T(8,128)(2,1)S(1)}, bf16[128,512]{1,0:T(8,128)(2,1)S(1)}, bf16[128,512]{1,0:T(8,128)(2,1)S(1)}) custom-call(f32[128,256]{1,0:T(8,128)S(1)} %get-tuple-element.63.refs_0_, bf16[256,256]{1,0:T(8,128)(2,1)S(1)} %collective-permute-done.9.refs_1_, ...), custom_call_target="tpu_custom_call" | custom-call | bytes 2293760 | tf_op jit(solution)/shard_map/scatter/pallas_call | solution.py:32
  55.9 0.8 %collective-permute-start.12 = (bf16[128,512]{1,0:T(8,128)(2,1)S(1)}, bf16[128,512]{1,0:T(8,128)(2,1)S(1)}, u32[]{:S(2)}, u32[]{:S(2)}) collective-permute-start(bf16[128,512]{1,0:T(8,128)(2,1)S(1)} %get-tuple-element.70), channel_id=1, source_target_pairs={{0,1},{1,0},{2,3},{3,2},{4,5},{5,4},{6,7},{7,6},{8,9},{9,8},{10,11... | collective-permute-start | bytes 393224 | tf_op jit(solution)/shard_map/ppermute | solution.py:47
  56.7 1.5 %collective-permute-start.13 = (bf16[128,512]{1,0:T(8,128)(2,1)S(1)}, bf16[128,512]{1,0:T(8,128)(2,1)S(1)}, u32[]{:S(2)}, u32[]{:S(2)}) collective-permute-start(bf16[128,512]{1,0:T(8,128)(2,1)S(1)} %get-tuple-element.71), channel_id=1, source_target_pairs={{0,2},{1,3},{2,0},{3,1},{4,6},{5,7},{6,4},{7,5},{8,10},{9,11},{10,... | collective-permute-start | bytes 393224 | tf_op jit(solution)/shard_map/ppermute | solution.py:47
  58.2 0.1 collective-permute-start.14
  58.3 7.0 %all-to-all-start.1 = ((bf16[64,16,128]{2,1,0:T(8,128)(2,1)}), bf16[64,16,128]{2,1,0:T(8,128)(2,1)S(1)}, u32[]{:S(2)}, u32[]{:S(2)}) async-start(bf16[64,16,128]{2,1,0:T(8,128)(2,1)} %get-tuple-element.75), calls=%async_computation.1 | async-start | bytes 524288 | tf_op jit(solution)/shard_map/all_to_all | solution.py:52
  65.3 0.0 collective-permute-done.12.refs_2_
  65.3 0.0 collective-permute-done.13.refs_3_
  65.3 0.0 collective-permute-done.14.refs_4_
  65.3 0.8 %merge.1 = (bf16[128,512]{1,0:T(8,128)(2,1)}, bf16[128,512]{1,0:T(8,128)(2,1)}, f32[128,1024]{1,0:T(8,128)S(1)}) custom-call(bf16[512,256]{1,0:T(8,128)(2,1)S(1)} %get-tuple-element.62.refs_6_.refs_0_, f32[128,256]{1,0:T(8,128)S(1)} %get-tuple-element.69.refs_1_, bf16[128,512]{1,0:T(8,128)(2,1)S(1)} %collective-permute-done.12.refs_2_, ...), custom_call_target="tpu_custom_call" | custom-call | flops 20000000000 | bytes 1572864 | tf_op jit(solution)/shard_map/merge/pallas_call | solution.py:32
  66.1 9.2 %all-to-all-done.1.refs_0_ = bf16[64,16,128]{2,1,0:T(8,128)(2,1)S(1)} async-done(((bf16[64,16,128]{2,1,0:T(8,128)(2,1)}), bf16[64,16,128]{2,1,0:T(8,128)(2,1)S(1)}, u32[]{:S(2)}, u32[]{:S(2)}) %all-to-all-start.1) | async-done | bytes 262176 | tf_op jit(solution)/shard_map/all_to_all | solution.py:52
  75.3 0.8 %finish.1 = bf16[128,1024]{1,0:T(8,128)(2,1)} custom-call(bf16[64,16,128]{2,1,0:T(8,128)(2,1)S(1)} %all-to-all-done.1.refs_0_, f32[128,1024]{1,0:T(8,128)S(1)} %get-tuple-element.76.refs_1_), custom_call_target="tpu_custom_call" | custom-call | bytes 1048576 | tf_op jit(solution)/shard_map/finish/pallas_call | solution.py:32
  (2 shorter events, 0.0 us)
Async XLA Ops:
  2.8 12.3 %collective-permute-start = (bf16[128,512]{1,0:T(8,128)(2,1)}, bf16[128,512]{1,0:T(8,128)(2,1)S(1)}, u32[]{:S(2)}, u32[]{:S(2)}) collective-permute-start(bf16[128,512]{1,0:T(8,128)(2,1)} %get-tuple-element.41), channel_id=1, source_target_pairs={{0,1},{1,0},{2,3},{3,2},{4,5},{5,4},{6,7},{7,6},{8,9},{9,8},{10,11... | collective-permute-start | bytes 393224 | tf_op jit(solution)/shard_map/ppermute | solution.py:47
  6.1 9.0 %collective-permute-start.1 = (bf16[128,512]{1,0:T(8,128)(2,1)}, bf16[128,512]{1,0:T(8,128)(2,1)S(1)}, u32[]{:S(2)}, u32[]{:S(2)}) collective-permute-start(bf16[128,512]{1,0:T(8,128)(2,1)} %get-tuple-element.42), channel_id=1, source_target_pairs={{0,2},{1,3},{2,0},{3,1},{4,6},{5,7},{6,4},{7,5},{8,10},{9,11},{10,... | collective-permute-start | bytes 393224 | tf_op jit(solution)/shard_map/ppermute | solution.py:47
  6.1 9.0 %collective-permute-start.2 = (bf16[128,512]{1,0:T(8,128)(2,1)}, bf16[128,512]{1,0:T(8,128)(2,1)S(1)}, u32[]{:S(2)}, u32[]{:S(2)}) collective-permute-start(bf16[128,512]{1,0:T(8,128)(2,1)} %get-tuple-element.43), channel_id=1, source_target_pairs={{0,3},{1,2},{2,1},{3,0},{4,7},{5,6},{6,5},{7,4},{8,11},{9,10},{10,... | collective-permute-start | bytes 393224 | tf_op jit(solution)/shard_map/ppermute | solution.py:47
  7.9 17.3 %all-to-all-start = ((bf16[64,16,128]{2,1,0:T(8,128)(2,1)}), bf16[64,16,128]{2,1,0:T(8,128)(2,1)S(1)}, u32[]{:S(2)}, u32[]{:S(2)}) async-start(bf16[64,16,128]{2,1,0:T(8,128)(2,1)} %get-tuple-element.46), calls=%async_computation | async-start | bytes 524288 | tf_op jit(solution)/shard_map/all_to_all | solution.py:52
  15.2 0.9 %copy-start = (bf16[128,512]{1,0:T(8,128)(2,1)S(1)}, bf16[128,512]{1,0:T(8,128)(2,1)}, u32[]{:S(2)}) copy-start(bf16[128,512]{1,0:T(8,128)(2,1)} %get-tuple-element.40.refs_0_) | copy-start | bytes 393220
  16.3 15.4 %collective-permute-start.5 = (bf16[64,256]{1,0:T(8,128)(2,1)S(1)}, bf16[64,256]{1,0:T(8,128)(2,1)S(1)}, u32[]{:S(2)}, u32[]{:S(2)}) collective-permute-start(bf16[64,256]{1,0:T(8,128)(2,1)S(1)} %get-tuple-element.48), channel_id=1, source_target_pairs={{0,8},{1,9},{2,10},{3,11},{4,12},{5,13},{6,14},{7,15},{8,0},{9,1},... | collective-permute-start | bytes 98312 | tf_op jit(solution)/shard_map/ppermute | solution.py:47
  22.4 10.3 %collective-permute-start.4 = (bf16[64,256]{1,0:T(8,128)(2,1)S(1)}, bf16[64,256]{1,0:T(8,128)(2,1)S(1)}, u32[]{:S(2)}, u32[]{:S(2)}) collective-permute-start(bf16[64,256]{1,0:T(8,128)(2,1)S(1)} %get-tuple-element.48), channel_id=1, source_target_pairs={{0,12},{1,13},{2,14},{3,15},{4,8},{5,9},{6,10},{7,11},{8,4},{9,5},... | collective-permute-start | bytes 98312 | tf_op jit(solution)/shard_map/ppermute | solution.py:47
  22.6 10.0 %collective-permute-start.3 = (bf16[128,256]{1,0:T(8,128)(2,1)S(1)}, bf16[128,256]{1,0:T(8,128)(2,1)S(1)}, u32[]{:S(2)}, u32[]{:S(2)}) collective-permute-start(bf16[128,256]{1,0:T(8,128)(2,1)S(1)} %get-tuple-element.47), channel_id=1, source_target_pairs={{0,4},{1,5},{2,6},{3,7},{4,0},{5,1},{6,2},{7,3},{8,12},{9,13},{10,... | collective-permute-start | bytes 196616 | tf_op jit(solution)/shard_map/ppermute | solution.py:47
  25.2 8.8 %collective-permute-start.8 = (bf16[128,256]{1,0:T(8,128)(2,1)S(1)}, bf16[128,256]{1,0:T(8,128)(2,1)S(1)}, u32[]{:S(2)}, u32[]{:S(2)}) collective-permute-start(bf16[128,256]{1,0:T(8,128)(2,1)S(1)} %collect.1.refs_2_), channel_id=1, source_target_pairs={{0,8},{1,9},{2,10},{3,11},{4,12},{5,13},{6,14},{7,15},{8,0},{9,1},... | collective-permute-start | bytes 196616 | tf_op jit(solution)/shard_map/ppermute | solution.py:47
  31.6 5.5 %collective-permute-start.7 = (bf16[128,256]{1,0:T(8,128)(2,1)S(1)}, bf16[128,256]{1,0:T(8,128)(2,1)S(1)}, u32[]{:S(2)}, u32[]{:S(2)}) collective-permute-start(bf16[128,256]{1,0:T(8,128)(2,1)S(1)} %collect.1.refs_2_), channel_id=1, source_target_pairs={{0,12},{1,13},{2,14},{3,15},{4,8},{5,9},{6,10},{7,11},{8,4},{9,5},... | collective-permute-start | bytes 196616 | tf_op jit(solution)/shard_map/ppermute | solution.py:47
  31.6 6.5 %collective-permute-start.6 = (bf16[128,256]{1,0:T(8,128)(2,1)S(1)}, bf16[128,256]{1,0:T(8,128)(2,1)S(1)}, u32[]{:S(2)}, u32[]{:S(2)}) collective-permute-start(bf16[128,256]{1,0:T(8,128)(2,1)S(1)} %collect.1.refs_2_), channel_id=1, source_target_pairs={{0,4},{1,5},{2,6},{3,7},{4,0},{5,1},{6,2},{7,3},{8,12},{9,13},{10,... | collective-permute-start | bytes 196616 | tf_op jit(solution)/shard_map/ppermute | solution.py:47
  40.1 14.9 %collective-permute-start.9 = (bf16[256,256]{1,0:T(8,128)(2,1)S(1)}, bf16[256,256]{1,0:T(8,128)(2,1)S(1)}, u32[]{:S(2)}, u32[]{:S(2)}) collective-permute-start(bf16[256,256]{1,0:T(8,128)(2,1)S(1)} %get-tuple-element.64), channel_id=1, source_target_pairs={{0,4},{1,5},{2,6},{3,7},{4,0},{5,1},{6,2},{7,3},{8,12},{9,13},{10,... | collective-permute-start | bytes 393224 | tf_op jit(solution)/shard_map/ppermute | solution.py:47
  42.4 10.1 %collective-permute-start.10 = (bf16[192,256]{1,0:T(8,128)(2,1)S(1)}, bf16[192,256]{1,0:T(8,128)(2,1)S(1)}, u32[]{:S(2)}, u32[]{:S(2)}) collective-permute-start(bf16[192,256]{1,0:T(8,128)(2,1)S(1)} %get-tuple-element.65), channel_id=1, source_target_pairs={{0,8},{1,9},{2,10},{3,11},{4,12},{5,13},{6,14},{7,15},{8,0},{9,1},... | collective-permute-start | bytes 294920 | tf_op jit(solution)/shard_map/ppermute | solution.py:47
  45.3 9.8 %collective-permute-start.11 = (bf16[192,256]{1,0:T(8,128)(2,1)S(1)}, bf16[192,256]{1,0:T(8,128)(2,1)S(1)}, u32[]{:S(2)}, u32[]{:S(2)}) collective-permute-start(bf16[192,256]{1,0:T(8,128)(2,1)S(1)} %get-tuple-element.66), channel_id=1, source_target_pairs={{0,12},{1,13},{2,14},{3,15},{4,8},{5,9},{6,10},{7,11},{8,4},{9,5},... | collective-permute-start | bytes 294920 | tf_op jit(solution)/shard_map/ppermute | solution.py:47
  55.9 9.4 %collective-permute-start.12 = (bf16[128,512]{1,0:T(8,128)(2,1)S(1)}, bf16[128,512]{1,0:T(8,128)(2,1)S(1)}, u32[]{:S(2)}, u32[]{:S(2)}) collective-permute-start(bf16[128,512]{1,0:T(8,128)(2,1)S(1)} %get-tuple-element.70), channel_id=1, source_target_pairs={{0,1},{1,0},{2,3},{3,2},{4,5},{5,4},{6,7},{7,6},{8,9},{9,8},{10,11... | collective-permute-start | bytes 393224 | tf_op jit(solution)/shard_map/ppermute | solution.py:47
  56.7 8.6 %collective-permute-start.13 = (bf16[128,512]{1,0:T(8,128)(2,1)S(1)}, bf16[128,512]{1,0:T(8,128)(2,1)S(1)}, u32[]{:S(2)}, u32[]{:S(2)}) collective-permute-start(bf16[128,512]{1,0:T(8,128)(2,1)S(1)} %get-tuple-element.71), channel_id=1, source_target_pairs={{0,2},{1,3},{2,0},{3,1},{4,6},{5,7},{6,4},{7,5},{8,10},{9,11},{10,... | collective-permute-start | bytes 393224 | tf_op jit(solution)/shard_map/ppermute | solution.py:47
  58.2 7.1 %collective-permute-start.14 = (bf16[128,512]{1,0:T(8,128)(2,1)S(1)}, bf16[128,512]{1,0:T(8,128)(2,1)S(1)}, u32[]{:S(2)}, u32[]{:S(2)}) collective-permute-start(bf16[128,512]{1,0:T(8,128)(2,1)S(1)} %get-tuple-element.72), channel_id=1, source_target_pairs={{0,3},{1,2},{2,1},{3,0},{4,7},{5,6},{6,5},{7,4},{8,11},{9,10},{10,... | collective-permute-start | bytes 393224 | tf_op jit(solution)/shard_map/ppermute | solution.py:47
  58.3 17.0 %all-to-all-start.1 = ((bf16[64,16,128]{2,1,0:T(8,128)(2,1)}), bf16[64,16,128]{2,1,0:T(8,128)(2,1)S(1)}, u32[]{:S(2)}, u32[]{:S(2)}) async-start(bf16[64,16,128]{2,1,0:T(8,128)(2,1)} %get-tuple-element.75), calls=%async_computation.1 | async-start | bytes 524288 | tf_op jit(solution)/shard_map/all_to_all | solution.py:52

commit v2 on v1

--- a/solution.py
+++ b/solution.py
@@ -37,7 +37,7 @@
             scratch_shapes=list(scratch),
             name=name,
             cost_estimate=pl.CostEstimate(flops=flops, bytes_accessed=moved, transcendentals=0),
-            compiler_params=pltpu.CompilerParams(vmem_limit_bytes=limit * 1024 * 1024),
+            compiler_params=pltpu.CompilerParams(vmem_limit_bytes=int(limit * 1024 * 1024)),
         )(*operands)
 
     return run
@@ -275,6 +275,10 @@
     return functools.reduce(jnp.add, [p.astype(F32) for p in parts])
 
 
+def hold_kernel(got_ref, out_ref):
+    out_ref[...] = got_ref[...]
+
+
 def scatter_kernel(
     block_ref, back2_ref, back4_ref, back6_ref, one_ref, zero_ref, results_ref,
     slots_ref, own_ref, out1_ref, out2_ref, out3_ref, rows_ref,
@@ -337,7 +341,7 @@
     team_rows = pltpu.VMEM((2, TEAM * LEAF, 128), F32)
 
     sent, own, out1, out2, out3 = call(
-        pool_kernel, "pool", [slots, piece, piece, piece, piece], [*loaded, own_rows, pltpu.SemaphoreType.DMA((3,))], spec=HBM, limit=56
+        pool_kernel, "pool", [slots, piece, piece, piece, piece], [*loaded, own_rows, pltpu.SemaphoreType.DMA((3,))], spec=HBM, limit=53.375
     )(queries, keys_values, cotangent)
     taken = trade_slots(sent)
     got2 = exchange(out2, 2)
@@ -385,6 +389,7 @@
         flops=8 * 1152 * 1024 * 128,
     )(keys, later_keys, q2, cot2, exps, dweights, factor, centre, rounded, dscores)
 
+    (back4,) = call(hold_kernel, "hold", [((192, 256), BF16)], flops=LONG)(back4)
     sent, own, out1, out2, out3 = call(
         scatter_kernel, "scatter", [slots, ((LEAF, 256), F32), piece, piece, piece], [team_rows]
     )(block, back2, back4, back6, one, zero, results)

time: 76.4 us -> 74.2 us (0.971)
  starting transfers between devices: 42.3 us -> 40.3 us
  waiting for transfers between devices: 22.6 us -> 23.6 us
  local copies, waits for them, and re-layouts: 0.9 us -> 0 us
    all_to_all x2, starting transfers between devices: 14.2 us -> 12.2 us  [trade_slots(): lax.all_to_all(slots, ('outer', 'inner'), 0, 0, axis_index_groups=groups,...]
    ppermute x15, waiting for transfers between devices: 11.9 us -> 13.3 us  [exchange(): return lax.ppermute(array, 'inner', [(i, i ^ bits) for i in range(16)])]
    unnamed x2 -> x0, local copies, waits for them, and re-layouts: 0.9 us -> none
    pallas_call x10 -> x11, Pallas kernels: 9.58 us -> 9.42 us  [run(): pl.pallas_call(lambda *refs: body(*refs[:count], *refs[count + len(after)...]
  transfers between devices with their start and end apart: 17 -> 17, of which waited for: 6 -> 8; matrix products, arithmetic and copies ran while one was open for 0% -> 0% of each run, Pallas kernels for 5% -> 5%
where the time goes in v2:
time: 74.2 us; the launch traced here: 74 us
  starting transfers between devices  40.3 us (54%)
  waiting for transfers between devices  23.6 us (32%)
  Pallas kernels  9.42 us (13%)
  between operations  0.75 us (1%)
    ppermute x15, starting transfers between devices, exchange(): return lax.ppermute(array, 'inner', [(i, i ^ bits) for i in range(16)])  28.1 us
    ppermute x15, waiting for transfers between devices, exchange(): return lax.ppermute(array, 'inner', [(i, i ^ bits) for i in range(16)])  13.3 us
    all_to_all x2, starting transfers between devices, trade_slots(): lax.all_to_all(slots, ('outer', 'inner'), 0, 0, axis_index_groups=groups,...  12.2 us
    all_to_all x2, waiting for transfers between devices, trade_slots(): lax.all_to_all(slots, ('outer', 'inner'), 0, 0, axis_index_groups=groups,...  10.2 us
    pallas_call x11, Pallas kernels, run(): pl.pallas_call(lambda *refs: body(*refs[:count], *refs[count + len(after)...  9.42 us
  transfers between devices with their start and end apart: 17, of which 8 were waited for; matrix products, arithmetic and copies ran while one was open for 0% of the time, Pallas kernels for 5%

profile of v2, /device:TPU:1, one launch (start us, length us, event | category | flops | bytes accessed | tf_op | source)
XLA Modules:
  0.0 74.0 jit_solution(4127760954253968532)
XLA Ops:
  0.6 2.0 %pool.1 = (bf16[64,16,128]{2,1,0:T(8,128)(2,1)}, bf16[128,512]{1,0:T(8,128)(2,1)S(1)}, bf16[128,512]{1,0:T(8,128)(2,1)S(1)}, bf16[128,512]{1,0:T(8,128)(2,1)S(1)}, bf16[128,512]{1,0:T(8,128)(2,1)S(1)}) custom-call(bf16[128,512]{1,0:T(8,128)(2,1)} %bitcast.8, bf16[128,1024]{1,0:T(8,128)(2,1)} %bitcast.6, bf16[128,512]{1,0:T(8,128)(2,1)} %bitcast.9), custom_call_target="tpu_custom_call" | custom-call | bytes 1310720 | tf_op jit(solution)/shard_map/pool/pallas_call | solution.py:32
  2.7 3.3 %collective-permute-start = (bf16[128,512]{1,0:T(8,128)(2,1)S(1)}, bf16[128,512]{1,0:T(8,128)(2,1)S(1)}, u32[]{:S(2)}, u32[]{:S(2)}) collective-permute-start(bf16[128,512]{1,0:T(8,128)(2,1)S(1)} %get-tuple-element.41), channel_id=1, source_target_pairs={{0,1},{1,0},{2,3},{3,2},{4,5},{5,4},{6,7},{7,6},{8,9},{9,8},{10,11... | collective-permute-start | bytes 393224 | tf_op jit(solution)/shard_map/ppermute | solution.py:47
  6.0 0.0 collective-permute-start.1
  6.0 1.7 %collective-permute-start.2 = (bf16[128,512]{1,0:T(8,128)(2,1)S(1)}, bf16[128,512]{1,0:T(8,128)(2,1)S(1)}, u32[]{:S(2)}, u32[]{:S(2)}) collective-permute-start(bf16[128,512]{1,0:T(8,128)(2,1)S(1)} %get-tuple-element.43), channel_id=1, source_target_pairs={{0,3},{1,2},{2,1},{3,0},{4,7},{5,6},{6,5},{7,4},{8,11},{9,10},{10,... | collective-permute-start | bytes 393224 | tf_op jit(solution)/shard_map/ppermute | solution.py:47
  7.7 7.3 %all-to-all-start = ((bf16[64,16,128]{2,1,0:T(8,128)(2,1)}), bf16[64,16,128]{2,1,0:T(8,128)(2,1)S(1)}, u32[]{:S(2)}, u32[]{:S(2)}) async-start(bf16[64,16,128]{2,1,0:T(8,128)(2,1)} %get-tuple-element.46), calls=%async_computation | async-start | bytes 524288 | tf_op jit(solution)/shard_map/all_to_all | solution.py:52
  15.0 0.0 collective-permute-done.refs_1_
  15.0 0.0 collective-permute-done.1.refs_2_
  15.0 0.0 collective-permute-done.2.refs_3_
  15.0 0.2 team.1
  15.2 6.1 %collective-permute-start.5 = (bf16[64,256]{1,0:T(8,128)(2,1)S(1)}, bf16[64,256]{1,0:T(8,128)(2,1)S(1)}, u32[]{:S(2)}, u32[]{:S(2)}) collective-permute-start(bf16[64,256]{1,0:T(8,128)(2,1)S(1)} %get-tuple-element.48), channel_id=1, source_target_pairs={{0,8},{1,9},{2,10},{3,11},{4,12},{5,13},{6,14},{7,15},{8,0},{9,1},... | collective-permute-start | bytes 98312 | tf_op jit(solution)/shard_map/ppermute | solution.py:47
  21.3 0.3 collective-permute-start.4
  21.6 0.9 %collective-permute-start.3 = (bf16[128,256]{1,0:T(8,128)(2,1)S(1)}, bf16[128,256]{1,0:T(8,128)(2,1)S(1)}, u32[]{:S(2)}, u32[]{:S(2)}) collective-permute-start(bf16[128,256]{1,0:T(8,128)(2,1)S(1)} %get-tuple-element.47), channel_id=1, source_target_pairs={{0,4},{1,5},{2,6},{3,7},{4,0},{5,1},{6,2},{7,3},{8,12},{9,13},{10,... | collective-permute-start | bytes 196616 | tf_op jit(solution)/shard_map/ppermute | solution.py:47
  22.5 2.5 %all-to-all-done.refs_0_ = bf16[64,16,128]{2,1,0:T(8,128)(2,1)S(1)} async-done(((bf16[64,16,128]{2,1,0:T(8,128)(2,1)}), bf16[64,16,128]{2,1,0:T(8,128)(2,1)S(1)}, u32[]{:S(2)}, u32[]{:S(2)}) %all-to-all-start) | async-done | bytes 262176 | tf_op jit(solution)/shard_map/all_to_all | solution.py:52
  25.0 6.4 %collective-permute-start.8 = (bf16[128,256]{1,0:T(8,128)(2,1)S(1)}, bf16[128,256]{1,0:T(8,128)(2,1)S(1)}, u32[]{:S(2)}, u32[]{:S(2)}) collective-permute-start(bf16[128,256]{1,0:T(8,128)(2,1)S(1)} %collect.1.refs_2_), channel_id=1, source_target_pairs={{0,8},{1,9},{2,10},{3,11},{4,12},{5,13},{6,14},{7,15},{8,0},{9,1},... | collective-permute-start | bytes 196616 | tf_op jit(solution)/shard_map/ppermute | solution.py:47
  31.5 0.0 collective-permute-start.7
  31.5 0.0 collective-permute-done.5.refs_2_
  31.5 1.2 %collective-permute-start.6 = (bf16[128,256]{1,0:T(8,128)(2,1)S(1)}, bf16[128,256]{1,0:T(8,128)(2,1)S(1)}, u32[]{:S(2)}, u32[]{:S(2)}) collective-permute-start(bf16[128,256]{1,0:T(8,128)(2,1)S(1)} %collect.1.refs_2_), channel_id=1, source_target_pairs={{0,4},{1,5},{2,6},{3,7},{4,0},{5,1},{6,2},{7,3},{8,12},{9,13},{10,... | collective-permute-start | bytes 196616 | tf_op jit(solution)/shard_map/ppermute | solution.py:47
  32.7 0.0 collective-permute-done.4.refs_1_
  32.7 0.0 collective-permute-done.3.refs_0_
  32.7 1.3 %first.1 = (bf16[2,768,256]{2,1,0:T(8,128)(2,1)S(1)}, bf16[2,512,128]{2,1,0:T(8,128)(2,1)S(1)}, bf16[2,512,128]{2,1,0:T(8,128)(2,1)S(1)}, f32[2,768,512]{2,1,0:T...) custom-call(bf16[512,512]{1,0:T(8,128)(2,1)S(1)} %get-tuple-element., ...), custom_call_target="tpu_custom_call" | custom-call | flops 402653184 | bytes 8466432 | tf_op jit(solution)/shard_map/first/pallas_call | solution.py:32
  34.0 0.0 collective-permute-done.8.refs_2_
  34.0 3.1 %collective-permute-done.7.refs_1_ = bf16[128,256]{1,0:T(8,128)(2,1)S(1)} collective-permute-done((bf16[128,256]{1,0:T(8,128)(2,1)S(1)}, bf16[128,256]{1,0:T(8,128)(2,1)S(1)}, u32[]{:S(2)}, u32[]{:S(2)}) %collective-permute-start.7) | collective-permute-done | bytes 65568 | tf_op jit(solution)/shard_map/ppermute | solution.py:47
  37.1 0.7 collective-permute-done.6.refs_0_
  37.7 2.0 %second.1 = (bf16[256,256]{1,0:T(8,128)(2,1)S(1)}, bf16[192,256]{1,0:T(8,128)(2,1)S(1)}, bf16[192,256]{1,0:T(8,128)(2,1)S(1)}, bf16[640,256]{1,0:T(8,128)(2,1)S(...) custom-call(bf16[128,256]{1,0:T(8,128)(2,1)S(1)} %collective-permute, ...), custom_call_target="tpu_custom_call" | custom-call | flops 671088640 | bytes 10440704 | tf_op jit(solution)/shard_map/second/pallas_call | solution.py:32
  39.7 4.6 %collective-permute-start.10 = (bf16[192,256]{1,0:T(8,128)(2,1)S(1)}, bf16[192,256]{1,0:T(8,128)(2,1)S(1)}, u32[]{:S(2)}, u32[]{:S(2)}) collective-permute-start(bf16[192,256]{1,0:T(8,128)(2,1)S(1)} %get-tuple-element.65), channel_id=1, source_target_pairs={{0,8},{1,9},{2,10},{3,11},{4,12},{5,13},{6,14},{7,15},{8,0},{9,1},... | collective-permute-start | bytes 294920 | tf_op jit(solution)/shard_map/ppermute | solution.py:47
  44.3 1.4 %collective-permute-start.11 = (bf16[192,256]{1,0:T(8,128)(2,1)S(1)}, bf16[192,256]{1,0:T(8,128)(2,1)S(1)}, u32[]{:S(2)}, u32[]{:S(2)}) collective-permute-start(bf16[192,256]{1,0:T(8,128)(2,1)S(1)} %get-tuple-element.66), channel_id=1, source_target_pairs={{0,12},{1,13},{2,14},{3,15},{4,8},{5,9},{6,10},{7,11},{8,4},{9,5},... | collective-permute-start | bytes 294920 | tf_op jit(solution)/shard_map/ppermute | solution.py:47
  45.7 0.0 collective-permute-start.9
  45.7 1.5 %rest.1 = (f32[128,256]{1,0:T(8,128)S(1)}, f32[256,256]{1,0:T(8,128)S(1)}, f32[512,256]{1,0:T(8,128)S(1)}, bf16[512,256]{1,0:T(8,128)(2,1)S(1)}) custom-call(bf16[2,768,256]{2,1,0:T(8,128)(2,1)S(1)} %get-tuple-element.49.refs_0_, bf16[640,256]{1,0:T(8,128)(2,1)S(1)} %get-tuple-element.57.refs_1_, bf16[2,512,128]{2,1,0:T(8,128)(2,1)S(1)} %get-tuple-element.50.refs_4_.refs_2_, ...), custom_call_target="tpu_custom_call" | custom-call | flops 1207959552 | bytes 11739136 | tf_op jit(solution)/shard_map/rest/pallas_call | solution.py:32
  47.1 0.2 collective-permute-done.10.refs_0_
  47.3 7.1 %collective-permute-done.11.refs_3_ = bf16[192,256]{1,0:T(8,128)(2,1)S(1)} collective-permute-done((bf16[192,256]{1,0:T(8,128)(2,1)S(1)}, bf16[192,256]{1,0:T(8,128)(2,1)S(1)}, u32[]{:S(2)}, u32[]{:S(2)}) %collective-permute-start.11) | collective-permute-done | bytes 98336 | tf_op jit(solution)/shard_map/ppermute | solution.py:47
  54.4 0.9 %collective-permute-done.9.refs_1_ = bf16[256,256]{1,0:T(8,128)(2,1)S(1)} collective-permute-done((bf16[256,256]{1,0:T(8,128)(2,1)S(1)}, bf16[256,256]{1,0:T(8,128)(2,1)S(1)}, u32[]{:S(2)}, u32[]{:S(2)}) %collective-permute-start.9) | collective-permute-done | bytes 131104 | tf_op jit(solution)/shard_map/ppermute | solution.py:47
  55.3 0.8 %scatter.1 = (bf16[64,16,128]{2,1,0:T(8,128)(2,1)}, f32[128,256]{1,0:T(8,128)S(1)}, bf16[128,512]{1,0:T(8,128)(2,1)S(1)}, bf16[128,512]{1,0:T(8,128)(2,1)S(1)}, bf16[128,512]{1,0:T(8,128)(2,1)S(1)}) custom-call(f32[128,256]{1,0:T(8,128)S(1)} %get-tuple-element.63.refs_0_, bf16[256,256]{1,0:T(8,128)(2,1)S(1)} %collective-permute-done.9.refs_1_, ...), custom_call_target="tpu_custom_call" | custom-call | bytes 2293760 | tf_op jit(solution)/shard_map/scatter/pallas_call | solution.py:32
  56.1 0.5 collective-permute-start.12
  56.6 0.6 collective-permute-start.13
  57.3 1.0 %collective-permute-start.14 = (bf16[128,512]{1,0:T(8,128)(2,1)S(1)}, bf16[128,512]{1,0:T(8,128)(2,1)S(1)}, u32[]{:S(2)}, u32[]{:S(2)}) collective-permute-start(bf16[128,512]{1,0:T(8,128)(2,1)S(1)} %get-tuple-element.72), channel_id=1, source_target_pairs={{0,3},{1,2},{2,1},{3,0},{4,7},{5,6},{6,5},{7,4},{8,11},{9,10},{10,... | collective-permute-start | bytes 393224 | tf_op jit(solution)/shard_map/ppermute | solution.py:47
  58.3 4.9 %all-to-all-start.1 = ((bf16[64,16,128]{2,1,0:T(8,128)(2,1)}), bf16[64,16,128]{2,1,0:T(8,128)(2,1)S(1)}, u32[]{:S(2)}, u32[]{:S(2)}) async-start(bf16[64,16,128]{2,1,0:T(8,128)(2,1)} %get-tuple-element.75), calls=%async_computation.1 | async-start | bytes 524288 | tf_op jit(solution)/shard_map/all_to_all | solution.py:52
  63.2 0.0 collective-permute-done.12.refs_2_
  63.2 0.0 collective-permute-done.13.refs_3_
  63.2 1.4 %collective-permute-done.14.refs_4_ = bf16[128,512]{1,0:T(8,128)(2,1)S(1)} collective-permute-done((bf16[128,512]{1,0:T(8,128)(2,1)S(1)}, bf16[128,512]{1,0:T(8,128)(2,1)S(1)}, u32[]{:S(2)}, u32[]{:S(2)}) %collective-permute-start.14) | collective-permute-done | bytes 131104 | tf_op jit(solution)/shard_map/ppermute | solution.py:47
  64.7 0.8 %merge.1 = (bf16[128,512]{1,0:T(8,128)(2,1)}, bf16[128,512]{1,0:T(8,128)(2,1)}, f32[128,1024]{1,0:T(8,128)S(1)}) custom-call(bf16[512,256]{1,0:T(8,128)(2,1)S(1)} %get-tuple-element.62.refs_6_.refs_0_, f32[128,256]{1,0:T(8,128)S(1)} %get-tuple-element.69.refs_1_, bf16[128,512]{1,0:T(8,128)(2,1)S(1)} %collective-permute-done.12.refs_2_, ...), custom_call_target="tpu_custom_call" | custom-call | flops 20000000000 | bytes 1572864 | tf_op jit(solution)/shard_map/merge/pallas_call | solution.py:32
  65.5 7.7 %all-to-all-done.1.refs_0_ = bf16[64,16,128]{2,1,0:T(8,128)(2,1)S(1)} async-done(((bf16[64,16,128]{2,1,0:T(8,128)(2,1)}), bf16[64,16,128]{2,1,0:T(8,128)(2,1)S(1)}, u32[]{:S(2)}, u32[]{:S(2)}) %all-to-all-start.1) | async-done | bytes 262176 | tf_op jit(solution)/shard_map/all_to_all | solution.py:52
  73.2 0.8 %finish.1 = bf16[128,1024]{1,0:T(8,128)(2,1)} custom-call(bf16[64,16,128]{2,1,0:T(8,128)(2,1)S(1)} %all-to-all-done.1.refs_0_, f32[128,1024]{1,0:T(8,128)S(1)} %get-tuple-element.76.refs_1_), custom_call_target="tpu_custom_call" | custom-call | bytes 1048576 | tf_op jit(solution)/shard_map/finish/pallas_call | solution.py:32
  (3 shorter events, 0.1 us)
Async XLA Ops:
  2.7 12.3 %collective-permute-start = (bf16[128,512]{1,0:T(8,128)(2,1)S(1)}, bf16[128,512]{1,0:T(8,128)(2,1)S(1)}, u32[]{:S(2)}, u32[]{:S(2)}) collective-permute-start(bf16[128,512]{1,0:T(8,128)(2,1)S(1)} %get-tuple-element.41), channel_id=1, source_target_pairs={{0,1},{1,0},{2,3},{3,2},{4,5},{5,4},{6,7},{7,6},{8,9},{9,8},{10,11... | collective-permute-start | bytes 393224 | tf_op jit(solution)/shard_map/ppermute | solution.py:47
  6.0 9.0 %collective-permute-start.1 = (bf16[128,512]{1,0:T(8,128)(2,1)S(1)}, bf16[128,512]{1,0:T(8,128)(2,1)S(1)}, u32[]{:S(2)}, u32[]{:S(2)}) collective-permute-start(bf16[128,512]{1,0:T(8,128)(2,1)S(1)} %get-tuple-element.42), channel_id=1, source_target_pairs={{0,2},{1,3},{2,0},{3,1},{4,6},{5,7},{6,4},{7,5},{8,10},{9,11},{10,... | collective-permute-start | bytes 393224 | tf_op jit(solution)/shard_map/ppermute | solution.py:47
  6.0 9.0 %collective-permute-start.2 = (bf16[128,512]{1,0:T(8,128)(2,1)S(1)}, bf16[128,512]{1,0:T(8,128)(2,1)S(1)}, u32[]{:S(2)}, u32[]{:S(2)}) collective-permute-start(bf16[128,512]{1,0:T(8,128)(2,1)S(1)} %get-tuple-element.43), channel_id=1, source_target_pairs={{0,3},{1,2},{2,1},{3,0},{4,7},{5,6},{6,5},{7,4},{8,11},{9,10},{10,... | collective-permute-start | bytes 393224 | tf_op jit(solution)/shard_map/ppermute | solution.py:47
  7.7 17.3 %all-to-all-start = ((bf16[64,16,128]{2,1,0:T(8,128)(2,1)}), bf16[64,16,128]{2,1,0:T(8,128)(2,1)S(1)}, u32[]{:S(2)}, u32[]{:S(2)}) async-start(bf16[64,16,128]{2,1,0:T(8,128)(2,1)} %get-tuple-element.46), calls=%async_computation | async-start | bytes 524288 | tf_op jit(solution)/shard_map/all_to_all | solution.py:52
  15.2 16.3 %collective-permute-start.5 = (bf16[64,256]{1,0:T(8,128)(2,1)S(1)}, bf16[64,256]{1,0:T(8,128)(2,1)S(1)}, u32[]{:S(2)}, u32[]{:S(2)}) collective-permute-start(bf16[64,256]{1,0:T(8,128)(2,1)S(1)} %get-tuple-element.48), channel_id=1, source_target_pairs={{0,8},{1,9},{2,10},{3,11},{4,12},{5,13},{6,14},{7,15},{8,0},{9,1},... | collective-permute-start | bytes 98312 | tf_op jit(solution)/shard_map/ppermute | solution.py:47
  21.3 11.4 %collective-permute-start.4 = (bf16[64,256]{1,0:T(8,128)(2,1)S(1)}, bf16[64,256]{1,0:T(8,128)(2,1)S(1)}, u32[]{:S(2)}, u32[]{:S(2)}) collective-permute-start(bf16[64,256]{1,0:T(8,128)(2,1)S(1)} %get-tuple-element.48), channel_id=1, source_target_pairs={{0,12},{1,13},{2,14},{3,15},{4,8},{5,9},{6,10},{7,11},{8,4},{9,5},... | collective-permute-start | bytes 98312 | tf_op jit(solution)/shard_map/ppermute | solution.py:47
  21.6 11.1 %collective-permute-start.3 = (bf16[128,256]{1,0:T(8,128)(2,1)S(1)}, bf16[128,256]{1,0:T(8,128)(2,1)S(1)}, u32[]{:S(2)}, u32[]{:S(2)}) collective-permute-start(bf16[128,256]{1,0:T(8,128)(2,1)S(1)} %get-tuple-element.47), channel_id=1, source_target_pairs={{0,4},{1,5},{2,6},{3,7},{4,0},{5,1},{6,2},{7,3},{8,12},{9,13},{10,... | collective-permute-start | bytes 196616 | tf_op jit(solution)/shard_map/ppermute | solution.py:47
  25.0 9.0 %collective-permute-start.8 = (bf16[128,256]{1,0:T(8,128)(2,1)S(1)}, bf16[128,256]{1,0:T(8,128)(2,1)S(1)}, u32[]{:S(2)}, u32[]{:S(2)}) collective-permute-start(bf16[128,256]{1,0:T(8,128)(2,1)S(1)} %collect.1.refs_2_), channel_id=1, source_target_pairs={{0,8},{1,9},{2,10},{3,11},{4,12},{5,13},{6,14},{7,15},{8,0},{9,1},... | collective-permute-start | bytes 196616 | tf_op jit(solution)/shard_map/ppermute | solution.py:47
  31.5 5.6 %collective-permute-start.7 = (bf16[128,256]{1,0:T(8,128)(2,1)S(1)}, bf16[128,256]{1,0:T(8,128)(2,1)S(1)}, u32[]{:S(2)}, u32[]{:S(2)}) collective-permute-start(bf16[128,256]{1,0:T(8,128)(2,1)S(1)} %collect.1.refs_2_), channel_id=1, source_target_pairs={{0,12},{1,13},{2,14},{3,15},{4,8},{5,9},{6,10},{7,11},{8,4},{9,5},... | collective-permute-start | bytes 196616 | tf_op jit(solution)/shard_map/ppermute | solution.py:47
  31.5 6.3 %collective-permute-start.6 = (bf16[128,256]{1,0:T(8,128)(2,1)S(1)}, bf16[128,256]{1,0:T(8,128)(2,1)S(1)}, u32[]{:S(2)}, u32[]{:S(2)}) collective-permute-start(bf16[128,256]{1,0:T(8,128)(2,1)S(1)} %collect.1.refs_2_), channel_id=1, source_target_pairs={{0,4},{1,5},{2,6},{3,7},{4,0},{5,1},{6,2},{7,3},{8,12},{9,13},{10,... | collective-permute-start | bytes 196616 | tf_op jit(solution)/shard_map/ppermute | solution.py:47
  39.7 7.6 %collective-permute-start.10 = (bf16[192,256]{1,0:T(8,128)(2,1)S(1)}, bf16[192,256]{1,0:T(8,128)(2,1)S(1)}, u32[]{:S(2)}, u32[]{:S(2)}) collective-permute-start(bf16[192,256]{1,0:T(8,128)(2,1)S(1)} %get-tuple-element.65), channel_id=1, source_target_pairs={{0,8},{1,9},{2,10},{3,11},{4,12},{5,13},{6,14},{7,15},{8,0},{9,1},... | collective-permute-start | bytes 294920 | tf_op jit(solution)/shard_map/ppermute | solution.py:47
  44.3 10.1 %collective-permute-start.11 = (bf16[192,256]{1,0:T(8,128)(2,1)S(1)}, bf16[192,256]{1,0:T(8,128)(2,1)S(1)}, u32[]{:S(2)}, u32[]{:S(2)}) collective-permute-start(bf16[192,256]{1,0:T(8,128)(2,1)S(1)} %get-tuple-element.66), channel_id=1, source_target_pairs={{0,12},{1,13},{2,14},{3,15},{4,8},{5,9},{6,10},{7,11},{8,4},{9,5},... | collective-permute-start | bytes 294920 | tf_op jit(solution)/shard_map/ppermute | solution.py:47
  45.7 9.6 %collective-permute-start.9 = (bf16[256,256]{1,0:T(8,128)(2,1)S(1)}, bf16[256,256]{1,0:T(8,128)(2,1)S(1)}, u32[]{:S(2)}, u32[]{:S(2)}) collective-permute-start(bf16[256,256]{1,0:T(8,128)(2,1)S(1)} %get-tuple-element.64), channel_id=1, source_target_pairs={{0,4},{1,5},{2,6},{3,7},{4,0},{5,1},{6,2},{7,3},{8,12},{9,13},{10,... | collective-permute-start | bytes 393224 | tf_op jit(solution)/shard_map/ppermute | solution.py:47
  56.1 7.1 %collective-permute-start.12 = (bf16[128,512]{1,0:T(8,128)(2,1)S(1)}, bf16[128,512]{1,0:T(8,128)(2,1)S(1)}, u32[]{:S(2)}, u32[]{:S(2)}) collective-permute-start(bf16[128,512]{1,0:T(8,128)(2,1)S(1)} %get-tuple-element.70), channel_id=1, source_target_pairs={{0,1},{1,0},{2,3},{3,2},{4,5},{5,4},{6,7},{7,6},{8,9},{9,8},{10,11... | collective-permute-start | bytes 393224 | tf_op jit(solution)/shard_map/ppermute | solution.py:47
  56.6 6.6 %collective-permute-start.13 = (bf16[128,512]{1,0:T(8,128)(2,1)S(1)}, bf16[128,512]{1,0:T(8,128)(2,1)S(1)}, u32[]{:S(2)}, u32[]{:S(2)}) collective-permute-start(bf16[128,512]{1,0:T(8,128)(2,1)S(1)} %get-tuple-element.71), channel_id=1, source_target_pairs={{0,2},{1,3},{2,0},{3,1},{4,6},{5,7},{6,4},{7,5},{8,10},{9,11},{10,... | collective-permute-start | bytes 393224 | tf_op jit(solution)/shard_map/ppermute | solution.py:47
  57.3 7.4 %collective-permute-start.14 = (bf16[128,512]{1,0:T(8,128)(2,1)S(1)}, bf16[128,512]{1,0:T(8,128)(2,1)S(1)}, u32[]{:S(2)}, u32[]{:S(2)}) collective-permute-start(bf16[128,512]{1,0:T(8,128)(2,1)S(1)} %get-tuple-element.72), channel_id=1, source_target_pairs={{0,3},{1,2},{2,1},{3,0},{4,7},{5,6},{6,5},{7,4},{8,11},{9,10},{10,... | collective-permute-start | bytes 393224 | tf_op jit(solution)/shard_map/ppermute | solution.py:47
  58.3 14.9 %all-to-all-start.1 = ((bf16[64,16,128]{2,1,0:T(8,128)(2,1)}), bf16[64,16,128]{2,1,0:T(8,128)(2,1)S(1)}, u32[]{:S(2)}, u32[]{:S(2)}) async-start(bf16[64,16,128]{2,1,0:T(8,128)(2,1)} %get-tuple-element.75), calls=%async_computation.1 | async-start | bytes 524288 | tf_op jit(solution)/shard_map/all_to_all | solution.py:52

commit v3 on v2

--- a/solution.py
+++ b/solution.py
@@ -23,7 +23,7 @@
 ANYWHERE = pl.BlockSpec(memory_space=pl.ANY)
 
 
-def call(body, name, outs, scratch=(), flops=0, spec=VMEM, limit=24, after=()):
+def call(body, name, outs, scratch=(), flops=0, spec=VMEM, limit=24, after=(), sent_first=False):
     def run(*operands):
         count = len(operands)
         operands = (*operands, *after)
@@ -33,7 +33,7 @@
             (lambda *refs: body(*refs[:count], *refs[count + len(after) :])),
             out_shape=shapes,
             in_specs=[spec] * count + [ANYWHERE] * len(after),
-            out_specs=[VMEM] * len(shapes),
+            out_specs=[HBM if sent_first and i == 0 else VMEM for i in range(len(shapes))],
             scratch_shapes=list(scratch),
             name=name,
             cost_estimate=pl.CostEstimate(flops=flops, bytes_accessed=moved, transcendentals=0),
@@ -94,7 +94,7 @@
 
 
 def pool_kernel(
-    q_hbm, kv_hbm, cot_hbm, slots_ref, own_ref, out1_ref, out2_ref, out3_ref, q_ref, kv_ref, cot_ref, rows_ref, sems
+    q_hbm, kv_hbm, cot_hbm, slots_hbm, own_ref, out1_ref, out2_ref, out3_ref, q_ref, kv_ref, cot_ref, rows_ref, slots_ref, sems
 ):
     pairs = ((kv_hbm, kv_ref), (q_hbm, q_ref), (cot_hbm, cot_ref))
     copies = [pltpu.make_async_copy(a, b, sems.at[i]) for i, (a, b) in enumerate(pairs)]
@@ -125,6 +125,8 @@
         slots_ref[outer * TEAM + m] = jnp.zeros_like(blocks[0])
         for k in range(1, 16):
             slots_ref[(outer ^ k) * TEAM + m] = blocks[class_of(k)]
+    sent = pltpu.make_async_copy(slots_ref, slots_hbm, sems.at[3])
+    sent.start()
     copies[1].wait()
     copies[2].wait()
     for k, ref in enumerate((own_ref, out1_ref, out2_ref, out3_ref)):
@@ -133,6 +135,7 @@
         ref[:, 128:256] = kv_ref[:, columns(0, group)]
         ref[:, 256:384] = kv_ref[:, columns(D, group)]
         ref[:, 384:512] = cot_ref[:, columns(0, group)]
+    sent.wait()
 
 
 def class_sums(slots_ref):
@@ -281,7 +284,7 @@
 
 def scatter_kernel(
     block_ref, back2_ref, back4_ref, back6_ref, one_ref, zero_ref, results_ref,
-    slots_ref, own_ref, out1_ref, out2_ref, out3_ref, rows_ref,
+    slots_hbm, own_ref, near_ref, far_ref, rows_ref, slots_ref, sem,
 ):
     outer = lax.axis_index("outer")
     total = add(block_ref[...], back2_ref[0:128, :], back4_ref[0:128, :], back6_ref[0:128, :]).astype(BF16)
@@ -292,6 +295,8 @@
             block = jnp.concatenate([rows[:, :COLS], rows[:, COLS:]], axis=0)
             for k in range(1 << c, 2 << c):
                 slots_ref[(outer ^ k) * TEAM + m] = block
+    sent = pltpu.make_async_copy(slots_ref, slots_hbm, sem)
+    sent.start()
     total = add(back4_ref[128:192, :], back6_ref[128:192, :])
     count = 64
     for level in (back2_ref[128:256, :], one_ref[...], zero_ref[...]):
@@ -300,23 +305,34 @@
         count *= 2
         total = level.astype(F32) + HALF_ROOT * read_rows(rows_ref, count)
     own_ref[...] = total[0:LEAF]
-    for k, ref in enumerate((out1_ref, out2_ref, out3_ref)):
+    for k, ref in enumerate((near_ref, far_ref.at[0:LEAF, :], far_ref.at[LEAF : 2 * LEAF, :])):
         rows = slice(LEAF * (k + 1), LEAF * (k + 2))
         ref[:, 0:256] = total[rows].astype(BF16)
         ref[:, 256:512] = results_ref[rows, :]
-
-
-def merge_kernel(results_ref, own_ref, got1_ref, got2_ref, got3_ref, att_ref, dq_ref, sum_ref):
-    for k, ref in enumerate((own_ref, got1_ref, got2_ref, got3_ref)):
-        group = member() ^ k
-        sum_ref[:, columns(0, group)] = ref[:, 0:128].astype(F32)
-        sum_ref[:, columns(D, group)] = ref[:, 128:256].astype(F32)
-        part = results_ref[0:LEAF, :] if k == 0 else ref[:, 256:512]
-        att_ref[:, columns(0, group)] = part[:, :COLS]
-        dq_ref[:, columns(0, group)] = part[:, COLS:]
-
-
-def finish_kernel(slots_ref, sum_ref, out_ref):
+    sent.wait()
+
+
+def merge_kernel(own_ref, near_ref, far_ref, sum_ref):
+    for k, ref in enumerate((own_ref, near_ref, far_ref)):
+        sum_ref[:, columns(0, member() ^ k)] = ref[0:LEAF, 0:128].astype(F32)
+        sum_ref[:, columns(D, member() ^ k)] = ref[0:LEAF, 128:256].astype(F32)
+
+
+def relay_kernel(far_ref, out_ref):
+    out_ref[...] = far_ref[LEAF : 2 * LEAF, :]
+
+
+def outputs_kernel(results_ref, near_ref, far_ref, last_ref, att_ref, dq_ref):
+    parts = [results_ref[0:LEAF, :]] + [ref[0:LEAF, 256:512] for ref in (near_ref, far_ref, last_ref)]
+    for k, part in enumerate(parts):
+        att_ref[:, columns(0, member() ^ k)] = part[:, :COLS]
+        dq_ref[:, columns(0, member() ^ k)] = part[:, COLS:]
+
+
+def finish_kernel(slots_ref, sum_in_ref, last_ref, out_ref, sum_ref):
+    sum_ref[...] = sum_in_ref[...]
+    sum_ref[:, columns(0, member() ^ 3)] = last_ref[:, 0:128].astype(F32)
+    sum_ref[:, columns(D, member() ^ 3)] = last_ref[:, 128:256].astype(F32)
     outer = lax.axis_index("outer")
     row = row_index()
     four, five, six, seven = [
@@ -334,6 +350,7 @@
 
 def shards(queries, keys_values, cotangent):
     queries, keys_values, cotangent = queries[0], keys_values[0], cotangent[0]
+    whole = ((LEAF, D), BF16)
     slots = ((16 * TEAM, 16, COLS), BF16)
     piece = ((LEAF, D), BF16)
     loaded = [pltpu.VMEM((LEAF, D), BF16), pltpu.VMEM((LEAF, 2 * D), BF16), pltpu.VMEM((LEAF, D), BF16)]
@@ -341,7 +358,7 @@
     team_rows = pltpu.VMEM((2, TEAM * LEAF, 128), F32)
 
     sent, own, out1, out2, out3 = call(
-        pool_kernel, "pool", [slots, piece, piece, piece, piece], [*loaded, own_rows, pltpu.SemaphoreType.DMA((3,))], spec=HBM, limit=53.375
+        pool_kernel, "pool", [slots, piece, piece, piece, piece], [*loaded, own_rows, pltpu.VMEM(*slots), pltpu.SemaphoreType.DMA((4,))], spec=HBM, limit=53.375, sent_first=True
     )(queries, keys_values, cotangent)
     taken = trade_slots(sent)
     got2 = exchange(out2, 2)
@@ -390,17 +407,21 @@
     )(keys, later_keys, q2, cot2, exps, dweights, factor, centre, rounded, dscores)
 
     (back4,) = call(hold_kernel, "hold", [((192, 256), BF16)], flops=LONG)(back4)
-    sent, own, out1, out2, out3 = call(
-        scatter_kernel, "scatter", [slots, ((LEAF, 256), F32), piece, piece, piece], [team_rows]
+    sent, own, near, far = call(
+        scatter_kernel,
+        "scatter",
+        [slots, ((LEAF, 256), F32), whole, ((2 * LEAF, D), BF16)],
+        [team_rows, pltpu.VMEM(*slots), pltpu.SemaphoreType.DMA],
+        sent_first=True,
     )(block, back2, back4, back6, one, zero, results)
     taken = trade_slots(sent)
-    got2 = exchange(out2, 2)
-    got3 = exchange(out3, 3)
-    got1 = exchange(out1, 1)
-    attended, query_grad, total = call(
-        merge_kernel, "merge", [((LEAF, D), BF16), ((LEAF, D), BF16), ((LEAF, 2 * D), F32)], flops=LONG
-    )(results, own, got1, got2, got3)
-    (kv_grad,) = call(finish_kernel, "finish", [((LEAF, 2 * D), BF16)])(taken, total)
+    far = exchange(far, 2)
+    near = exchange(near, 1)
+    (total,) = call(merge_kernel, "merge", [((LEAF, 2 * D), F32)], flops=LONG)(own, near, far)
+    (relayed,) = call(relay_kernel, "relay", [whole], after=(total,))(far)
+    last = exchange(relayed, 1)
+    attended, query_grad = call(outputs_kernel, "outputs", [whole, whole])(results, near, far, last)
+    (kv_grad,) = call(finish_kernel, "finish", [((LEAF, 2 * D), BF16)], [pltpu.VMEM((LEAF, 2 * D), F32)])(taken, total, last)
     return attended[None], query_grad[None], kv_grad[None]
 
 

time: 74.2 us -> 74 us (level)
  waiting for transfers between devices: 23.6 us -> 22.1 us
  starting transfers between devices: 40.3 us -> 41.5 us
    all_to_all x2, waiting for transfers between devices: 10.2 us -> 8.67 us  [trade_slots(): lax.all_to_all(slots, ('outer', 'inner'), 0, 0, axis_index_groups=groups,...]
    ppermute x15, starting transfers between devices: 28.1 us -> 28.8 us  [exchange(): return lax.ppermute(array, 'inner', [(i, i ^ bits) for i in range(16)])]
    pallas_call x11 -> x13, Pallas kernels: 9.42 us -> 9.33 us  [run(): pl.pallas_call(lambda *refs: body(*refs[:count], *refs[count + len(after)...]
  transfers between devices with their start and end apart: 17 -> 17, of which waited for: 8 -> 9; matrix products, arithmetic and copies ran while one was open for 0% -> 0% of each run, Pallas kernels for 5% -> 5%
where the time goes in v3:
time: 74 us; the launch traced here: 73.8 us
  starting transfers between devices  41.5 us (56%)
  waiting for transfers between devices  22.1 us (30%)
  Pallas kernels  9.33 us (13%)
  between operations  0.77 us (1%)
    ppermute x15, starting transfers between devices, exchange(): return lax.ppermute(array, 'inner', [(i, i ^ bits) for i in range(16)])  28.8 us
    ppermute x15, waiting for transfers between devices, exchange(): return lax.ppermute(array, 'inner', [(i, i ^ bits) for i in range(16)])  13.5 us
    all_to_all x2, starting transfers between devices, trade_slots(): lax.all_to_all(slots, ('outer', 'inner'), 0, 0, axis_index_groups=groups,...  12.7 us
    pallas_call x13, Pallas kernels, run(): pl.pallas_call(lambda *refs: body(*refs[:count], *refs[count + len(after)...  9.33 us
    all_to_all x2, waiting for transfers between devices, trade_slots(): lax.all_to_all(slots, ('outer', 'inner'), 0, 0, axis_index_groups=groups,...  8.67 us
  transfers between devices with their start and end apart: 17, of which 9 were waited for; matrix products, arithmetic and copies ran while one was open for 0% of the time, Pallas kernels for 5%

profile of v3, /device:TPU:1, one launch (start us, length us, event | category | flops | bytes accessed | tf_op | source)
XLA Modules:
  0.0 73.8 jit_solution(15183762588991909029)
XLA Ops:
  0.6 1.9 %pool.1 = (bf16[64,16,128]{2,1,0:T(8,128)(2,1)}, bf16[128,512]{1,0:T(8,128)(2,1)S(1)}, bf16[128,512]{1,0:T(8,128)(2,1)S(1)}, bf16[128,512]{1,0:T(8,128)(2,1)S(1)}, bf16[128,512]{1,0:T(8,128)(2,1)S(1)}) custom-call(bf16[128,512]{1,0:T(8,128)(2,1)} %bitcast.8, bf16[128,1024]{1,0:T(8,128)(2,1)} %bitcast.6, bf16[128,512]{1,0:T(8,128)(2,1)} %bitcast.9), custom_call_target="tpu_custom_call" | custom-call | bytes 1310720 | tf_op jit(solution)/shard_map/pool/pallas_call | solution.py:32
  2.6 3.3 %collective-permute-start = (bf16[128,512]{1,0:T(8,128)(2,1)S(1)}, bf16[128,512]{1,0:T(8,128)(2,1)S(1)}, u32[]{:S(2)}, u32[]{:S(2)}) collective-permute-start(bf16[128,512]{1,0:T(8,128)(2,1)S(1)} %get-tuple-element.39), channel_id=1, source_target_pairs={{0,1},{1,0},{2,3},{3,2},{4,5},{5,4},{6,7},{7,6},{8,9},{9,8},{10,11... | collective-permute-start | bytes 393224 | tf_op jit(solution)/shard_map/ppermute | solution.py:47
  5.9 0.0 collective-permute-start.1
  5.9 1.7 %collective-permute-start.2 = (bf16[128,512]{1,0:T(8,128)(2,1)S(1)}, bf16[128,512]{1,0:T(8,128)(2,1)S(1)}, u32[]{:S(2)}, u32[]{:S(2)}) collective-permute-start(bf16[128,512]{1,0:T(8,128)(2,1)S(1)} %get-tuple-element.41), channel_id=1, source_target_pairs={{0,3},{1,2},{2,1},{3,0},{4,7},{5,6},{6,5},{7,4},{8,11},{9,10},{10,... | collective-permute-start | bytes 393224 | tf_op jit(solution)/shard_map/ppermute | solution.py:47
  7.6 7.3 %all-to-all-start = ((bf16[64,16,128]{2,1,0:T(8,128)(2,1)}), bf16[64,16,128]{2,1,0:T(8,128)(2,1)S(1)}, u32[]{:S(2)}, u32[]{:S(2)}) async-start(bf16[64,16,128]{2,1,0:T(8,128)(2,1)} %get-tuple-element.44), calls=%async_computation | async-start | bytes 524288 | tf_op jit(solution)/shard_map/all_to_all | solution.py:52
  14.9 0.0 collective-permute-done.refs_1_
  14.9 0.0 collective-permute-done.1.refs_2_
  14.9 0.0 collective-permute-done.2.refs_3_
  14.9 0.2 team.1
  15.1 6.1 %collective-permute-start.5 = (bf16[64,256]{1,0:T(8,128)(2,1)S(1)}, bf16[64,256]{1,0:T(8,128)(2,1)S(1)}, u32[]{:S(2)}, u32[]{:S(2)}) collective-permute-start(bf16[64,256]{1,0:T(8,128)(2,1)S(1)} %get-tuple-element.46), channel_id=1, source_target_pairs={{0,8},{1,9},{2,10},{3,11},{4,12},{5,13},{6,14},{7,15},{8,0},{9,1},... | collective-permute-start | bytes 98312 | tf_op jit(solution)/shard_map/ppermute | solution.py:47
  21.2 0.3 collective-permute-start.4
  21.5 0.9 %collective-permute-start.3 = (bf16[128,256]{1,0:T(8,128)(2,1)S(1)}, bf16[128,256]{1,0:T(8,128)(2,1)S(1)}, u32[]{:S(2)}, u32[]{:S(2)}) collective-permute-start(bf16[128,256]{1,0:T(8,128)(2,1)S(1)} %get-tuple-element.45), channel_id=1, source_target_pairs={{0,4},{1,5},{2,6},{3,7},{4,0},{5,1},{6,2},{7,3},{8,12},{9,13},{10,... | collective-permute-start | bytes 196616 | tf_op jit(solution)/shard_map/ppermute | solution.py:47
  22.4 2.5 %all-to-all-done.refs_0_ = bf16[64,16,128]{2,1,0:T(8,128)(2,1)S(1)} async-done(((bf16[64,16,128]{2,1,0:T(8,128)(2,1)}), bf16[64,16,128]{2,1,0:T(8,128)(2,1)S(1)}, u32[]{:S(2)}, u32[]{:S(2)}) %all-to-all-start) | async-done | bytes 262176 | tf_op jit(solution)/shard_map/all_to_all | solution.py:52
  24.9 6.4 %collective-permute-start.8 = (bf16[128,256]{1,0:T(8,128)(2,1)S(1)}, bf16[128,256]{1,0:T(8,128)(2,1)S(1)}, u32[]{:S(2)}, u32[]{:S(2)}) collective-permute-start(bf16[128,256]{1,0:T(8,128)(2,1)S(1)} %collect.1.refs_2_), channel_id=1, source_target_pairs={{0,8},{1,9},{2,10},{3,11},{4,12},{5,13},{6,14},{7,15},{8,0},{9,1},... | collective-permute-start | bytes 196616 | tf_op jit(solution)/shard_map/ppermute | solution.py:47
  31.4 0.0 collective-permute-start.7
  31.4 0.0 collective-permute-done.5.refs_2_
  31.4 1.2 %collective-permute-start.6 = (bf16[128,256]{1,0:T(8,128)(2,1)S(1)}, bf16[128,256]{1,0:T(8,128)(2,1)S(1)}, u32[]{:S(2)}, u32[]{:S(2)}) collective-permute-start(bf16[128,256]{1,0:T(8,128)(2,1)S(1)} %collect.1.refs_2_), channel_id=1, source_target_pairs={{0,4},{1,5},{2,6},{3,7},{4,0},{5,1},{6,2},{7,3},{8,12},{9,13},{10,... | collective-permute-start | bytes 196616 | tf_op jit(solution)/shard_map/ppermute | solution.py:47
  32.6 0.0 collective-permute-done.4.refs_1_
  32.6 0.0 collective-permute-done.3.refs_0_
  32.6 1.3 %first.1 = (bf16[2,768,256]{2,1,0:T(8,128)(2,1)S(1)}, bf16[2,512,128]{2,1,0:T(8,128)(2,1)S(1)}, bf16[2,512,128]{2,1,0:T(8,128)(2,1)S(1)}, f32[2,768,512]{2,1,0:T...) custom-call(bf16[512,512]{1,0:T(8,128)(2,1)S(1)} %get-tuple-element., ...), custom_call_target="tpu_custom_call" | custom-call | flops 402653184 | bytes 8466432 | tf_op jit(solution)/shard_map/first/pallas_call | solution.py:32
  33.9 0.0 collective-permute-done.8.refs_2_
  33.9 3.1 %collective-permute-done.7.refs_1_ = bf16[128,256]{1,0:T(8,128)(2,1)S(1)} collective-permute-done((bf16[128,256]{1,0:T(8,128)(2,1)S(1)}, bf16[128,256]{1,0:T(8,128)(2,1)S(1)}, u32[]{:S(2)}, u32[]{:S(2)}) %collective-permute-start.7) | collective-permute-done | bytes 65568 | tf_op jit(solution)/shard_map/ppermute | solution.py:47
  37.0 0.7 collective-permute-done.6.refs_0_
  37.6 2.0 %second.1 = (bf16[256,256]{1,0:T(8,128)(2,1)S(1)}, bf16[192,256]{1,0:T(8,128)(2,1)S(1)}, bf16[192,256]{1,0:T(8,128)(2,1)S(1)}, bf16[640,256]{1,0:T(8,128)(2,1)S(...) custom-call(bf16[128,256]{1,0:T(8,128)(2,1)S(1)} %collective-permute, ...), custom_call_target="tpu_custom_call" | custom-call | flops 671088640 | bytes 10440704 | tf_op jit(solution)/shard_map/second/pallas_call | solution.py:32
  39.6 4.6 %collective-permute-start.10 = (bf16[192,256]{1,0:T(8,128)(2,1)S(1)}, bf16[192,256]{1,0:T(8,128)(2,1)S(1)}, u32[]{:S(2)}, u32[]{:S(2)}) collective-permute-start(bf16[192,256]{1,0:T(8,128)(2,1)S(1)} %get-tuple-element.63), channel_id=1, source_target_pairs={{0,8},{1,9},{2,10},{3,11},{4,12},{5,13},{6,14},{7,15},{8,0},{9,1},... | collective-permute-start | bytes 294920 | tf_op jit(solution)/shard_map/ppermute | solution.py:47
  44.2 1.4 %collective-permute-start.11 = (bf16[192,256]{1,0:T(8,128)(2,1)S(1)}, bf16[192,256]{1,0:T(8,128)(2,1)S(1)}, u32[]{:S(2)}, u32[]{:S(2)}) collective-permute-start(bf16[192,256]{1,0:T(8,128)(2,1)S(1)} %get-tuple-element.64), channel_id=1, source_target_pairs={{0,12},{1,13},{2,14},{3,15},{4,8},{5,9},{6,10},{7,11},{8,4},{9,5},... | collective-permute-start | bytes 294920 | tf_op jit(solution)/shard_map/ppermute | solution.py:47
  45.6 0.0 collective-permute-start.9
  45.6 1.5 %rest.1 = (f32[128,256]{1,0:T(8,128)S(1)}, f32[256,256]{1,0:T(8,128)S(1)}, f32[512,256]{1,0:T(8,128)S(1)}, bf16[512,256]{1,0:T(8,128)(2,1)S(1)}) custom-call(bf16[2,768,256]{2,1,0:T(8,128)(2,1)S(1)} %get-tuple-element.47.refs_0_, bf16[640,256]{1,0:T(8,128)(2,1)S(1)} %get-tuple-element.55.refs_1_, bf16[2,512,128]{2,1,0:T(8,128)(2,1)S(1)} %get-tuple-element.48.refs_4_.refs_2_, ...), custom_call_target="tpu_custom_call" | custom-call | flops 1207959552 | bytes 11739136 | tf_op jit(solution)/shard_map/rest/pallas_call | solution.py:32
  47.0 0.2 collective-permute-done.10.refs_0_
  47.2 7.1 %collective-permute-done.11.refs_3_ = bf16[192,256]{1,0:T(8,128)(2,1)S(1)} collective-permute-done((bf16[192,256]{1,0:T(8,128)(2,1)S(1)}, bf16[192,256]{1,0:T(8,128)(2,1)S(1)}, u32[]{:S(2)}, u32[]{:S(2)}) %collective-permute-start.11) | collective-permute-done | bytes 98336 | tf_op jit(solution)/shard_map/ppermute | solution.py:47
  54.3 0.9 %collective-permute-done.9.refs_1_ = bf16[256,256]{1,0:T(8,128)(2,1)S(1)} collective-permute-done((bf16[256,256]{1,0:T(8,128)(2,1)S(1)}, bf16[256,256]{1,0:T(8,128)(2,1)S(1)}, u32[]{:S(2)}, u32[]{:S(2)}) %collective-permute-start.9) | collective-permute-done | bytes 131104 | tf_op jit(solution)/shard_map/ppermute | solution.py:47
  55.2 0.8 %scatter.1 = (bf16[64,16,128]{2,1,0:T(8,128)(2,1)}, f32[128,256]{1,0:T(8,128)S(1)}, bf16[128,512]{1,0:T(8,128)(2,1)S(1)}, bf16[256,512]{1,0:T(8,128)(2,1)S(1)}) custom-call(f32[128,256]{1,0:T(8,128)S(1)} %get-tuple-element.61.refs_0_, bf16[256,256]{1,0:T(8,128)(2,1)S(1)} %collective-permute-done.9.refs_1_, bf16[192,256]{1,0:T(8,128)(2,1)S(1)} %hold.1.refs_2_, ...), custom_call_target="tpu_custom_call" | custom-call | bytes 2293760 | tf_op jit(solution)/shard_map/scatter/pallas_call | solution.py:32
  56.0 0.1 collective-permute-start.13
  56.1 1.4 %collective-permute-start.12 = (bf16[128,512]{1,0:T(8,128)(2,1)S(1)}, bf16[128,512]{1,0:T(8,128)(2,1)S(1)}, u32[]{:S(2)}, u32[]{:S(2)}) collective-permute-start(bf16[128,512]{1,0:T(8,128)(2,1)S(1)} %get-tuple-element.67), channel_id=1, source_target_pairs={{0,1},{1,0},{2,3},{3,2},{4,5},{5,4},{6,7},{7,6},{8,9},{9,8},{10,11... | collective-permute-start | bytes 393224 | tf_op jit(solution)/shard_map/ppermute | solution.py:47
  57.5 5.4 %all-to-all-start.1 = ((bf16[64,16,128]{2,1,0:T(8,128)(2,1)}), bf16[64,16,128]{2,1,0:T(8,128)(2,1)S(1)}, u32[]{:S(2)}, u32[]{:S(2)}) async-start(bf16[64,16,128]{2,1,0:T(8,128)(2,1)} %get-tuple-element.72), calls=%async_computation.1 | async-start | bytes 524288 | tf_op jit(solution)/shard_map/all_to_all | solution.py:52
  62.9 0.0 collective-permute-done.12.refs_1_
  62.9 0.6 collective-permute-done.13.refs_2_.refs_0_
  63.6 1.4 %collective-permute-start.14 = (bf16[128,512]{1,0:T(8,128)(2,1)S(1)}, bf16[128,512]{1,0:T(8,128)(2,1)S(1)}, u32[]{:S(2)}, u32[]{:S(2)}) collective-permute-start(bf16[128,512]{1,0:T(8,128)(2,1)S(1)} %relay.1), channel_id=1, source_target_pairs={{0,1},{1,0},{2,3},{3,2},{4,5},{5,4},{6,7},{7,6},{8,9},{9,8},{10,11... | collective-permute-start | bytes 393224 | tf_op jit(solution)/shard_map/ppermute | solution.py:47
  65.0 1.0 %collective-permute-done.14.refs_3_.refs_2_ = bf16[128,512]{1,0:T(8,128)(2,1)S(1)} collective-permute-done((bf16[128,512]{1,0:T(8,128)(2,1)S(1)}, bf16[128,512]{1,0:T(8,128)(2,1)S(1)}, u32[]{:S(2)}, u32[]{:S(2)}) %collective-permute-start.14) | collective-permute-done | bytes 131104 | tf_op jit(solution)/shard_map/ppermute | solution.py:47
  66.0 0.7 outputs.1
  66.7 6.2 %all-to-all-done.1.refs_0_ = bf16[64,16,128]{2,1,0:T(8,128)(2,1)S(1)} async-done(((bf16[64,16,128]{2,1,0:T(8,128)(2,1)}), bf16[64,16,128]{2,1,0:T(8,128)(2,1)S(1)}, u32[]{:S(2)}, u32[]{:S(2)}) %all-to-all-start.1) | async-done | bytes 262176 | tf_op jit(solution)/shard_map/all_to_all | solution.py:52
  72.9 0.8 %finish.1 = bf16[128,1024]{1,0:T(8,128)(2,1)} custom-call(bf16[64,16,128]{2,1,0:T(8,128)(2,1)S(1)} %all-to-all-done.1.refs_0_, f32[128,1024]{1,0:T(8,128)S(1)} %merge.1.refs_1_, bf16[128,512]{1,0:T(8,128)(2,1)S(1)} %collective-permute-done.14.refs_3_.refs_2_), custom_call_target="tpu_custom_call" | custom-call | bytes 1179648 | tf_op jit(solution)/shard_map/finish/pallas_call | solution.py:32
  (5 shorter events, 0.1 us)
Async XLA Ops:
  2.6 12.3 %collective-permute-start = (bf16[128,512]{1,0:T(8,128)(2,1)S(1)}, bf16[128,512]{1,0:T(8,128)(2,1)S(1)}, u32[]{:S(2)}, u32[]{:S(2)}) collective-permute-start(bf16[128,512]{1,0:T(8,128)(2,1)S(1)} %get-tuple-element.39), channel_id=1, source_target_pairs={{0,1},{1,0},{2,3},{3,2},{4,5},{5,4},{6,7},{7,6},{8,9},{9,8},{10,11... | collective-permute-start | bytes 393224 | tf_op jit(solution)/shard_map/ppermute | solution.py:47
  5.9 9.0 %collective-permute-start.1 = (bf16[128,512]{1,0:T(8,128)(2,1)S(1)}, bf16[128,512]{1,0:T(8,128)(2,1)S(1)}, u32[]{:S(2)}, u32[]{:S(2)}) collective-permute-start(bf16[128,512]{1,0:T(8,128)(2,1)S(1)} %get-tuple-element.40), channel_id=1, source_target_pairs={{0,2},{1,3},{2,0},{3,1},{4,6},{5,7},{6,4},{7,5},{8,10},{9,11},{10,... | collective-permute-start | bytes 393224 | tf_op jit(solution)/shard_map/ppermute | solution.py:47
  5.9 9.0 %collective-permute-start.2 = (bf16[128,512]{1,0:T(8,128)(2,1)S(1)}, bf16[128,512]{1,0:T(8,128)(2,1)S(1)}, u32[]{:S(2)}, u32[]{:S(2)}) collective-permute-start(bf16[128,512]{1,0:T(8,128)(2,1)S(1)} %get-tuple-element.41), channel_id=1, source_target_pairs={{0,3},{1,2},{2,1},{3,0},{4,7},{5,6},{6,5},{7,4},{8,11},{9,10},{10,... | collective-permute-start | bytes 393224 | tf_op jit(solution)/shard_map/ppermute | solution.py:47
  7.6 17.3 %all-to-all-start = ((bf16[64,16,128]{2,1,0:T(8,128)(2,1)}), bf16[64,16,128]{2,1,0:T(8,128)(2,1)S(1)}, u32[]{:S(2)}, u32[]{:S(2)}) async-start(bf16[64,16,128]{2,1,0:T(8,128)(2,1)} %get-tuple-element.44), calls=%async_computation | async-start | bytes 524288 | tf_op jit(solution)/shard_map/all_to_all | solution.py:52
  15.1 16.3 %collective-permute-start.5 = (bf16[64,256]{1,0:T(8,128)(2,1)S(1)}, bf16[64,256]{1,0:T(8,128)(2,1)S(1)}, u32[]{:S(2)}, u32[]{:S(2)}) collective-permute-start(bf16[64,256]{1,0:T(8,128)(2,1)S(1)} %get-tuple-element.46), channel_id=1, source_target_pairs={{0,8},{1,9},{2,10},{3,11},{4,12},{5,13},{6,14},{7,15},{8,0},{9,1},... | collective-permute-start | bytes 98312 | tf_op jit(solution)/shard_map/ppermute | solution.py:47
  21.2 11.4 %collective-permute-start.4 = (bf16[64,256]{1,0:T(8,128)(2,1)S(1)}, bf16[64,256]{1,0:T(8,128)(2,1)S(1)}, u32[]{:S(2)}, u32[]{:S(2)}) collective-permute-start(bf16[64,256]{1,0:T(8,128)(2,1)S(1)} %get-tuple-element.46), channel_id=1, source_target_pairs={{0,12},{1,13},{2,14},{3,15},{4,8},{5,9},{6,10},{7,11},{8,4},{9,5},... | collective-permute-start | bytes 98312 | tf_op jit(solution)/shard_map/ppermute | solution.py:47
  21.5 11.1 %collective-permute-start.3 = (bf16[128,256]{1,0:T(8,128)(2,1)S(1)}, bf16[128,256]{1,0:T(8,128)(2,1)S(1)}, u32[]{:S(2)}, u32[]{:S(2)}) collective-permute-start(bf16[128,256]{1,0:T(8,128)(2,1)S(1)} %get-tuple-element.45), channel_id=1, source_target_pairs={{0,4},{1,5},{2,6},{3,7},{4,0},{5,1},{6,2},{7,3},{8,12},{9,13},{10,... | collective-permute-start | bytes 196616 | tf_op jit(solution)/shard_map/ppermute | solution.py:47
  24.9 9.0 %collective-permute-start.8 = (bf16[128,256]{1,0:T(8,128)(2,1)S(1)}, bf16[128,256]{1,0:T(8,128)(2,1)S(1)}, u32[]{:S(2)}, u32[]{:S(2)}) collective-permute-start(bf16[128,256]{1,0:T(8,128)(2,1)S(1)} %collect.1.refs_2_), channel_id=1, source_target_pairs={{0,8},{1,9},{2,10},{3,11},{4,12},{5,13},{6,14},{7,15},{8,0},{9,1},... | collective-permute-start | bytes 196616 | tf_op jit(solution)/shard_map/ppermute | solution.py:47
  31.4 5.6 %collective-permute-start.7 = (bf16[128,256]{1,0:T(8,128)(2,1)S(1)}, bf16[128,256]{1,0:T(8,128)(2,1)S(1)}, u32[]{:S(2)}, u32[]{:S(2)}) collective-permute-start(bf16[128,256]{1,0:T(8,128)(2,1)S(1)} %collect.1.refs_2_), channel_id=1, source_target_pairs={{0,12},{1,13},{2,14},{3,15},{4,8},{5,9},{6,10},{7,11},{8,4},{9,5},... | collective-permute-start | bytes 196616 | tf_op jit(solution)/shard_map/ppermute | solution.py:47
  31.4 6.3 %collective-permute-start.6 = (bf16[128,256]{1,0:T(8,128)(2,1)S(1)}, bf16[128,256]{1,0:T(8,128)(2,1)S(1)}, u32[]{:S(2)}, u32[]{:S(2)}) collective-permute-start(bf16[128,256]{1,0:T(8,128)(2,1)S(1)} %collect.1.refs_2_), channel_id=1, source_target_pairs={{0,4},{1,5},{2,6},{3,7},{4,0},{5,1},{6,2},{7,3},{8,12},{9,13},{10,... | collective-permute-start | bytes 196616 | tf_op jit(solution)/shard_map/ppermute | solution.py:47
  39.6 7.6 %collective-permute-start.10 = (bf16[192,256]{1,0:T(8,128)(2,1)S(1)}, bf16[192,256]{1,0:T(8,128)(2,1)S(1)}, u32[]{:S(2)}, u32[]{:S(2)}) collective-permute-start(bf16[192,256]{1,0:T(8,128)(2,1)S(1)} %get-tuple-element.63), channel_id=1, source_target_pairs={{0,8},{1,9},{2,10},{3,11},{4,12},{5,13},{6,14},{7,15},{8,0},{9,1},... | collective-permute-start | bytes 294920 | tf_op jit(solution)/shard_map/ppermute | solution.py:47
  44.2 10.1 %collective-permute-start.11 = (bf16[192,256]{1,0:T(8,128)(2,1)S(1)}, bf16[192,256]{1,0:T(8,128)(2,1)S(1)}, u32[]{:S(2)}, u32[]{:S(2)}) collective-permute-start(bf16[192,256]{1,0:T(8,128)(2,1)S(1)} %get-tuple-element.64), channel_id=1, source_target_pairs={{0,12},{1,13},{2,14},{3,15},{4,8},{5,9},{6,10},{7,11},{8,4},{9,5},... | collective-permute-start | bytes 294920 | tf_op jit(solution)/shard_map/ppermute | solution.py:47
  45.6 9.7 %collective-permute-start.9 = (bf16[256,256]{1,0:T(8,128)(2,1)S(1)}, bf16[256,256]{1,0:T(8,128)(2,1)S(1)}, u32[]{:S(2)}, u32[]{:S(2)}) collective-permute-start(bf16[256,256]{1,0:T(8,128)(2,1)S(1)} %get-tuple-element.62), channel_id=1, source_target_pairs={{0,4},{1,5},{2,6},{3,7},{4,0},{5,1},{6,2},{7,3},{8,12},{9,13},{10,... | collective-permute-start | bytes 393224 | tf_op jit(solution)/shard_map/ppermute | solution.py:47
  56.0 7.5 %collective-permute-start.13 = (bf16[256,512]{1,0:T(8,128)(2,1)S(1)}, bf16[256,512]{1,0:T(8,128)(2,1)S(1)}, u32[]{:S(2)}, u32[]{:S(2)}) collective-permute-start(bf16[256,512]{1,0:T(8,128)(2,1)S(1)} %get-tuple-element.68), channel_id=1, source_target_pairs={{0,2},{1,3},{2,0},{3,1},{4,6},{5,7},{6,4},{7,5},{8,10},{9,11},{10,... | collective-permute-start | bytes 786440 | tf_op jit(solution)/shard_map/ppermute | solution.py:47
  56.1 6.8 %collective-permute-start.12 = (bf16[128,512]{1,0:T(8,128)(2,1)S(1)}, bf16[128,512]{1,0:T(8,128)(2,1)S(1)}, u32[]{:S(2)}, u32[]{:S(2)}) collective-permute-start(bf16[128,512]{1,0:T(8,128)(2,1)S(1)} %get-tuple-element.67), channel_id=1, source_target_pairs={{0,1},{1,0},{2,3},{3,2},{4,5},{5,4},{6,7},{7,6},{8,9},{9,8},{10,11... | collective-permute-start | bytes 393224 | tf_op jit(solution)/shard_map/ppermute | solution.py:47
  57.5 15.4 %all-to-all-start.1 = ((bf16[64,16,128]{2,1,0:T(8,128)(2,1)}), bf16[64,16,128]{2,1,0:T(8,128)(2,1)S(1)}, u32[]{:S(2)}, u32[]{:S(2)}) async-start(bf16[64,16,128]{2,1,0:T(8,128)(2,1)} %get-tuple-element.72), calls=%async_computation.1 | async-start | bytes 524288 | tf_op jit(solution)/shard_map/all_to_all | solution.py:52
  63.6 2.4 %collective-permute-start.14 = (bf16[128,512]{1,0:T(8,128)(2,1)S(1)}, bf16[128,512]{1,0:T(8,128)(2,1)S(1)}, u32[]{:S(2)}, u32[]{:S(2)}) collective-permute-start(bf16[128,512]{1,0:T(8,128)(2,1)S(1)} %relay.1), channel_id=1, source_target_pairs={{0,1},{1,0},{2,3},{3,2},{4,5},{5,4},{6,7},{7,6},{8,9},{9,8},{10,11... | collective-permute-start | bytes 393224 | tf_op jit(solution)/shard_map/ppermute | solution.py:47

commit v4 on v3

--- a/solution.py
+++ b/solution.py
@@ -287,12 +287,12 @@
     slots_hbm, own_ref, near_ref, far_ref, rows_ref, slots_ref, sem,
 ):
     outer = lax.axis_index("outer")
-    total = add(block_ref[...], back2_ref[0:128, :], back4_ref[0:128, :], back6_ref[0:128, :]).astype(BF16)
+    total = add(block_ref[...], back2_ref[0:128, :], back4_ref[0:128, :], back6_ref[0:128, :])
     for m in range(TEAM):
         slots_ref[outer * TEAM + m] = jnp.zeros((16, COLS), BF16)
         for c in range(4):
             rows = total[32 * c + 8 * m : 32 * c + 8 * m + 8]
-            block = jnp.concatenate([rows[:, :COLS], rows[:, COLS:]], axis=0)
+            block = jnp.concatenate([rows[:, :COLS], rows[:, COLS:]], axis=0).astype(BF16)
             for k in range(1 << c, 2 << c):
                 slots_ref[(outer ^ k) * TEAM + m] = block
     sent = pltpu.make_async_copy(slots_ref, slots_hbm, sem)

time: 74 us -> 74 us (level)
  no operation moved by 1% of the time
where the time goes in v4:
time: 74 us; the launch traced here: 73.7 us
  starting transfers between devices  41.5 us (56%)
  waiting for transfers between devices  22.1 us (30%)
  Pallas kernels  9.3 us (13%)
  between operations  0.77 us (1%)
    ppermute x15, starting transfers between devices, exchange(): return lax.ppermute(array, 'inner', [(i, i ^ bits) for i in range(16)])  28.8 us
    ppermute x15, waiting for transfers between devices, exchange(): return lax.ppermute(array, 'inner', [(i, i ^ bits) for i in range(16)])  13.5 us
    all_to_all x2, starting transfers between devices, trade_slots(): lax.all_to_all(slots, ('outer', 'inner'), 0, 0, axis_index_groups=groups,...  12.7 us
    pallas_call x13, Pallas kernels, run(): pl.pallas_call(lambda *refs: body(*refs[:count], *refs[count + len(after)...  9.3 us
    all_to_all x2, waiting for transfers between devices, trade_slots(): lax.all_to_all(slots, ('outer', 'inner'), 0, 0, axis_index_groups=groups,...  8.67 us
  transfers between devices with their start and end apart: 17, of which 9 were waited for; matrix products, arithmetic and copies ran while one was open for 0% of the time, Pallas kernels for 5%

profile of v4, /device:TPU:1, one launch (start us, length us, event | category | flops | bytes accessed | tf_op | source)
XLA Modules:
  0.0 73.7 jit_solution(3672290038170213218)
XLA Ops:
  0.6 1.9 %pool.1 = (bf16[64,16,128]{2,1,0:T(8,128)(2,1)}, bf16[128,512]{1,0:T(8,128)(2,1)S(1)}, bf16[128,512]{1,0:T(8,128)(2,1)S(1)}, bf16[128,512]{1,0:T(8,128)(2,1)S(1)}, bf16[128,512]{1,0:T(8,128)(2,1)S(1)}) custom-call(bf16[128,512]{1,0:T(8,128)(2,1)} %bitcast.8, bf16[128,1024]{1,0:T(8,128)(2,1)} %bitcast.6, bf16[128,512]{1,0:T(8,128)(2,1)} %bitcast.9), custom_call_target="tpu_custom_call" | custom-call | bytes 1310720 | tf_op jit(solution)/shard_map/pool/pallas_call | solution.py:32
  2.6 3.3 %collective-permute-start = (bf16[128,512]{1,0:T(8,128)(2,1)S(1)}, bf16[128,512]{1,0:T(8,128)(2,1)S(1)}, u32[]{:S(2)}, u32[]{:S(2)}) collective-permute-start(bf16[128,512]{1,0:T(8,128)(2,1)S(1)} %get-tuple-element.39), channel_id=1, source_target_pairs={{0,1},{1,0},{2,3},{3,2},{4,5},{5,4},{6,7},{7,6},{8,9},{9,8},{10,11... | collective-permute-start | bytes 393224 | tf_op jit(solution)/shard_map/ppermute | solution.py:47
  5.9 0.0 collective-permute-start.1
  5.9 1.7 %collective-permute-start.2 = (bf16[128,512]{1,0:T(8,128)(2,1)S(1)}, bf16[128,512]{1,0:T(8,128)(2,1)S(1)}, u32[]{:S(2)}, u32[]{:S(2)}) collective-permute-start(bf16[128,512]{1,0:T(8,128)(2,1)S(1)} %get-tuple-element.41), channel_id=1, source_target_pairs={{0,3},{1,2},{2,1},{3,0},{4,7},{5,6},{6,5},{7,4},{8,11},{9,10},{10,... | collective-permute-start | bytes 393224 | tf_op jit(solution)/shard_map/ppermute | solution.py:47
  7.6 7.3 %all-to-all-start = ((bf16[64,16,128]{2,1,0:T(8,128)(2,1)}), bf16[64,16,128]{2,1,0:T(8,128)(2,1)S(1)}, u32[]{:S(2)}, u32[]{:S(2)}) async-start(bf16[64,16,128]{2,1,0:T(8,128)(2,1)} %get-tuple-element.44), calls=%async_computation | async-start | bytes 524288 | tf_op jit(solution)/shard_map/all_to_all | solution.py:52
  14.9 0.0 collective-permute-done.refs_1_
  14.9 0.0 collective-permute-done.1.refs_2_
  14.9 0.0 collective-permute-done.2.refs_3_
  14.9 0.2 team.1
  15.1 6.1 %collective-permute-start.5 = (bf16[64,256]{1,0:T(8,128)(2,1)S(1)}, bf16[64,256]{1,0:T(8,128)(2,1)S(1)}, u32[]{:S(2)}, u32[]{:S(2)}) collective-permute-start(bf16[64,256]{1,0:T(8,128)(2,1)S(1)} %get-tuple-element.46), channel_id=1, source_target_pairs={{0,8},{1,9},{2,10},{3,11},{4,12},{5,13},{6,14},{7,15},{8,0},{9,1},... | collective-permute-start | bytes 98312 | tf_op jit(solution)/shard_map/ppermute | solution.py:47
  21.2 0.3 collective-permute-start.4
  21.5 0.9 %collective-permute-start.3 = (bf16[128,256]{1,0:T(8,128)(2,1)S(1)}, bf16[128,256]{1,0:T(8,128)(2,1)S(1)}, u32[]{:S(2)}, u32[]{:S(2)}) collective-permute-start(bf16[128,256]{1,0:T(8,128)(2,1)S(1)} %get-tuple-element.45), channel_id=1, source_target_pairs={{0,4},{1,5},{2,6},{3,7},{4,0},{5,1},{6,2},{7,3},{8,12},{9,13},{10,... | collective-permute-start | bytes 196616 | tf_op jit(solution)/shard_map/ppermute | solution.py:47
  22.4 2.5 %all-to-all-done.refs_0_ = bf16[64,16,128]{2,1,0:T(8,128)(2,1)S(1)} async-done(((bf16[64,16,128]{2,1,0:T(8,128)(2,1)}), bf16[64,16,128]{2,1,0:T(8,128)(2,1)S(1)}, u32[]{:S(2)}, u32[]{:S(2)}) %all-to-all-start) | async-done | bytes 262176 | tf_op jit(solution)/shard_map/all_to_all | solution.py:52
  24.9 6.4 %collective-permute-start.8 = (bf16[128,256]{1,0:T(8,128)(2,1)S(1)}, bf16[128,256]{1,0:T(8,128)(2,1)S(1)}, u32[]{:S(2)}, u32[]{:S(2)}) collective-permute-start(bf16[128,256]{1,0:T(8,128)(2,1)S(1)} %collect.1.refs_2_), channel_id=1, source_target_pairs={{0,8},{1,9},{2,10},{3,11},{4,12},{5,13},{6,14},{7,15},{8,0},{9,1},... | collective-permute-start | bytes 196616 | tf_op jit(solution)/shard_map/ppermute | solution.py:47
  31.4 0.0 collective-permute-start.7
  31.4 0.0 collective-permute-done.5.refs_2_
  31.4 1.2 %collective-permute-start.6 = (bf16[128,256]{1,0:T(8,128)(2,1)S(1)}, bf16[128,256]{1,0:T(8,128)(2,1)S(1)}, u32[]{:S(2)}, u32[]{:S(2)}) collective-permute-start(bf16[128,256]{1,0:T(8,128)(2,1)S(1)} %collect.1.refs_2_), channel_id=1, source_target_pairs={{0,4},{1,5},{2,6},{3,7},{4,0},{5,1},{6,2},{7,3},{8,12},{9,13},{10,... | collective-permute-start | bytes 196616 | tf_op jit(solution)/shard_map/ppermute | solution.py:47
  32.6 0.0 collective-permute-done.4.refs_1_
  32.6 0.0 collective-permute-done.3.refs_0_
  32.6 1.3 %first.1 = (bf16[2,768,256]{2,1,0:T(8,128)(2,1)S(1)}, bf16[2,512,128]{2,1,0:T(8,128)(2,1)S(1)}, bf16[2,512,128]{2,1,0:T(8,128)(2,1)S(1)}, f32[2,768,512]{2,1,0:T...) custom-call(bf16[512,512]{1,0:T(8,128)(2,1)S(1)} %get-tuple-element., ...), custom_call_target="tpu_custom_call" | custom-call | flops 402653184 | bytes 8466432 | tf_op jit(solution)/shard_map/first/pallas_call | solution.py:32
  33.9 0.0 collective-permute-done.8.refs_2_
  33.9 3.1 %collective-permute-done.7.refs_1_ = bf16[128,256]{1,0:T(8,128)(2,1)S(1)} collective-permute-done((bf16[128,256]{1,0:T(8,128)(2,1)S(1)}, bf16[128,256]{1,0:T(8,128)(2,1)S(1)}, u32[]{:S(2)}, u32[]{:S(2)}) %collective-permute-start.7) | collective-permute-done | bytes 65568 | tf_op jit(solution)/shard_map/ppermute | solution.py:47
  37.0 0.7 collective-permute-done.6.refs_0_
  37.6 2.0 %second.1 = (bf16[256,256]{1,0:T(8,128)(2,1)S(1)}, bf16[192,256]{1,0:T(8,128)(2,1)S(1)}, bf16[192,256]{1,0:T(8,128)(2,1)S(1)}, bf16[640,256]{1,0:T(8,128)(2,1)S(...) custom-call(bf16[128,256]{1,0:T(8,128)(2,1)S(1)} %collective-permute, ...), custom_call_target="tpu_custom_call" | custom-call | flops 671088640 | bytes 10440704 | tf_op jit(solution)/shard_map/second/pallas_call | solution.py:32
  39.6 4.6 %collective-permute-start.10 = (bf16[192,256]{1,0:T(8,128)(2,1)S(1)}, bf16[192,256]{1,0:T(8,128)(2,1)S(1)}, u32[]{:S(2)}, u32[]{:S(2)}) collective-permute-start(bf16[192,256]{1,0:T(8,128)(2,1)S(1)} %get-tuple-element.63), channel_id=1, source_target_pairs={{0,8},{1,9},{2,10},{3,11},{4,12},{5,13},{6,14},{7,15},{8,0},{9,1},... | collective-permute-start | bytes 294920 | tf_op jit(solution)/shard_map/ppermute | solution.py:47
  44.2 1.4 %collective-permute-start.11 = (bf16[192,256]{1,0:T(8,128)(2,1)S(1)}, bf16[192,256]{1,0:T(8,128)(2,1)S(1)}, u32[]{:S(2)}, u32[]{:S(2)}) collective-permute-start(bf16[192,256]{1,0:T(8,128)(2,1)S(1)} %get-tuple-element.64), channel_id=1, source_target_pairs={{0,12},{1,13},{2,14},{3,15},{4,8},{5,9},{6,10},{7,11},{8,4},{9,5},... | collective-permute-start | bytes 294920 | tf_op jit(solution)/shard_map/ppermute | solution.py:47
  45.6 0.0 collective-permute-start.9
  45.6 1.5 %rest.1 = (f32[128,256]{1,0:T(8,128)S(1)}, f32[256,256]{1,0:T(8,128)S(1)}, f32[512,256]{1,0:T(8,128)S(1)}, bf16[512,256]{1,0:T(8,128)(2,1)S(1)}) custom-call(bf16[2,768,256]{2,1,0:T(8,128)(2,1)S(1)} %get-tuple-element.47.refs_0_, bf16[640,256]{1,0:T(8,128)(2,1)S(1)} %get-tuple-element.55.refs_1_, bf16[2,512,128]{2,1,0:T(8,128)(2,1)S(1)} %get-tuple-element.48.refs_4_.refs_2_, ...), custom_call_target="tpu_custom_call" | custom-call | flops 1207959552 | bytes 11739136 | tf_op jit(solution)/shard_map/rest/pallas_call | solution.py:32
  47.0 0.2 collective-permute-done.10.refs_0_
  47.2 7.1 %collective-permute-done.11.refs_3_ = bf16[192,256]{1,0:T(8,128)(2,1)S(1)} collective-permute-done((bf16[192,256]{1,0:T(8,128)(2,1)S(1)}, bf16[192,256]{1,0:T(8,128)(2,1)S(1)}, u32[]{:S(2)}, u32[]{:S(2)}) %collective-permute-start.11) | collective-permute-done | bytes 98336 | tf_op jit(solution)/shard_map/ppermute | solution.py:47
  54.3 0.9 %collective-permute-done.9.refs_1_ = bf16[256,256]{1,0:T(8,128)(2,1)S(1)} collective-permute-done((bf16[256,256]{1,0:T(8,128)(2,1)S(1)}, bf16[256,256]{1,0:T(8,128)(2,1)S(1)}, u32[]{:S(2)}, u32[]{:S(2)}) %collective-permute-start.9) | collective-permute-done | bytes 131104 | tf_op jit(solution)/shard_map/ppermute | solution.py:47
  55.2 0.8 %scatter.1 = (bf16[64,16,128]{2,1,0:T(8,128)(2,1)}, f32[128,256]{1,0:T(8,128)S(1)}, bf16[128,512]{1,0:T(8,128)(2,1)S(1)}, bf16[256,512]{1,0:T(8,128)(2,1)S(1)}) custom-call(f32[128,256]{1,0:T(8,128)S(1)} %get-tuple-element.61.refs_0_, bf16[256,256]{1,0:T(8,128)(2,1)S(1)} %collective-permute-done.9.refs_1_, bf16[192,256]{1,0:T(8,128)(2,1)S(1)} %hold.1.refs_2_, ...), custom_call_target="tpu_custom_call" | custom-call | bytes 2293760 | tf_op jit(solution)/shard_map/scatter/pallas_call | solution.py:32
  56.0 0.1 collective-permute-start.13
  56.1 1.4 %collective-permute-start.12 = (bf16[128,512]{1,0:T(8,128)(2,1)S(1)}, bf16[128,512]{1,0:T(8,128)(2,1)S(1)}, u32[]{:S(2)}, u32[]{:S(2)}) collective-permute-start(bf16[128,512]{1,0:T(8,128)(2,1)S(1)} %get-tuple-element.67), channel_id=1, source_target_pairs={{0,1},{1,0},{2,3},{3,2},{4,5},{5,4},{6,7},{7,6},{8,9},{9,8},{10,11... | collective-permute-start | bytes 393224 | tf_op jit(solution)/shard_map/ppermute | solution.py:47
  57.5 5.4 %all-to-all-start.1 = ((bf16[64,16,128]{2,1,0:T(8,128)(2,1)}), bf16[64,16,128]{2,1,0:T(8,128)(2,1)S(1)}, u32[]{:S(2)}, u32[]{:S(2)}) async-start(bf16[64,16,128]{2,1,0:T(8,128)(2,1)} %get-tuple-element.72), calls=%async_computation.1 | async-start | bytes 524288 | tf_op jit(solution)/shard_map/all_to_all | solution.py:52
  62.9 0.0 collective-permute-done.12.refs_1_
  62.9 0.6 collective-permute-done.13.refs_2_.refs_0_
  63.5 1.4 %collective-permute-start.14 = (bf16[128,512]{1,0:T(8,128)(2,1)S(1)}, bf16[128,512]{1,0:T(8,128)(2,1)S(1)}, u32[]{:S(2)}, u32[]{:S(2)}) collective-permute-start(bf16[128,512]{1,0:T(8,128)(2,1)S(1)} %relay.1), channel_id=1, source_target_pairs={{0,1},{1,0},{2,3},{3,2},{4,5},{5,4},{6,7},{7,6},{8,9},{9,8},{10,11... | collective-permute-start | bytes 393224 | tf_op jit(solution)/shard_map/ppermute | solution.py:47
  65.0 1.0 %collective-permute-done.14.refs_3_.refs_2_ = bf16[128,512]{1,0:T(8,128)(2,1)S(1)} collective-permute-done((bf16[128,512]{1,0:T(8,128)(2,1)S(1)}, bf16[128,512]{1,0:T(8,128)(2,1)S(1)}, u32[]{:S(2)}, u32[]{:S(2)}) %collective-permute-start.14) | collective-permute-done | bytes 131104 | tf_op jit(solution)/shard_map/ppermute | solution.py:47
  65.9 0.7 outputs.1
  66.7 6.2 %all-to-all-done.1.refs_0_ = bf16[64,16,128]{2,1,0:T(8,128)(2,1)S(1)} async-done(((bf16[64,16,128]{2,1,0:T(8,128)(2,1)}), bf16[64,16,128]{2,1,0:T(8,128)(2,1)S(1)}, u32[]{:S(2)}, u32[]{:S(2)}) %all-to-all-start.1) | async-done | bytes 262176 | tf_op jit(solution)/shard_map/all_to_all | solution.py:52
  72.9 0.8 %finish.1 = bf16[128,1024]{1,0:T(8,128)(2,1)} custom-call(bf16[64,16,128]{2,1,0:T(8,128)(2,1)S(1)} %all-to-all-done.1.refs_0_, f32[128,1024]{1,0:T(8,128)S(1)} %merge.1.refs_1_, bf16[128,512]{1,0:T(8,128)(2,1)S(1)} %collective-permute-done.14.refs_3_.refs_2_), custom_call_target="tpu_custom_call" | custom-call | bytes 1179648 | tf_op jit(solution)/shard_map/finish/pallas_call | solution.py:32
  (5 shorter events, 0.1 us)
Async XLA Ops:
  2.6 12.3 %collective-permute-start = (bf16[128,512]{1,0:T(8,128)(2,1)S(1)}, bf16[128,512]{1,0:T(8,128)(2,1)S(1)}, u32[]{:S(2)}, u32[]{:S(2)}) collective-permute-start(bf16[128,512]{1,0:T(8,128)(2,1)S(1)} %get-tuple-element.39), channel_id=1, source_target_pairs={{0,1},{1,0},{2,3},{3,2},{4,5},{5,4},{6,7},{7,6},{8,9},{9,8},{10,11... | collective-permute-start | bytes 393224 | tf_op jit(solution)/shard_map/ppermute | solution.py:47
  5.9 9.0 %collective-permute-start.1 = (bf16[128,512]{1,0:T(8,128)(2,1)S(1)}, bf16[128,512]{1,0:T(8,128)(2,1)S(1)}, u32[]{:S(2)}, u32[]{:S(2)}) collective-permute-start(bf16[128,512]{1,0:T(8,128)(2,1)S(1)} %get-tuple-element.40), channel_id=1, source_target_pairs={{0,2},{1,3},{2,0},{3,1},{4,6},{5,7},{6,4},{7,5},{8,10},{9,11},{10,... | collective-permute-start | bytes 393224 | tf_op jit(solution)/shard_map/ppermute | solution.py:47
  5.9 9.0 %collective-permute-start.2 = (bf16[128,512]{1,0:T(8,128)(2,1)S(1)}, bf16[128,512]{1,0:T(8,128)(2,1)S(1)}, u32[]{:S(2)}, u32[]{:S(2)}) collective-permute-start(bf16[128,512]{1,0:T(8,128)(2,1)S(1)} %get-tuple-element.41), channel_id=1, source_target_pairs={{0,3},{1,2},{2,1},{3,0},{4,7},{5,6},{6,5},{7,4},{8,11},{9,10},{10,... | collective-permute-start | bytes 393224 | tf_op jit(solution)/shard_map/ppermute | solution.py:47
  7.6 17.3 %all-to-all-start = ((bf16[64,16,128]{2,1,0:T(8,128)(2,1)}), bf16[64,16,128]{2,1,0:T(8,128)(2,1)S(1)}, u32[]{:S(2)}, u32[]{:S(2)}) async-start(bf16[64,16,128]{2,1,0:T(8,128)(2,1)} %get-tuple-element.44), calls=%async_computation | async-start | bytes 524288 | tf_op jit(solution)/shard_map/all_to_all | solution.py:52
  15.1 16.3 %collective-permute-start.5 = (bf16[64,256]{1,0:T(8,128)(2,1)S(1)}, bf16[64,256]{1,0:T(8,128)(2,1)S(1)}, u32[]{:S(2)}, u32[]{:S(2)}) collective-permute-start(bf16[64,256]{1,0:T(8,128)(2,1)S(1)} %get-tuple-element.46), channel_id=1, source_target_pairs={{0,8},{1,9},{2,10},{3,11},{4,12},{5,13},{6,14},{7,15},{8,0},{9,1},... | collective-permute-start | bytes 98312 | tf_op jit(solution)/shard_map/ppermute | solution.py:47
  21.2 11.4 %collective-permute-start.4 = (bf16[64,256]{1,0:T(8,128)(2,1)S(1)}, bf16[64,256]{1,0:T(8,128)(2,1)S(1)}, u32[]{:S(2)}, u32[]{:S(2)}) collective-permute-start(bf16[64,256]{1,0:T(8,128)(2,1)S(1)} %get-tuple-element.46), channel_id=1, source_target_pairs={{0,12},{1,13},{2,14},{3,15},{4,8},{5,9},{6,10},{7,11},{8,4},{9,5},... | collective-permute-start | bytes 98312 | tf_op jit(solution)/shard_map/ppermute | solution.py:47
  21.5 11.1 %collective-permute-start.3 = (bf16[128,256]{1,0:T(8,128)(2,1)S(1)}, bf16[128,256]{1,0:T(8,128)(2,1)S(1)}, u32[]{:S(2)}, u32[]{:S(2)}) collective-permute-start(bf16[128,256]{1,0:T(8,128)(2,1)S(1)} %get-tuple-element.45), channel_id=1, source_target_pairs={{0,4},{1,5},{2,6},{3,7},{4,0},{5,1},{6,2},{7,3},{8,12},{9,13},{10,... | collective-permute-start | bytes 196616 | tf_op jit(solution)/shard_map/ppermute | solution.py:47
  24.9 9.0 %collective-permute-start.8 = (bf16[128,256]{1,0:T(8,128)(2,1)S(1)}, bf16[128,256]{1,0:T(8,128)(2,1)S(1)}, u32[]{:S(2)}, u32[]{:S(2)}) collective-permute-start(bf16[128,256]{1,0:T(8,128)(2,1)S(1)} %collect.1.refs_2_), channel_id=1, source_target_pairs={{0,8},{1,9},{2,10},{3,11},{4,12},{5,13},{6,14},{7,15},{8,0},{9,1},... | collective-permute-start | bytes 196616 | tf_op jit(solution)/shard_map/ppermute | solution.py:47
  31.4 5.6 %collective-permute-start.7 = (bf16[128,256]{1,0:T(8,128)(2,1)S(1)}, bf16[128,256]{1,0:T(8,128)(2,1)S(1)}, u32[]{:S(2)}, u32[]{:S(2)}) collective-permute-start(bf16[128,256]{1,0:T(8,128)(2,1)S(1)} %collect.1.refs_2_), channel_id=1, source_target_pairs={{0,12},{1,13},{2,14},{3,15},{4,8},{5,9},{6,10},{7,11},{8,4},{9,5},... | collective-permute-start | bytes 196616 | tf_op jit(solution)/shard_map/ppermute | solution.py:47
  31.4 6.3 %collective-permute-start.6 = (bf16[128,256]{1,0:T(8,128)(2,1)S(1)}, bf16[128,256]{1,0:T(8,128)(2,1)S(1)}, u32[]{:S(2)}, u32[]{:S(2)}) collective-permute-start(bf16[128,256]{1,0:T(8,128)(2,1)S(1)} %collect.1.refs_2_), channel_id=1, source_target_pairs={{0,4},{1,5},{2,6},{3,7},{4,0},{5,1},{6,2},{7,3},{8,12},{9,13},{10,... | collective-permute-start | bytes 196616 | tf_op jit(solution)/shard_map/ppermute | solution.py:47
  39.6 7.6 %collective-permute-start.10 = (bf16[192,256]{1,0:T(8,128)(2,1)S(1)}, bf16[192,256]{1,0:T(8,128)(2,1)S(1)}, u32[]{:S(2)}, u32[]{:S(2)}) collective-permute-start(bf16[192,256]{1,0:T(8,128)(2,1)S(1)} %get-tuple-element.63), channel_id=1, source_target_pairs={{0,8},{1,9},{2,10},{3,11},{4,12},{5,13},{6,14},{7,15},{8,0},{9,1},... | collective-permute-start | bytes 294920 | tf_op jit(solution)/shard_map/ppermute | solution.py:47
  44.2 10.1 %collective-permute-start.11 = (bf16[192,256]{1,0:T(8,128)(2,1)S(1)}, bf16[192,256]{1,0:T(8,128)(2,1)S(1)}, u32[]{:S(2)}, u32[]{:S(2)}) collective-permute-start(bf16[192,256]{1,0:T(8,128)(2,1)S(1)} %get-tuple-element.64), channel_id=1, source_target_pairs={{0,12},{1,13},{2,14},{3,15},{4,8},{5,9},{6,10},{7,11},{8,4},{9,5},... | collective-permute-start | bytes 294920 | tf_op jit(solution)/shard_map/ppermute | solution.py:47
  45.6 9.7 %collective-permute-start.9 = (bf16[256,256]{1,0:T(8,128)(2,1)S(1)}, bf16[256,256]{1,0:T(8,128)(2,1)S(1)}, u32[]{:S(2)}, u32[]{:S(2)}) collective-permute-start(bf16[256,256]{1,0:T(8,128)(2,1)S(1)} %get-tuple-element.62), channel_id=1, source_target_pairs={{0,4},{1,5},{2,6},{3,7},{4,0},{5,1},{6,2},{7,3},{8,12},{9,13},{10,... | collective-permute-start | bytes 393224 | tf_op jit(solution)/shard_map/ppermute | solution.py:47
  56.0 7.5 %collective-permute-start.13 = (bf16[256,512]{1,0:T(8,128)(2,1)S(1)}, bf16[256,512]{1,0:T(8,128)(2,1)S(1)}, u32[]{:S(2)}, u32[]{:S(2)}) collective-permute-start(bf16[256,512]{1,0:T(8,128)(2,1)S(1)} %get-tuple-element.68), channel_id=1, source_target_pairs={{0,2},{1,3},{2,0},{3,1},{4,6},{5,7},{6,4},{7,5},{8,10},{9,11},{10,... | collective-permute-start | bytes 786440 | tf_op jit(solution)/shard_map/ppermute | solution.py:47
  56.1 6.8 %collective-permute-start.12 = (bf16[128,512]{1,0:T(8,128)(2,1)S(1)}, bf16[128,512]{1,0:T(8,128)(2,1)S(1)}, u32[]{:S(2)}, u32[]{:S(2)}) collective-permute-start(bf16[128,512]{1,0:T(8,128)(2,1)S(1)} %get-tuple-element.67), channel_id=1, source_target_pairs={{0,1},{1,0},{2,3},{3,2},{4,5},{5,4},{6,7},{7,6},{8,9},{9,8},{10,11... | collective-permute-start | bytes 393224 | tf_op jit(solution)/shard_map/ppermute | solution.py:47
  57.5 15.4 %all-to-all-start.1 = ((bf16[64,16,128]{2,1,0:T(8,128)(2,1)}), bf16[64,16,128]{2,1,0:T(8,128)(2,1)S(1)}, u32[]{:S(2)}, u32[]{:S(2)}) async-start(bf16[64,16,128]{2,1,0:T(8,128)(2,1)} %get-tuple-element.72), calls=%async_computation.1 | async-start | bytes 524288 | tf_op jit(solution)/shard_map/all_to_all | solution.py:52
  63.5 2.4 %collective-permute-start.14 = (bf16[128,512]{1,0:T(8,128)(2,1)S(1)}, bf16[128,512]{1,0:T(8,128)(2,1)S(1)}, u32[]{:S(2)}, u32[]{:S(2)}) collective-permute-start(bf16[128,512]{1,0:T(8,128)(2,1)S(1)} %relay.1), channel_id=1, source_target_pairs={{0,1},{1,0},{2,3},{3,2},{4,5},{5,4},{6,7},{7,6},{8,9},{9,8},{10,11... | collective-permute-start | bytes 393224 | tf_op jit(solution)/shard_map/ppermute | solution.py:47

commit v5 on v4

--- a/solution.py
+++ b/solution.py
@@ -151,7 +151,7 @@
     return jnp.concatenate([block[:8], block[8:]], axis=1)
 
 
-def team_kernel(own_ref, got1_ref, got2_ref, got3_ref, tokens_ref, one_ref, two_ref, three_ref, rows_ref):
+def team_kernel(own_ref, got2_ref, got3_ref, got1_ref, tokens_ref, one_ref, two_ref, three_ref, rows_ref):
     for k, ref in enumerate((own_ref, got1_ref, got2_ref, got3_ref)):
         tokens_ref[LEAF * k : LEAF * k + LEAF, :] = ref[...]
     write_rows(rows_ref, tokens_ref[:, 128:384].astype(F32))
@@ -209,27 +209,47 @@
         dot_ref[s] = jnp.sum(exps * dweights, axis=0, keepdims=True)
 
 
+def middle_kernel(
+    got6_ref, got4_ref, q2_ref, cot2_ref, max_ref, sum_ref, dot_ref,
+    keys_ref, exps_ref, dweights_ref, top_ref, total_ref, dots_ref, before_ref,
+):
+    keys_ref[0:128, :] = got4_ref[...]
+    keys_ref[128:256, :] = got6_ref[...]
+    for s in range(2):
+        scores = across(keys_ref[:, 0:128], q2_ref[s])
+        dweights = across(keys_ref[:, 128:256], cot2_ref[s])
+        top = jnp.maximum(max_ref[s], jnp.max(scores, axis=0, keepdims=True))
+        exps = jnp.exp(scores - top)
+        before = jnp.exp(max_ref[s] - top)
+        exps_ref[s] = exps
+        dweights_ref[s] = dweights
+        top_ref[s] = top
+        total_ref[s] = sum_ref[s] * before + jnp.sum(exps, axis=0, keepdims=True)
+        dots_ref[s] = dot_ref[s] * before + jnp.sum(exps * dweights, axis=0, keepdims=True)
+        before_ref[s] = before
+
+
 def second_kernel(
-    got2_ref, got6_ref, got4_ref, low_ref, q2_ref, cot2_ref, exps_ref, dweights_ref, max_ref, sum_ref, dot_ref,
+    got2_ref, mid_ref, low_ref, q2_ref, cot2_ref, exps_ref, dweights_ref, mid_exps_ref, mid_dweights_ref, max_ref, sum_ref, dot_ref, first_ref,
     send2_ref, send4_ref, send6_ref, keys_ref, factor_ref, centre_ref, rounded_ref, dscores_ref,
 ):
     keys_ref[0:128, :] = got2_ref[...]
-    keys_ref[128:256, :] = got4_ref[...]
-    keys_ref[256:384, :] = got6_ref[...]
+    keys_ref[128:384, :] = mid_ref[...]
     keys_ref[384:640, :] = low_ref[...]
     dkeys, dvals = [], []
     for s in range(2):
         queries, grads = q2_ref[s], cot2_ref[s]
-        scores = across(keys_ref[0:384, 0:128], queries)
-        dweights = across(keys_ref[0:384, 128:256], grads)
+        scores = across(keys_ref[0:128, 0:128], queries)
+        dweights = across(keys_ref[0:128, 128:256], grads)
         top = jnp.maximum(max_ref[s], jnp.max(scores, axis=0, keepdims=True))
         exps = jnp.exp(scores - top)
         before = jnp.exp(max_ref[s] - top)
         inverse = 1.0 / (sum_ref[s] * before + jnp.sum(exps, axis=0, keepdims=True))
         centre = (dot_ref[s] * before + jnp.sum(exps * dweights, axis=0, keepdims=True)) * inverse
-        factor = before * inverse
-        weights = jnp.concatenate([exps * inverse, exps_ref[s, 512:768, :] * factor], axis=0)
-        dweights = jnp.concatenate([dweights, dweights_ref[s, 512:768, :]], axis=0)
+        middle = before * inverse
+        factor = first_ref[s] * middle
+        weights = jnp.concatenate([exps * inverse, mid_exps_ref[s] * middle, exps_ref[s, 512:768, :] * factor], axis=0)
+        dweights = jnp.concatenate([dweights, mid_dweights_ref[s], dweights_ref[s, 512:768, :]], axis=0)
         rounded = weights.astype(BF16)
         dscores = (weights * (dweights - centre)).astype(BF16)
         factor_ref[s] = factor
@@ -370,7 +390,7 @@
         [((512, D), BF16), ((256, 256), BF16), ((128, 256), BF16), ((64, 256), BF16)],
         [team_rows],
         flops=LONG,
-    )(own, got1, got2, got3)
+    )(own, got2, got3, got1)
     low4 = exchange(three, 8)
     low6 = exchange(three, 12)
     low2 = exchange(two, 4)
@@ -389,13 +409,17 @@
         [((2, 768, 256), BF16), stacks, stacks, squares, squares, stat, stat, stat],
         flops=4 * 768 * 1024 * 128,
     )(tokens, one, block, low)
+    mids = ((2, 256, 512), F32)
+    mid_keys, mid_exps, mid_dweights, top, sums, dots, before = call(
+        middle_kernel, "middle", [((256, 256), BF16), mids, mids, stat, stat, stat, stat], flops=4 * 256 * 1024 * 128
+    )(got6, got4, q2, cot2, top, sums, dots)
     later = ((2, 640, 512), BF16)
     send2, send4, send6, later_keys, factor, centre, rounded, dscores = call(
         second_kernel,
         "second",
         [((256, 256), BF16), ((192, 256), BF16), ((192, 256), BF16), ((640, 256), BF16), stat, stat, later, later],
         flops=8 * 640 * 1024 * 128,
-    )(got2, got6, got4, low, q2, cot2, exps, dweights, top, sums, dots)
+    )(got2, mid_keys, low, q2, cot2, exps, dweights, mid_exps, mid_dweights, top, sums, dots, before)
     back4 = exchange(send4, 8)
     back6 = exchange(send6, 12)
     back2 = exchange(send2, 4)

time: 74 us -> 73.9 us (level)
    all_to_all x2, starting transfers between devices: 12.7 us -> 13.4 us  [trade_slots(): lax.all_to_all(slots, ('outer', 'inner'), 0, 0, axis_index_groups=groups,...]
    pallas_call x13 -> x14, Pallas kernels: 9.3 us -> 9.3 us  [run(): pl.pallas_call(lambda *refs: body(*refs[:count], *refs[count + len(after)...]
  transfers between devices with their start and end apart: 17 -> 17, of which waited for: 9 -> 9; matrix products, arithmetic and copies ran while one was open for 0% -> 0% of each run, Pallas kernels for 5% -> 6%
where the time goes in v5:
time: 73.9 us; the launch traced here: 73.6 us
  starting transfers between devices  42 us (57%)
  waiting for transfers between devices  21.6 us (29%)
  Pallas kernels  9.3 us (13%)
  between operations  0.78 us (1%)
    ppermute x15, starting transfers between devices, exchange(): return lax.ppermute(array, 'inner', [(i, i ^ bits) for i in range(16)])  28.5 us
    all_to_all x2, starting transfers between devices, trade_slots(): lax.all_to_all(slots, ('outer', 'inner'), 0, 0, axis_index_groups=groups,...  13.4 us
    ppermute x15, waiting for transfers between devices, exchange(): return lax.ppermute(array, 'inner', [(i, i ^ bits) for i in range(16)])  12.7 us
    pallas_call x14, Pallas kernels, run(): pl.pallas_call(lambda *refs: body(*refs[:count], *refs[count + len(after)...  9.3 us
    all_to_all x2, waiting for transfers between devices, trade_slots(): lax.all_to_all(slots, ('outer', 'inner'), 0, 0, axis_index_groups=groups,...  8.86 us
  transfers between devices with their start and end apart: 17, of which 9 were waited for; matrix products, arithmetic and copies ran while one was open for 0% of the time, Pallas kernels for 6%

profile of v5, /device:TPU:1, one launch (start us, length us, event | category | flops | bytes accessed | tf_op | source)
XLA Modules:
  0.0 73.6 jit_solution(13751507388897899436)
XLA Ops:
  0.6 1.9 %pool.1 = (bf16[64,16,128]{2,1,0:T(8,128)(2,1)}, bf16[128,512]{1,0:T(8,128)(2,1)S(1)}, bf16[128,512]{1,0:T(8,128)(2,1)S(1)}, bf16[128,512]{1,0:T(8,128)(2,1)S(1)}, bf16[128,512]{1,0:T(8,128)(2,1)S(1)}) custom-call(bf16[128,512]{1,0:T(8,128)(2,1)} %bitcast.8, bf16[128,1024]{1,0:T(8,128)(2,1)} %bitcast.6, bf16[128,512]{1,0:T(8,128)(2,1)} %bitcast.9), custom_call_target="tpu_custom_call" | custom-call | bytes 1310720 | tf_op jit(solution)/shard_map/pool/pallas_call | solution.py:32
  2.6 2.6 %collective-permute-start = (bf16[128,512]{1,0:T(8,128)(2,1)S(1)}, bf16[128,512]{1,0:T(8,128)(2,1)S(1)}, u32[]{:S(2)}, u32[]{:S(2)}) collective-permute-start(bf16[128,512]{1,0:T(8,128)(2,1)S(1)} %get-tuple-element.46), channel_id=1, source_target_pairs={{0,2},{1,3},{2,0},{3,1},{4,6},{5,7},{6,4},{7,5},{8,10},{9,11},{10,... | collective-permute-start | bytes 393224 | tf_op jit(solution)/shard_map/ppermute | solution.py:47
  5.1 2.4 %collective-permute-start.1 = (bf16[128,512]{1,0:T(8,128)(2,1)S(1)}, bf16[128,512]{1,0:T(8,128)(2,1)S(1)}, u32[]{:S(2)}, u32[]{:S(2)}) collective-permute-start(bf16[128,512]{1,0:T(8,128)(2,1)S(1)} %get-tuple-element.47), channel_id=1, source_target_pairs={{0,3},{1,2},{2,1},{3,0},{4,7},{5,6},{6,5},{7,4},{8,11},{9,10},{10,... | collective-permute-start | bytes 393224 | tf_op jit(solution)/shard_map/ppermute | solution.py:47
  7.5 0.0 collective-permute-start.2
  7.5 7.6 %all-to-all-start = ((bf16[64,16,128]{2,1,0:T(8,128)(2,1)}), bf16[64,16,128]{2,1,0:T(8,128)(2,1)S(1)}, u32[]{:S(2)}, u32[]{:S(2)}) async-start(bf16[64,16,128]{2,1,0:T(8,128)(2,1)} %get-tuple-element.51), calls=%async_computation | async-start | bytes 524288 | tf_op jit(solution)/shard_map/all_to_all | solution.py:52
  15.1 0.0 collective-permute-done.refs_1_
  15.1 0.0 collective-permute-done.1.refs_2_
  15.2 0.0 collective-permute-done.2.refs_3_
  15.2 0.2 team.1
  15.4 6.1 %collective-permute-start.5 = (bf16[64,256]{1,0:T(8,128)(2,1)S(1)}, bf16[64,256]{1,0:T(8,128)(2,1)S(1)}, u32[]{:S(2)}, u32[]{:S(2)}) collective-permute-start(bf16[64,256]{1,0:T(8,128)(2,1)S(1)} %get-tuple-element.53), channel_id=1, source_target_pairs={{0,8},{1,9},{2,10},{3,11},{4,12},{5,13},{6,14},{7,15},{8,0},{9,1},... | collective-permute-start | bytes 98312 | tf_op jit(solution)/shard_map/ppermute | solution.py:47
  21.4 0.3 collective-permute-start.4
  21.7 0.9 %collective-permute-start.3 = (bf16[128,256]{1,0:T(8,128)(2,1)S(1)}, bf16[128,256]{1,0:T(8,128)(2,1)S(1)}, u32[]{:S(2)}, u32[]{:S(2)}) collective-permute-start(bf16[128,256]{1,0:T(8,128)(2,1)S(1)} %get-tuple-element.52), channel_id=1, source_target_pairs={{0,4},{1,5},{2,6},{3,7},{4,0},{5,1},{6,2},{7,3},{8,12},{9,13},{10,... | collective-permute-start | bytes 196616 | tf_op jit(solution)/shard_map/ppermute | solution.py:47
  22.6 2.5 %all-to-all-done.refs_0_ = bf16[64,16,128]{2,1,0:T(8,128)(2,1)S(1)} async-done(((bf16[64,16,128]{2,1,0:T(8,128)(2,1)}), bf16[64,16,128]{2,1,0:T(8,128)(2,1)S(1)}, u32[]{:S(2)}, u32[]{:S(2)}) %all-to-all-start) | async-done | bytes 262176 | tf_op jit(solution)/shard_map/all_to_all | solution.py:52
  25.2 6.4 %collective-permute-start.8 = (bf16[128,256]{1,0:T(8,128)(2,1)S(1)}, bf16[128,256]{1,0:T(8,128)(2,1)S(1)}, u32[]{:S(2)}, u32[]{:S(2)}) collective-permute-start(bf16[128,256]{1,0:T(8,128)(2,1)S(1)} %collect.1.refs_2_), channel_id=1, source_target_pairs={{0,8},{1,9},{2,10},{3,11},{4,12},{5,13},{6,14},{7,15},{8,0},{9,1},... | collective-permute-start | bytes 196616 | tf_op jit(solution)/shard_map/ppermute | solution.py:47
  31.6 0.0 collective-permute-start.7
  31.6 0.0 collective-permute-done.5.refs_2_
  31.6 1.2 %collective-permute-start.6 = (bf16[128,256]{1,0:T(8,128)(2,1)S(1)}, bf16[128,256]{1,0:T(8,128)(2,1)S(1)}, u32[]{:S(2)}, u32[]{:S(2)}) collective-permute-start(bf16[128,256]{1,0:T(8,128)(2,1)S(1)} %collect.1.refs_2_), channel_id=1, source_target_pairs={{0,4},{1,5},{2,6},{3,7},{4,0},{5,1},{6,2},{7,3},{8,12},{9,13},{10,... | collective-permute-start | bytes 196616 | tf_op jit(solution)/shard_map/ppermute | solution.py:47
  32.8 0.0 collective-permute-done.4.refs_1_
  32.8 0.0 collective-permute-done.3.refs_0_
  32.8 1.3 %first.1 = (bf16[2,768,256]{2,1,0:T(8,128)(2,1)S(1)}, bf16[2,512,128]{2,1,0:T(8,128)(2,1)S(1)}, bf16[2,512,128]{2,1,0:T(8,128)(2,1)S(1)}, f32[2,768,512]{2,1,0:T...) custom-call(bf16[512,512]{1,0:T(8,128)(2,1)S(1)} %get-tuple-element., ...), custom_call_target="tpu_custom_call" | custom-call | flops 402653184 | bytes 8466432 | tf_op jit(solution)/shard_map/first/pallas_call | solution.py:32
  34.1 0.0 collective-permute-done.8.refs_1_
  34.1 3.1 %collective-permute-done.7.refs_0_ = bf16[128,256]{1,0:T(8,128)(2,1)S(1)} collective-permute-done((bf16[128,256]{1,0:T(8,128)(2,1)S(1)}, bf16[128,256]{1,0:T(8,128)(2,1)S(1)}, u32[]{:S(2)}, u32[]{:S(2)}) %collective-permute-start.7) | collective-permute-done | bytes 65568 | tf_op jit(solution)/shard_map/ppermute | solution.py:47
  37.2 0.5 middle.1
  37.7 0.1 collective-permute-done.6.refs_0_
  37.9 1.5 %second.1 = (bf16[256,256]{1,0:T(8,128)(2,1)S(1)}, bf16[192,256]{1,0:T(8,128)(2,1)S(1)}, bf16[192,256]{1,0:T(8,128)(2,1)S(1)}, bf16[640,256]{1,0:T(8,128)(2,1)S(...) custom-call(bf16[128,256]{1,0:T(8,128)(2,1)S(1)} %collective-permute, ...), custom_call_target="tpu_custom_call" | custom-call | flops 671088640 | bytes 12541952 | tf_op jit(solution)/shard_map/second/pallas_call | solution.py:32
  39.3 5.1 %collective-permute-start.10 = (bf16[192,256]{1,0:T(8,128)(2,1)S(1)}, bf16[192,256]{1,0:T(8,128)(2,1)S(1)}, u32[]{:S(2)}, u32[]{:S(2)}) collective-permute-start(bf16[192,256]{1,0:T(8,128)(2,1)S(1)} %get-tuple-element.77), channel_id=1, source_target_pairs={{0,8},{1,9},{2,10},{3,11},{4,12},{5,13},{6,14},{7,15},{8,0},{9,1},... | collective-permute-start | bytes 294920 | tf_op jit(solution)/shard_map/ppermute | solution.py:47
  44.5 0.8 %collective-permute-start.11 = (bf16[192,256]{1,0:T(8,128)(2,1)S(1)}, bf16[192,256]{1,0:T(8,128)(2,1)S(1)}, u32[]{:S(2)}, u32[]{:S(2)}) collective-permute-start(bf16[192,256]{1,0:T(8,128)(2,1)S(1)} %get-tuple-element.78), channel_id=1, source_target_pairs={{0,12},{1,13},{2,14},{3,15},{4,8},{5,9},{6,10},{7,11},{8,4},{9,5},... | collective-permute-start | bytes 294920 | tf_op jit(solution)/shard_map/ppermute | solution.py:47
  45.3 0.0 collective-permute-start.9
  45.3 1.5 %rest.1 = (f32[128,256]{1,0:T(8,128)S(1)}, f32[256,256]{1,0:T(8,128)S(1)}, f32[512,256]{1,0:T(8,128)S(1)}, bf16[512,256]{1,0:T(8,128)(2,1)S(1)}) custom-call(bf16[2,768,256]{2,1,0:T(8,128)(2,1)S(1)} %get-tuple-element.54.refs_0_, bf16[640,256]{1,0:T(8,128)(2,1)S(1)} %get-tuple-element.69.refs_1_, bf16[2,512,128]{2,1,0:T(8,128)(2,1)S(1)} %get-tuple-element.55.refs_2_.refs_3_, ...), custom_call_target="tpu_custom_call" | custom-call | flops 1207959552 | bytes 11739136 | tf_op jit(solution)/shard_map/rest/pallas_call | solution.py:32
  46.8 0.2 collective-permute-done.10.refs_0_
  47.0 7.4 %collective-permute-done.11.refs_3_ = bf16[192,256]{1,0:T(8,128)(2,1)S(1)} collective-permute-done((bf16[192,256]{1,0:T(8,128)(2,1)S(1)}, bf16[192,256]{1,0:T(8,128)(2,1)S(1)}, u32[]{:S(2)}, u32[]{:S(2)}) %collective-permute-start.11) | collective-permute-done | bytes 98336 | tf_op jit(solution)/shard_map/ppermute | solution.py:47
  54.4 0.6 collective-permute-done.9.refs_1_
  54.9 0.8 %scatter.1 = (bf16[64,16,128]{2,1,0:T(8,128)(2,1)}, f32[128,256]{1,0:T(8,128)S(1)}, bf16[128,512]{1,0:T(8,128)(2,1)S(1)}, bf16[256,512]{1,0:T(8,128)(2,1)S(1)}) custom-call(f32[128,256]{1,0:T(8,128)S(1)} %get-tuple-element.75.refs_0_, bf16[256,256]{1,0:T(8,128)(2,1)S(1)} %collective-permute-done.9.refs_1_, bf16[192,256]{1,0:T(8,128)(2,1)S(1)} %hold.1.refs_2_, ...), custom_call_target="tpu_custom_call" | custom-call | bytes 2293760 | tf_op jit(solution)/shard_map/scatter/pallas_call | solution.py:32
  55.7 0.1 collective-permute-start.13
  55.8 1.1 %collective-permute-start.12 = (bf16[128,512]{1,0:T(8,128)(2,1)S(1)}, bf16[128,512]{1,0:T(8,128)(2,1)S(1)}, u32[]{:S(2)}, u32[]{:S(2)}) collective-permute-start(bf16[128,512]{1,0:T(8,128)(2,1)S(1)} %get-tuple-element.81), channel_id=1, source_target_pairs={{0,1},{1,0},{2,3},{3,2},{4,5},{5,4},{6,7},{7,6},{8,9},{9,8},{10,11... | collective-permute-start | bytes 393224 | tf_op jit(solution)/shard_map/ppermute | solution.py:47
  57.0 5.8 %all-to-all-start.1 = ((bf16[64,16,128]{2,1,0:T(8,128)(2,1)}), bf16[64,16,128]{2,1,0:T(8,128)(2,1)S(1)}, u32[]{:S(2)}, u32[]{:S(2)}) async-start(bf16[64,16,128]{2,1,0:T(8,128)(2,1)} %get-tuple-element.86), calls=%async_computation.1 | async-start | bytes 524288 | tf_op jit(solution)/shard_map/all_to_all | solution.py:52
  62.8 0.0 collective-permute-done.12.refs_1_
  62.8 0.4 collective-permute-done.13.refs_2_.refs_0_
  63.3 1.4 %collective-permute-start.14 = (bf16[128,512]{1,0:T(8,128)(2,1)S(1)}, bf16[128,512]{1,0:T(8,128)(2,1)S(1)}, u32[]{:S(2)}, u32[]{:S(2)}) collective-permute-start(bf16[128,512]{1,0:T(8,128)(2,1)S(1)} %relay.1), channel_id=1, source_target_pairs={{0,1},{1,0},{2,3},{3,2},{4,5},{5,4},{6,7},{7,6},{8,9},{9,8},{10,11... | collective-permute-start | bytes 393224 | tf_op jit(solution)/shard_map/ppermute | solution.py:47
  64.7 1.0 %collective-permute-done.14.refs_3_.refs_2_ = bf16[128,512]{1,0:T(8,128)(2,1)S(1)} collective-permute-done((bf16[128,512]{1,0:T(8,128)(2,1)S(1)}, bf16[128,512]{1,0:T(8,128)(2,1)S(1)}, u32[]{:S(2)}, u32[]{:S(2)}) %collective-permute-start.14) | collective-permute-done | bytes 131104 | tf_op jit(solution)/shard_map/ppermute | solution.py:47
  65.7 0.7 outputs.1
  66.4 6.4 %all-to-all-done.1.refs_0_ = bf16[64,16,128]{2,1,0:T(8,128)(2,1)S(1)} async-done(((bf16[64,16,128]{2,1,0:T(8,128)(2,1)}), bf16[64,16,128]{2,1,0:T(8,128)(2,1)S(1)}, u32[]{:S(2)}, u32[]{:S(2)}) %all-to-all-start.1) | async-done | bytes 262176 | tf_op jit(solution)/shard_map/all_to_all | solution.py:52
  72.8 0.8 %finish.1 = bf16[128,1024]{1,0:T(8,128)(2,1)} custom-call(bf16[64,16,128]{2,1,0:T(8,128)(2,1)S(1)} %all-to-all-done.1.refs_0_, f32[128,1024]{1,0:T(8,128)S(1)} %merge.1.refs_1_, bf16[128,512]{1,0:T(8,128)(2,1)S(1)} %collective-permute-done.14.refs_3_.refs_2_), custom_call_target="tpu_custom_call" | custom-call | bytes 1179648 | tf_op jit(solution)/shard_map/finish/pallas_call | solution.py:32
  (5 shorter events, 0.1 us)
Async XLA Ops:
  2.6 12.6 %collective-permute-start = (bf16[128,512]{1,0:T(8,128)(2,1)S(1)}, bf16[128,512]{1,0:T(8,128)(2,1)S(1)}, u32[]{:S(2)}, u32[]{:S(2)}) collective-permute-start(bf16[128,512]{1,0:T(8,128)(2,1)S(1)} %get-tuple-element.46), channel_id=1, source_target_pairs={{0,2},{1,3},{2,0},{3,1},{4,6},{5,7},{6,4},{7,5},{8,10},{9,11},{10,... | collective-permute-start | bytes 393224 | tf_op jit(solution)/shard_map/ppermute | solution.py:47
  5.1 10.0 %collective-permute-start.1 = (bf16[128,512]{1,0:T(8,128)(2,1)S(1)}, bf16[128,512]{1,0:T(8,128)(2,1)S(1)}, u32[]{:S(2)}, u32[]{:S(2)}) collective-permute-start(bf16[128,512]{1,0:T(8,128)(2,1)S(1)} %get-tuple-element.47), channel_id=1, source_target_pairs={{0,3},{1,2},{2,1},{3,0},{4,7},{5,6},{6,5},{7,4},{8,11},{9,10},{10,... | collective-permute-start | bytes 393224 | tf_op jit(solution)/shard_map/ppermute | solution.py:47
  7.5 7.6 %collective-permute-start.2 = (bf16[128,512]{1,0:T(8,128)(2,1)S(1)}, bf16[128,512]{1,0:T(8,128)(2,1)S(1)}, u32[]{:S(2)}, u32[]{:S(2)}) collective-permute-start(bf16[128,512]{1,0:T(8,128)(2,1)S(1)} %get-tuple-element.48), channel_id=1, source_target_pairs={{0,1},{1,0},{2,3},{3,2},{4,5},{5,4},{6,7},{7,6},{8,9},{9,8},{10,11... | collective-permute-start | bytes 393224 | tf_op jit(solution)/shard_map/ppermute | solution.py:47
  7.5 17.6 %all-to-all-start = ((bf16[64,16,128]{2,1,0:T(8,128)(2,1)}), bf16[64,16,128]{2,1,0:T(8,128)(2,1)S(1)}, u32[]{:S(2)}, u32[]{:S(2)}) async-start(bf16[64,16,128]{2,1,0:T(8,128)(2,1)} %get-tuple-element.51), calls=%async_computation | async-start | bytes 524288 | tf_op jit(solution)/shard_map/all_to_all | solution.py:52
  15.4 16.3 %collective-permute-start.5 = (bf16[64,256]{1,0:T(8,128)(2,1)S(1)}, bf16[64,256]{1,0:T(8,128)(2,1)S(1)}, u32[]{:S(2)}, u32[]{:S(2)}) collective-permute-start(bf16[64,256]{1,0:T(8,128)(2,1)S(1)} %get-tuple-element.53), channel_id=1, source_target_pairs={{0,8},{1,9},{2,10},{3,11},{4,12},{5,13},{6,14},{7,15},{8,0},{9,1},... | collective-permute-start | bytes 98312 | tf_op jit(solution)/shard_map/ppermute | solution.py:47
  21.4 11.4 %collective-permute-start.4 = (bf16[64,256]{1,0:T(8,128)(2,1)S(1)}, bf16[64,256]{1,0:T(8,128)(2,1)S(1)}, u32[]{:S(2)}, u32[]{:S(2)}) collective-permute-start(bf16[64,256]{1,0:T(8,128)(2,1)S(1)} %get-tuple-element.53), channel_id=1, source_target_pairs={{0,12},{1,13},{2,14},{3,15},{4,8},{5,9},{6,10},{7,11},{8,4},{9,5},... | collective-permute-start | bytes 98312 | tf_op jit(solution)/shard_map/ppermute | solution.py:47
  21.7 11.1 %collective-permute-start.3 = (bf16[128,256]{1,0:T(8,128)(2,1)S(1)}, bf16[128,256]{1,0:T(8,128)(2,1)S(1)}, u32[]{:S(2)}, u32[]{:S(2)}) collective-permute-start(bf16[128,256]{1,0:T(8,128)(2,1)S(1)} %get-tuple-element.52), channel_id=1, source_target_pairs={{0,4},{1,5},{2,6},{3,7},{4,0},{5,1},{6,2},{7,3},{8,12},{9,13},{10,... | collective-permute-start | bytes 196616 | tf_op jit(solution)/shard_map/ppermute | solution.py:47
  25.2 9.0 %collective-permute-start.8 = (bf16[128,256]{1,0:T(8,128)(2,1)S(1)}, bf16[128,256]{1,0:T(8,128)(2,1)S(1)}, u32[]{:S(2)}, u32[]{:S(2)}) collective-permute-start(bf16[128,256]{1,0:T(8,128)(2,1)S(1)} %collect.1.refs_2_), channel_id=1, source_target_pairs={{0,8},{1,9},{2,10},{3,11},{4,12},{5,13},{6,14},{7,15},{8,0},{9,1},... | collective-permute-start | bytes 196616 | tf_op jit(solution)/shard_map/ppermute | solution.py:47
  31.6 5.6 %collective-permute-start.7 = (bf16[128,256]{1,0:T(8,128)(2,1)S(1)}, bf16[128,256]{1,0:T(8,128)(2,1)S(1)}, u32[]{:S(2)}, u32[]{:S(2)}) collective-permute-start(bf16[128,256]{1,0:T(8,128)(2,1)S(1)} %collect.1.refs_2_), channel_id=1, source_target_pairs={{0,12},{1,13},{2,14},{3,15},{4,8},{5,9},{6,10},{7,11},{8,4},{9,5},... | collective-permute-start | bytes 196616 | tf_op jit(solution)/shard_map/ppermute | solution.py:47
  31.6 6.3 %collective-permute-start.6 = (bf16[128,256]{1,0:T(8,128)(2,1)S(1)}, bf16[128,256]{1,0:T(8,128)(2,1)S(1)}, u32[]{:S(2)}, u32[]{:S(2)}) collective-permute-start(bf16[128,256]{1,0:T(8,128)(2,1)S(1)} %collect.1.refs_2_), channel_id=1, source_target_pairs={{0,4},{1,5},{2,6},{3,7},{4,0},{5,1},{6,2},{7,3},{8,12},{9,13},{10,... | collective-permute-start | bytes 196616 | tf_op jit(solution)/shard_map/ppermute | solution.py:47
  39.3 7.6 %collective-permute-start.10 = (bf16[192,256]{1,0:T(8,128)(2,1)S(1)}, bf16[192,256]{1,0:T(8,128)(2,1)S(1)}, u32[]{:S(2)}, u32[]{:S(2)}) collective-permute-start(bf16[192,256]{1,0:T(8,128)(2,1)S(1)} %get-tuple-element.77), channel_id=1, source_target_pairs={{0,8},{1,9},{2,10},{3,11},{4,12},{5,13},{6,14},{7,15},{8,0},{9,1},... | collective-permute-start | bytes 294920 | tf_op jit(solution)/shard_map/ppermute | solution.py:47
  44.5 9.9 %collective-permute-start.11 = (bf16[192,256]{1,0:T(8,128)(2,1)S(1)}, bf16[192,256]{1,0:T(8,128)(2,1)S(1)}, u32[]{:S(2)}, u32[]{:S(2)}) collective-permute-start(bf16[192,256]{1,0:T(8,128)(2,1)S(1)} %get-tuple-element.78), channel_id=1, source_target_pairs={{0,12},{1,13},{2,14},{3,15},{4,8},{5,9},{6,10},{7,11},{8,4},{9,5},... | collective-permute-start | bytes 294920 | tf_op jit(solution)/shard_map/ppermute | solution.py:47
  45.3 9.7 %collective-permute-start.9 = (bf16[256,256]{1,0:T(8,128)(2,1)S(1)}, bf16[256,256]{1,0:T(8,128)(2,1)S(1)}, u32[]{:S(2)}, u32[]{:S(2)}) collective-permute-start(bf16[256,256]{1,0:T(8,128)(2,1)S(1)} %get-tuple-element.76), channel_id=1, source_target_pairs={{0,4},{1,5},{2,6},{3,7},{4,0},{5,1},{6,2},{7,3},{8,12},{9,13},{10,... | collective-permute-start | bytes 393224 | tf_op jit(solution)/shard_map/ppermute | solution.py:47
  55.7 7.5 %collective-permute-start.13 = (bf16[256,512]{1,0:T(8,128)(2,1)S(1)}, bf16[256,512]{1,0:T(8,128)(2,1)S(1)}, u32[]{:S(2)}, u32[]{:S(2)}) collective-permute-start(bf16[256,512]{1,0:T(8,128)(2,1)S(1)} %get-tuple-element.82), channel_id=1, source_target_pairs={{0,2},{1,3},{2,0},{3,1},{4,6},{5,7},{6,4},{7,5},{8,10},{9,11},{10,... | collective-permute-start | bytes 786440 | tf_op jit(solution)/shard_map/ppermute | solution.py:47
  55.8 7.0 %collective-permute-start.12 = (bf16[128,512]{1,0:T(8,128)(2,1)S(1)}, bf16[128,512]{1,0:T(8,128)(2,1)S(1)}, u32[]{:S(2)}, u32[]{:S(2)}) collective-permute-start(bf16[128,512]{1,0:T(8,128)(2,1)S(1)} %get-tuple-element.81), channel_id=1, source_target_pairs={{0,1},{1,0},{2,3},{3,2},{4,5},{5,4},{6,7},{7,6},{8,9},{9,8},{10,11... | collective-permute-start | bytes 393224 | tf_op jit(solution)/shard_map/ppermute | solution.py:47
  57.0 15.8 %all-to-all-start.1 = ((bf16[64,16,128]{2,1,0:T(8,128)(2,1)}), bf16[64,16,128]{2,1,0:T(8,128)(2,1)S(1)}, u32[]{:S(2)}, u32[]{:S(2)}) async-start(bf16[64,16,128]{2,1,0:T(8,128)(2,1)} %get-tuple-element.86), calls=%async_computation.1 | async-start | bytes 524288 | tf_op jit(solution)/shard_map/all_to_all | solution.py:52
  63.3 2.4 %collective-permute-start.14 = (bf16[128,512]{1,0:T(8,128)(2,1)S(1)}, bf16[128,512]{1,0:T(8,128)(2,1)S(1)}, u32[]{:S(2)}, u32[]{:S(2)}) collective-permute-start(bf16[128,512]{1,0:T(8,128)(2,1)S(1)} %relay.1), channel_id=1, source_target_pairs={{0,1},{1,0},{2,3},{3,2},{4,5},{5,4},{6,7},{7,6},{8,9},{9,8},{10,11... | collective-permute-start | bytes 393224 | tf_op jit(solution)/shard_map/ppermute | solution.py:47

commit v6 on v5

--- a/solution.py
+++ b/solution.py
@@ -298,16 +298,17 @@
     return functools.reduce(jnp.add, [p.astype(F32) for p in parts])
 
 
-def hold_kernel(got_ref, out_ref):
-    out_ref[...] = got_ref[...]
+def four_kernel(block_ref, got_ref, out_ref):
+    out_ref[0:128, :] = add(block_ref[...], got_ref[0:128, :])
+    out_ref[128:192, :] = got_ref[128:192, :].astype(F32)
 
 
 def scatter_kernel(
-    block_ref, back2_ref, back4_ref, back6_ref, one_ref, zero_ref, results_ref,
+    back2_ref, back4_ref, back6_ref, one_ref, zero_ref, results_ref,
     slots_hbm, own_ref, near_ref, far_ref, rows_ref, slots_ref, sem,
 ):
     outer = lax.axis_index("outer")
-    total = add(block_ref[...], back2_ref[0:128, :], back4_ref[0:128, :], back6_ref[0:128, :])
+    total = add(back2_ref[0:128, :], back4_ref[0:128, :], back6_ref[0:128, :])
     for m in range(TEAM):
         slots_ref[outer * TEAM + m] = jnp.zeros((16, COLS), BF16)
         for c in range(4):
@@ -430,14 +431,14 @@
         flops=8 * 1152 * 1024 * 128,
     )(keys, later_keys, q2, cot2, exps, dweights, factor, centre, rounded, dscores)
 
-    (back4,) = call(hold_kernel, "hold", [((192, 256), BF16)], flops=LONG)(back4)
+    (back4,) = call(four_kernel, "four", [((192, 256), F32)], flops=LONG)(block, back4)
     sent, own, near, far = call(
         scatter_kernel,
         "scatter",
         [slots, ((LEAF, 256), F32), whole, ((2 * LEAF, D), BF16)],
         [team_rows, pltpu.VMEM(*slots), pltpu.SemaphoreType.DMA],
         sent_first=True,
-    )(block, back2, back4, back6, one, zero, results)
+    )(back2, back4, back6, one, zero, results)
     taken = trade_slots(sent)
     far = exchange(far, 2)
     near = exchange(near, 1)

time: 73.9 us -> 73.9 us (level)
  no operation moved by 1% of the time
where the time goes in v6:
time: 73.9 us; the launch traced here: 73.6 us
  starting transfers between devices  42 us (57%)
  waiting for transfers between devices  21.6 us (29%)
  Pallas kernels  9.3 us (13%)
  between operations  0.78 us (1%)
    ppermute x15, starting transfers between devices, exchange(): return lax.ppermute(array, 'inner', [(i, i ^ bits) for i in range(16)])  28.5 us
    all_to_all x2, starting transfers between devices, trade_slots(): lax.all_to_all(slots, ('outer', 'inner'), 0, 0, axis_index_groups=groups,...  13.4 us
    ppermute x15, waiting for transfers between devices, exchange(): return lax.ppermute(array, 'inner', [(i, i ^ bits) for i in range(16)])  12.7 us
    pallas_call x14, Pallas kernels, run(): pl.pallas_call(lambda *refs: body(*refs[:count], *refs[count + len(after)...  9.3 us
    all_to_all x2, waiting for transfers between devices, trade_slots(): lax.all_to_all(slots, ('outer', 'inner'), 0, 0, axis_index_groups=groups,...  8.86 us
  transfers between devices with their start and end apart: 17, of which 9 were waited for; matrix products, arithmetic and copies ran while one was open for 0% of the time, Pallas kernels for 6%

profile of v6, /device:TPU:1, one launch (start us, length us, event | category | flops | bytes accessed | tf_op | source)
XLA Modules:
  0.0 73.6 jit_solution(9103258912816994070)
XLA Ops:
  0.6 1.9 %pool.1 = (bf16[64,16,128]{2,1,0:T(8,128)(2,1)}, bf16[128,512]{1,0:T(8,128)(2,1)S(1)}, bf16[128,512]{1,0:T(8,128)(2,1)S(1)}, bf16[128,512]{1,0:T(8,128)(2,1)S(1)}, bf16[128,512]{1,0:T(8,128)(2,1)S(1)}) custom-call(bf16[128,512]{1,0:T(8,128)(2,1)} %bitcast.8, bf16[128,1024]{1,0:T(8,128)(2,1)} %bitcast.6, bf16[128,512]{1,0:T(8,128)(2,1)} %bitcast.9), custom_call_target="tpu_custom_call" | custom-call | bytes 1310720 | tf_op jit(solution)/shard_map/pool/pallas_call | solution.py:32
  2.6 2.6 %collective-permute-start = (bf16[128,512]{1,0:T(8,128)(2,1)S(1)}, bf16[128,512]{1,0:T(8,128)(2,1)S(1)}, u32[]{:S(2)}, u32[]{:S(2)}) collective-permute-start(bf16[128,512]{1,0:T(8,128)(2,1)S(1)} %get-tuple-element.46), channel_id=1, source_target_pairs={{0,2},{1,3},{2,0},{3,1},{4,6},{5,7},{6,4},{7,5},{8,10},{9,11},{10,... | collective-permute-start | bytes 393224 | tf_op jit(solution)/shard_map/ppermute | solution.py:47
  5.1 2.4 %collective-permute-start.1 = (bf16[128,512]{1,0:T(8,128)(2,1)S(1)}, bf16[128,512]{1,0:T(8,128)(2,1)S(1)}, u32[]{:S(2)}, u32[]{:S(2)}) collective-permute-start(bf16[128,512]{1,0:T(8,128)(2,1)S(1)} %get-tuple-element.47), channel_id=1, source_target_pairs={{0,3},{1,2},{2,1},{3,0},{4,7},{5,6},{6,5},{7,4},{8,11},{9,10},{10,... | collective-permute-start | bytes 393224 | tf_op jit(solution)/shard_map/ppermute | solution.py:47
  7.5 0.0 collective-permute-start.2
  7.5 7.6 %all-to-all-start = ((bf16[64,16,128]{2,1,0:T(8,128)(2,1)}), bf16[64,16,128]{2,1,0:T(8,128)(2,1)S(1)}, u32[]{:S(2)}, u32[]{:S(2)}) async-start(bf16[64,16,128]{2,1,0:T(8,128)(2,1)} %get-tuple-element.51), calls=%async_computation | async-start | bytes 524288 | tf_op jit(solution)/shard_map/all_to_all | solution.py:52
  15.1 0.0 collective-permute-done.refs_1_
  15.1 0.0 collective-permute-done.1.refs_2_
  15.2 0.0 collective-permute-done.2.refs_3_
  15.2 0.2 team.1
  15.4 6.1 %collective-permute-start.5 = (bf16[64,256]{1,0:T(8,128)(2,1)S(1)}, bf16[64,256]{1,0:T(8,128)(2,1)S(1)}, u32[]{:S(2)}, u32[]{:S(2)}) collective-permute-start(bf16[64,256]{1,0:T(8,128)(2,1)S(1)} %get-tuple-element.53), channel_id=1, source_target_pairs={{0,8},{1,9},{2,10},{3,11},{4,12},{5,13},{6,14},{7,15},{8,0},{9,1},... | collective-permute-start | bytes 98312 | tf_op jit(solution)/shard_map/ppermute | solution.py:47
  21.4 0.3 collective-permute-start.4
  21.7 0.9 %collective-permute-start.3 = (bf16[128,256]{1,0:T(8,128)(2,1)S(1)}, bf16[128,256]{1,0:T(8,128)(2,1)S(1)}, u32[]{:S(2)}, u32[]{:S(2)}) collective-permute-start(bf16[128,256]{1,0:T(8,128)(2,1)S(1)} %get-tuple-element.52), channel_id=1, source_target_pairs={{0,4},{1,5},{2,6},{3,7},{4,0},{5,1},{6,2},{7,3},{8,12},{9,13},{10,... | collective-permute-start | bytes 196616 | tf_op jit(solution)/shard_map/ppermute | solution.py:47
  22.6 2.5 %all-to-all-done.refs_0_ = bf16[64,16,128]{2,1,0:T(8,128)(2,1)S(1)} async-done(((bf16[64,16,128]{2,1,0:T(8,128)(2,1)}), bf16[64,16,128]{2,1,0:T(8,128)(2,1)S(1)}, u32[]{:S(2)}, u32[]{:S(2)}) %all-to-all-start) | async-done | bytes 262176 | tf_op jit(solution)/shard_map/all_to_all | solution.py:52
  25.2 6.4 %collective-permute-start.8 = (bf16[128,256]{1,0:T(8,128)(2,1)S(1)}, bf16[128,256]{1,0:T(8,128)(2,1)S(1)}, u32[]{:S(2)}, u32[]{:S(2)}) collective-permute-start(bf16[128,256]{1,0:T(8,128)(2,1)S(1)} %collect.1.refs_2_), channel_id=1, source_target_pairs={{0,8},{1,9},{2,10},{3,11},{4,12},{5,13},{6,14},{7,15},{8,0},{9,1},... | collective-permute-start | bytes 196616 | tf_op jit(solution)/shard_map/ppermute | solution.py:47
  31.6 0.0 collective-permute-start.7
  31.6 0.0 collective-permute-done.5.refs_2_
  31.6 1.2 %collective-permute-start.6 = (bf16[128,256]{1,0:T(8,128)(2,1)S(1)}, bf16[128,256]{1,0:T(8,128)(2,1)S(1)}, u32[]{:S(2)}, u32[]{:S(2)}) collective-permute-start(bf16[128,256]{1,0:T(8,128)(2,1)S(1)} %collect.1.refs_2_), channel_id=1, source_target_pairs={{0,4},{1,5},{2,6},{3,7},{4,0},{5,1},{6,2},{7,3},{8,12},{9,13},{10,... | collective-permute-start | bytes 196616 | tf_op jit(solution)/shard_map/ppermute | solution.py:47
  32.8 0.0 collective-permute-done.4.refs_1_
  32.8 0.0 collective-permute-done.3.refs_0_
  32.8 1.3 %first.1 = (bf16[2,768,256]{2,1,0:T(8,128)(2,1)S(1)}, bf16[2,512,128]{2,1,0:T(8,128)(2,1)S(1)}, bf16[2,512,128]{2,1,0:T(8,128)(2,1)S(1)}, f32[2,768,512]{2,1,0:T...) custom-call(bf16[512,512]{1,0:T(8,128)(2,1)S(1)} %get-tuple-element., ...), custom_call_target="tpu_custom_call" | custom-call | flops 402653184 | bytes 8466432 | tf_op jit(solution)/shard_map/first/pallas_call | solution.py:32
  34.1 0.0 collective-permute-done.8.refs_1_
  34.1 3.1 %collective-permute-done.7.refs_0_ = bf16[128,256]{1,0:T(8,128)(2,1)S(1)} collective-permute-done((bf16[128,256]{1,0:T(8,128)(2,1)S(1)}, bf16[128,256]{1,0:T(8,128)(2,1)S(1)}, u32[]{:S(2)}, u32[]{:S(2)}) %collective-permute-start.7) | collective-permute-done | bytes 65568 | tf_op jit(solution)/shard_map/ppermute | solution.py:47
  37.2 0.5 middle.1
  37.7 0.1 collective-permute-done.6.refs_0_
  37.9 1.5 %second.1 = (bf16[256,256]{1,0:T(8,128)(2,1)S(1)}, bf16[192,256]{1,0:T(8,128)(2,1)S(1)}, bf16[192,256]{1,0:T(8,128)(2,1)S(1)}, bf16[640,256]{1,0:T(8,128)(2,1)S(...) custom-call(bf16[128,256]{1,0:T(8,128)(2,1)S(1)} %collective-permute, ...), custom_call_target="tpu_custom_call" | custom-call | flops 671088640 | bytes 12541952 | tf_op jit(solution)/shard_map/second/pallas_call | solution.py:32
  39.3 5.1 %collective-permute-start.10 = (bf16[192,256]{1,0:T(8,128)(2,1)S(1)}, bf16[192,256]{1,0:T(8,128)(2,1)S(1)}, u32[]{:S(2)}, u32[]{:S(2)}) collective-permute-start(bf16[192,256]{1,0:T(8,128)(2,1)S(1)} %get-tuple-element.77), channel_id=1, source_target_pairs={{0,8},{1,9},{2,10},{3,11},{4,12},{5,13},{6,14},{7,15},{8,0},{9,1},... | collective-permute-start | bytes 294920 | tf_op jit(solution)/shard_map/ppermute | solution.py:47
  44.5 0.8 %collective-permute-start.11 = (bf16[192,256]{1,0:T(8,128)(2,1)S(1)}, bf16[192,256]{1,0:T(8,128)(2,1)S(1)}, u32[]{:S(2)}, u32[]{:S(2)}) collective-permute-start(bf16[192,256]{1,0:T(8,128)(2,1)S(1)} %get-tuple-element.78), channel_id=1, source_target_pairs={{0,12},{1,13},{2,14},{3,15},{4,8},{5,9},{6,10},{7,11},{8,4},{9,5},... | collective-permute-start | bytes 294920 | tf_op jit(solution)/shard_map/ppermute | solution.py:47
  45.3 0.0 collective-permute-start.9
  45.3 1.5 %rest.1 = (f32[128,256]{1,0:T(8,128)S(1)}, f32[256,256]{1,0:T(8,128)S(1)}, f32[512,256]{1,0:T(8,128)S(1)}, bf16[512,256]{1,0:T(8,128)(2,1)S(1)}) custom-call(bf16[2,768,256]{2,1,0:T(8,128)(2,1)S(1)} %get-tuple-element.54.refs_0_, bf16[640,256]{1,0:T(8,128)(2,1)S(1)} %get-tuple-element.69.refs_1_, bf16[2,512,128]{2,1,0:T(8,128)(2,1)S(1)} %get-tuple-element.55.refs_2_.refs_3_, ...), custom_call_target="tpu_custom_call" | custom-call | flops 1207959552 | bytes 11739136 | tf_op jit(solution)/shard_map/rest/pallas_call | solution.py:32
  46.8 0.2 collective-permute-done.10.refs_1_
  47.0 7.4 %collective-permute-done.11.refs_2_ = bf16[192,256]{1,0:T(8,128)(2,1)S(1)} collective-permute-done((bf16[192,256]{1,0:T(8,128)(2,1)S(1)}, bf16[192,256]{1,0:T(8,128)(2,1)S(1)}, u32[]{:S(2)}, u32[]{:S(2)}) %collective-permute-start.11) | collective-permute-done | bytes 98336 | tf_op jit(solution)/shard_map/ppermute | solution.py:47
  54.4 0.6 collective-permute-done.9.refs_0_
  54.9 0.8 %scatter.1 = (bf16[64,16,128]{2,1,0:T(8,128)(2,1)}, f32[128,256]{1,0:T(8,128)S(1)}, bf16[128,512]{1,0:T(8,128)(2,1)S(1)}, bf16[256,512]{1,0:T(8,128)(2,1)S(1)}) custom-call(bf16[256,256]{1,0:T(8,128)(2,1)S(1)} %collective-permute-done.9.refs_0_, f32[192,256]{1,0:T(8,128)S(1)} %four.1.refs_1_, bf16[192,256]{1,0:T(8,128)(2,1)S(1)} %collective-permute-done.11.refs_2_, ...), custom_call_target="tpu_custom_call" | custom-call | bytes 2260992 | tf_op jit(solution)/shard_map/scatter/pallas_call | solution.py:32
  55.7 0.1 collective-permute-start.13
  55.8 1.1 %collective-permute-start.12 = (bf16[128,512]{1,0:T(8,128)(2,1)S(1)}, bf16[128,512]{1,0:T(8,128)(2,1)S(1)}, u32[]{:S(2)}, u32[]{:S(2)}) collective-permute-start(bf16[128,512]{1,0:T(8,128)(2,1)S(1)} %get-tuple-element.81), channel_id=1, source_target_pairs={{0,1},{1,0},{2,3},{3,2},{4,5},{5,4},{6,7},{7,6},{8,9},{9,8},{10,11... | collective-permute-start | bytes 393224 | tf_op jit(solution)/shard_map/ppermute | solution.py:47
  56.9 5.8 %all-to-all-start.1 = ((bf16[64,16,128]{2,1,0:T(8,128)(2,1)}), bf16[64,16,128]{2,1,0:T(8,128)(2,1)S(1)}, u32[]{:S(2)}, u32[]{:S(2)}) async-start(bf16[64,16,128]{2,1,0:T(8,128)(2,1)} %get-tuple-element.86), calls=%async_computation.1 | async-start | bytes 524288 | tf_op jit(solution)/shard_map/all_to_all | solution.py:52
  62.8 0.0 collective-permute-done.12.refs_1_
  62.8 0.4 collective-permute-done.13.refs_2_.refs_0_
  63.3 1.4 %collective-permute-start.14 = (bf16[128,512]{1,0:T(8,128)(2,1)S(1)}, bf16[128,512]{1,0:T(8,128)(2,1)S(1)}, u32[]{:S(2)}, u32[]{:S(2)}) collective-permute-start(bf16[128,512]{1,0:T(8,128)(2,1)S(1)} %relay.1), channel_id=1, source_target_pairs={{0,1},{1,0},{2,3},{3,2},{4,5},{5,4},{6,7},{7,6},{8,9},{9,8},{10,11... | collective-permute-start | bytes 393224 | tf_op jit(solution)/shard_map/ppermute | solution.py:47
  64.7 1.0 %collective-permute-done.14.refs_3_.refs_2_ = bf16[128,512]{1,0:T(8,128)(2,1)S(1)} collective-permute-done((bf16[128,512]{1,0:T(8,128)(2,1)S(1)}, bf16[128,512]{1,0:T(8,128)(2,1)S(1)}, u32[]{:S(2)}, u32[]{:S(2)}) %collective-permute-start.14) | collective-permute-done | bytes 131104 | tf_op jit(solution)/shard_map/ppermute | solution.py:47
  65.7 0.7 outputs.1
  66.4 6.4 %all-to-all-done.1.refs_0_ = bf16[64,16,128]{2,1,0:T(8,128)(2,1)S(1)} async-done(((bf16[64,16,128]{2,1,0:T(8,128)(2,1)}), bf16[64,16,128]{2,1,0:T(8,128)(2,1)S(1)}, u32[]{:S(2)}, u32[]{:S(2)}) %all-to-all-start.1) | async-done | bytes 262176 | tf_op jit(solution)/shard_map/all_to_all | solution.py:52
  72.8 0.8 %finish.1 = bf16[128,1024]{1,0:T(8,128)(2,1)} custom-call(bf16[64,16,128]{2,1,0:T(8,128)(2,1)S(1)} %all-to-all-done.1.refs_0_, f32[128,1024]{1,0:T(8,128)S(1)} %merge.1.refs_1_, bf16[128,512]{1,0:T(8,128)(2,1)S(1)} %collective-permute-done.14.refs_3_.refs_2_), custom_call_target="tpu_custom_call" | custom-call | bytes 1179648 | tf_op jit(solution)/shard_map/finish/pallas_call | solution.py:32
  (5 shorter events, 0.1 us)
Async XLA Ops:
  2.6 12.6 %collective-permute-start = (bf16[128,512]{1,0:T(8,128)(2,1)S(1)}, bf16[128,512]{1,0:T(8,128)(2,1)S(1)}, u32[]{:S(2)}, u32[]{:S(2)}) collective-permute-start(bf16[128,512]{1,0:T(8,128)(2,1)S(1)} %get-tuple-element.46), channel_id=1, source_target_pairs={{0,2},{1,3},{2,0},{3,1},{4,6},{5,7},{6,4},{7,5},{8,10},{9,11},{10,... | collective-permute-start | bytes 393224 | tf_op jit(solution)/shard_map/ppermute | solution.py:47
  5.1 10.0 %collective-permute-start.1 = (bf16[128,512]{1,0:T(8,128)(2,1)S(1)}, bf16[128,512]{1,0:T(8,128)(2,1)S(1)}, u32[]{:S(2)}, u32[]{:S(2)}) collective-permute-start(bf16[128,512]{1,0:T(8,128)(2,1)S(1)} %get-tuple-element.47), channel_id=1, source_target_pairs={{0,3},{1,2},{2,1},{3,0},{4,7},{5,6},{6,5},{7,4},{8,11},{9,10},{10,... | collective-permute-start | bytes 393224 | tf_op jit(solution)/shard_map/ppermute | solution.py:47
  7.5 7.6 %collective-permute-start.2 = (bf16[128,512]{1,0:T(8,128)(2,1)S(1)}, bf16[128,512]{1,0:T(8,128)(2,1)S(1)}, u32[]{:S(2)}, u32[]{:S(2)}) collective-permute-start(bf16[128,512]{1,0:T(8,128)(2,1)S(1)} %get-tuple-element.48), channel_id=1, source_target_pairs={{0,1},{1,0},{2,3},{3,2},{4,5},{5,4},{6,7},{7,6},{8,9},{9,8},{10,11... | collective-permute-start | bytes 393224 | tf_op jit(solution)/shard_map/ppermute | solution.py:47
  7.5 17.6 %all-to-all-start = ((bf16[64,16,128]{2,1,0:T(8,128)(2,1)}), bf16[64,16,128]{2,1,0:T(8,128)(2,1)S(1)}, u32[]{:S(2)}, u32[]{:S(2)}) async-start(bf16[64,16,128]{2,1,0:T(8,128)(2,1)} %get-tuple-element.51), calls=%async_computation | async-start | bytes 524288 | tf_op jit(solution)/shard_map/all_to_all | solution.py:52
  15.4 16.3 %collective-permute-start.5 = (bf16[64,256]{1,0:T(8,128)(2,1)S(1)}, bf16[64,256]{1,0:T(8,128)(2,1)S(1)}, u32[]{:S(2)}, u32[]{:S(2)}) collective-permute-start(bf16[64,256]{1,0:T(8,128)(2,1)S(1)} %get-tuple-element.53), channel_id=1, source_target_pairs={{0,8},{1,9},{2,10},{3,11},{4,12},{5,13},{6,14},{7,15},{8,0},{9,1},... | collective-permute-start | bytes 98312 | tf_op jit(solution)/shard_map/ppermute | solution.py:47
  21.4 11.4 %collective-permute-start.4 = (bf16[64,256]{1,0:T(8,128)(2,1)S(1)}, bf16[64,256]{1,0:T(8,128)(2,1)S(1)}, u32[]{:S(2)}, u32[]{:S(2)}) collective-permute-start(bf16[64,256]{1,0:T(8,128)(2,1)S(1)} %get-tuple-element.53), channel_id=1, source_target_pairs={{0,12},{1,13},{2,14},{3,15},{4,8},{5,9},{6,10},{7,11},{8,4},{9,5},... | collective-permute-start | bytes 98312 | tf_op jit(solution)/shard_map/ppermute | solution.py:47
  21.7 11.1 %collective-permute-start.3 = (bf16[128,256]{1,0:T(8,128)(2,1)S(1)}, bf16[128,256]{1,0:T(8,128)(2,1)S(1)}, u32[]{:S(2)}, u32[]{:S(2)}) collective-permute-start(bf16[128,256]{1,0:T(8,128)(2,1)S(1)} %get-tuple-element.52), channel_id=1, source_target_pairs={{0,4},{1,5},{2,6},{3,7},{4,0},{5,1},{6,2},{7,3},{8,12},{9,13},{10,... | collective-permute-start | bytes 196616 | tf_op jit(solution)/shard_map/ppermute | solution.py:47
  25.2 9.0 %collective-permute-start.8 = (bf16[128,256]{1,0:T(8,128)(2,1)S(1)}, bf16[128,256]{1,0:T(8,128)(2,1)S(1)}, u32[]{:S(2)}, u32[]{:S(2)}) collective-permute-start(bf16[128,256]{1,0:T(8,128)(2,1)S(1)} %collect.1.refs_2_), channel_id=1, source_target_pairs={{0,8},{1,9},{2,10},{3,11},{4,12},{5,13},{6,14},{7,15},{8,0},{9,1},... | collective-permute-start | bytes 196616 | tf_op jit(solution)/shard_map/ppermute | solution.py:47
  31.6 5.6 %collective-permute-start.7 = (bf16[128,256]{1,0:T(8,128)(2,1)S(1)}, bf16[128,256]{1,0:T(8,128)(2,1)S(1)}, u32[]{:S(2)}, u32[]{:S(2)}) collective-permute-start(bf16[128,256]{1,0:T(8,128)(2,1)S(1)} %collect.1.refs_2_), channel_id=1, source_target_pairs={{0,12},{1,13},{2,14},{3,15},{4,8},{5,9},{6,10},{7,11},{8,4},{9,5},... | collective-permute-start | bytes 196616 | tf_op jit(solution)/shard_map/ppermute | solution.py:47
  31.6 6.3 %collective-permute-start.6 = (bf16[128,256]{1,0:T(8,128)(2,1)S(1)}, bf16[128,256]{1,0:T(8,128)(2,1)S(1)}, u32[]{:S(2)}, u32[]{:S(2)}) collective-permute-start(bf16[128,256]{1,0:T(8,128)(2,1)S(1)} %collect.1.refs_2_), channel_id=1, source_target_pairs={{0,4},{1,5},{2,6},{3,7},{4,0},{5,1},{6,2},{7,3},{8,12},{9,13},{10,... | collective-permute-start | bytes 196616 | tf_op jit(solution)/shard_map/ppermute | solution.py:47
  39.3 7.6 %collective-permute-start.10 = (bf16[192,256]{1,0:T(8,128)(2,1)S(1)}, bf16[192,256]{1,0:T(8,128)(2,1)S(1)}, u32[]{:S(2)}, u32[]{:S(2)}) collective-permute-start(bf16[192,256]{1,0:T(8,128)(2,1)S(1)} %get-tuple-element.77), channel_id=1, source_target_pairs={{0,8},{1,9},{2,10},{3,11},{4,12},{5,13},{6,14},{7,15},{8,0},{9,1},... | collective-permute-start | bytes 294920 | tf_op jit(solution)/shard_map/ppermute | solution.py:47
  44.5 9.9 %collective-permute-start.11 = (bf16[192,256]{1,0:T(8,128)(2,1)S(1)}, bf16[192,256]{1,0:T(8,128)(2,1)S(1)}, u32[]{:S(2)}, u32[]{:S(2)}) collective-permute-start(bf16[192,256]{1,0:T(8,128)(2,1)S(1)} %get-tuple-element.78), channel_id=1, source_target_pairs={{0,12},{1,13},{2,14},{3,15},{4,8},{5,9},{6,10},{7,11},{8,4},{9,5},... | collective-permute-start | bytes 294920 | tf_op jit(solution)/shard_map/ppermute | solution.py:47
  45.3 9.7 %collective-permute-start.9 = (bf16[256,256]{1,0:T(8,128)(2,1)S(1)}, bf16[256,256]{1,0:T(8,128)(2,1)S(1)}, u32[]{:S(2)}, u32[]{:S(2)}) collective-permute-start(bf16[256,256]{1,0:T(8,128)(2,1)S(1)} %get-tuple-element.75), channel_id=1, source_target_pairs={{0,4},{1,5},{2,6},{3,7},{4,0},{5,1},{6,2},{7,3},{8,12},{9,13},{10,... | collective-permute-start | bytes 393224 | tf_op jit(solution)/shard_map/ppermute | solution.py:47
  55.7 7.5 %collective-permute-start.13 = (bf16[256,512]{1,0:T(8,128)(2,1)S(1)}, bf16[256,512]{1,0:T(8,128)(2,1)S(1)}, u32[]{:S(2)}, u32[]{:S(2)}) collective-permute-start(bf16[256,512]{1,0:T(8,128)(2,1)S(1)} %get-tuple-element.82), channel_id=1, source_target_pairs={{0,2},{1,3},{2,0},{3,1},{4,6},{5,7},{6,4},{7,5},{8,10},{9,11},{10,... | collective-permute-start | bytes 786440 | tf_op jit(solution)/shard_map/ppermute | solution.py:47
  55.8 7.0 %collective-permute-start.12 = (bf16[128,512]{1,0:T(8,128)(2,1)S(1)}, bf16[128,512]{1,0:T(8,128)(2,1)S(1)}, u32[]{:S(2)}, u32[]{:S(2)}) collective-permute-start(bf16[128,512]{1,0:T(8,128)(2,1)S(1)} %get-tuple-element.81), channel_id=1, source_target_pairs={{0,1},{1,0},{2,3},{3,2},{4,5},{5,4},{6,7},{7,6},{8,9},{9,8},{10,11... | collective-permute-start | bytes 393224 | tf_op jit(solution)/shard_map/ppermute | solution.py:47
  56.9 15.8 %all-to-all-start.1 = ((bf16[64,16,128]{2,1,0:T(8,128)(2,1)}), bf16[64,16,128]{2,1,0:T(8,128)(2,1)S(1)}, u32[]{:S(2)}, u32[]{:S(2)}) async-start(bf16[64,16,128]{2,1,0:T(8,128)(2,1)} %get-tuple-element.86), calls=%async_computation.1 | async-start | bytes 524288 | tf_op jit(solution)/shard_map/all_to_all | solution.py:52
  63.3 2.4 %collective-permute-start.14 = (bf16[128,512]{1,0:T(8,128)(2,1)S(1)}, bf16[128,512]{1,0:T(8,128)(2,1)S(1)}, u32[]{:S(2)}, u32[]{:S(2)}) collective-permute-start(bf16[128,512]{1,0:T(8,128)(2,1)S(1)} %relay.1), channel_id=1, source_target_pairs={{0,1},{1,0},{2,3},{3,2},{4,5},{5,4},{6,7},{7,6},{8,9},{9,8},{10,11... | collective-permute-start | bytes 393224 | tf_op jit(solution)/shard_map/ppermute | solution.py:47
